TPU v7x, 256 devices: a whole 4x4x8 slice. The times are simulated.
256 devices in a mesh: pb: 32 (over y, x, core), ka: 8 (over z).
Axes of the slice: x: 4, y: 4, z: 8, core: 2. Of those that a mesh axis runs over, the one named last changes fastest.
Arguments:
- queries: bfloat16 [16384, 1024], P('pb'), may hold values from -8 to 8
- keys: bfloat16 [8, 2048, 128], P('ka', 'pb'), may hold values from -4 to 4
- values: bfloat16 [8, 2048, 128], P('ka', 'pb'), may hold values from -4 to 4
- span_of: int32 [64], replicated, may hold values from 0 to 63, as said below
Outputs:
- attended: bfloat16 [16384, 1024], P('pb', 'ka')
- log_norm: float32 [8, 16384], P('ka', 'pb')
Inputs may be any that keep to these rules, and one draw needn't show every extreme that they name: `span_of`: for each index p of pb, slots 2 p and 2 p + 1 hold a span c and its mirror 64 - 1 - c, in either order; every span is held once.
All inputs are finite; a program needn't handle non-finite values.
Results may differ from a plain program's by a relative error of at most 0.018.
Values may be sent and summed in bfloat16 or wider, within the bound.
No kernel may reach another device: no remote copies, remote signals or barrier semaphores. Data moves between devices by JAX's collectives and lax.ppermute only.
A program may use at most 128 MiB of HBM per device.

v0:
```python
import math

import jax
import jax.numpy as jnp
from jax import lax
from jax.sharding import PartitionSpec as P

NEG = -1e30


def lookup(table, index):
    match = index[:, None] == jnp.arange(table.shape[0], dtype=jnp.int32)[None, :]
    return jnp.sum(jnp.where(match, table[None, :], 0), axis=1)


def update(state, block_keys, block_values, block_pos, query_flat, pos_flat, scale):
    best, total, accum = state
    scores = (
        lax.dot_general(
            query_flat, block_keys, (((1,), (1,)), ((), ())), preferred_element_type=jnp.float32
        )
        * scale
    )
    seen = block_pos[None, :] <= pos_flat[:, None]
    newbest = jnp.maximum(best, jnp.max(jnp.where(seen, scores, NEG), axis=1))
    factor = jnp.exp(best - newbest)
    weights = jnp.where(seen, jnp.exp(scores - newbest[:, None]), 0.0)
    total = total * factor + jnp.sum(weights, axis=1)
    accum = accum * factor[:, None] + jnp.dot(
        weights.astype(jnp.bfloat16), block_values, preferred_element_type=jnp.float32
    )
    return (newbest, total, accum)


def local(queries, keys, values, span_of):
    group = lax.axis_index("ka")
    groups = lax.axis_size("ka")
    place = lax.axis_index("pb")
    rows, width = queries.shape
    head_dim = keys.shape[2]
    heads = width // head_dim
    per_span = rows // 2
    key_rows = per_span // groups
    scale = 1.0 / math.sqrt(head_dim)
    local_spans = lookup(span_of, 2 * place + jnp.arange(2, dtype=jnp.int32))
    query_pos = (
        local_spans[:, None] * per_span + jnp.arange(per_span, dtype=jnp.int32)[None, :]
    ).reshape(rows)
    flat_queries = queries.reshape(rows * heads, head_dim)
    flat_pos = jnp.repeat(query_pos, heads)
    count = rows * heads
    state = (
        jnp.full((count,), NEG, jnp.float32),
        jnp.zeros((count,), jnp.float32),
        jnp.zeros((count, head_dim), jnp.float32),
    )
    start = jnp.int32(0)
    piece_keys = lax.all_gather(keys, "pb", axis=1, tiled=True)[0]
    piece_values = lax.all_gather(values, "pb", axis=1, tiled=True)[0]
    absorb_count = piece_keys.shape[0]
    step = min(absorb_count, 512)
    for first in range(0, absorb_count, step):
        size = min(step, absorb_count - first)
        index = start + first + jnp.arange(size, dtype=jnp.int32)
        block_pos = (
            lookup(span_of, index // key_rows) * per_span + index % key_rows * groups + group
        )
        state = update(
            state,
            piece_keys[first : first + size],
            piece_values[first : first + size],
            block_pos,
            flat_queries,
            flat_pos,
            scale,
        )
    best, total, accum = state
    partial_value = (
        (accum / jnp.maximum(total, 1.0)[:, None]).astype(jnp.bfloat16).reshape(rows, width)
    )
    best = best.reshape(rows, heads)
    total = total.reshape(rows, heads)
    local_heads = heads // groups
    received = lax.all_to_all(
        partial_value.reshape(1, rows, width), "ka", split_axis=2, concat_axis=0, tiled=True
    )
    got_best, got_total = (
        lax.all_to_all(best.reshape(1, rows, heads), "ka", split_axis=2, concat_axis=0, tiled=True),
        lax.all_to_all(
            total.reshape(1, rows, heads), "ka", split_axis=2, concat_axis=0, tiled=True
        ),
    )
    top = jnp.max(got_best, axis=0)
    share = got_total * jnp.exp(got_best - top)
    norm = jnp.sum(share, axis=0)
    pieces = received.reshape(groups, rows, local_heads, head_dim).astype(jnp.float32)
    merged = jnp.sum(share[..., None] * pieces, axis=0) / norm[..., None]
    attended = merged.reshape(rows, local_heads * head_dim).astype(jnp.bfloat16)
    log_norm = (top + jnp.log(norm)).T
    return (attended, log_norm)


def solution(mesh):
    placed = (P("pb", None), P("ka", "pb", None), P("ka", "pb", None), P())
    return jax.shard_map(
        local, mesh=mesh, in_specs=placed, out_specs=(P("pb", "ka"), P("ka", "pb")), check_vma=False
    )
```

profile of v0, /device:TPU:1, one launch (start us, length us, event | category | flops | bytes accessed | tf_op | source)
XLA Modules:
  0.0 185.1 jit_solution(387766933692637548)
XLA Ops:
  0.7 1.5 reshape.520
  2.2 26.4 %all_gather.6 = bf16[1,2048,128]{2,1,0:T(8,128)(2,1)S(1)} all-gather(bf16[1,64,128]{2,1,0:T(8,128)(2,1)} %param.5), channel_id=1, replica_groups=mesh['pb'=32,'ka'=8] {'pb'}, dimensions={1}, use_global_device_ids=true | all-gather | bytes 540672 | tf_op jit(solution)/shard_map/all_gather | solution.py:58
  28.6 4.5 %fusion.38 = f32[4096,512]{0,1:T(8,128)} fusion(bf16[4096,128]{1,0:T(8,128)(2,1)S(1)} %reshape.520, bf16[1,2048,128]{2,1,0:T(8,128)(2,1)S(1)} %all_gather.6), kind=kOutput, calls=%fused_computation.53 | convolution fusion | flops 536870912 | bytes 9568256 | tf_op jit(solution)/shard_map/dot_general | solution.py:19
  33.1 4.5 %fusion.39 = f32[4096,512]{0,1:T(8,128)} fusion(bf16[4096,128]{1,0:T(8,128)(2,1)S(1)} %reshape.520, bf16[1,2048,128]{2,1,0:T(8,128)(2,1)S(1)} %all_gather.6), kind=kOutput, calls=%fused_computation.55 | convolution fusion | flops 536870912 | bytes 9568256 | tf_op jit(solution)/shard_map/dot_general | solution.py:19
  37.6 0.2 fusion.75
  37.9 0.1 broadcast_in_dim.101
  38.0 0.2 le.21
  38.1 0.2 select_reduce_fusion
  38.3 4.5 %fusion = (f32[4096]{0:T(1024)S(1)}, f32[4096,512]{0,1:T(8,128)}) fusion(s32[4096]{0:T(1024)S(1)} %le.21, s32[512]{0:T(512)S(1)} %get-tuple-element.37, bf16[4096,128]{1,0:T(8,128)(2,1)S(1)} %reshape.520, bf16[1,2048,128]{2,1,0:T(8,128)(2,1)S(1)} %all_gather.6), kind=kOutput, calls=%fused_computation.8 | convolution fusion | flops 545255424 | bytes 9603072 | tf_op jit(solution)/shard_map/dot_general | solution.py:19
  42.9 0.2 max_broadcast_in_dim.46
  43.0 16.2 %fusion.5 = (f32[4096]{0:T(1024)S(1)}, f32[4096]{0:T(1024)S(1)}, f32[4096]{0:T(1024)S(1)}, f32[4096]{0:T(1024)S(1)}, f32[4096,512]{0,1:T(8,128)}) fusion(f32[4096,512]{0,1:T(8,128)} %get-tuple-element.32, f32[4096]{0:T(1024)S(1)} %broadcast_maximum_fusion, s32[4096]{0:T(1024)S(1)} %le.21, s32[512]{0:T(512)S(1)} %get-tuple-element.37, ...), kind=kOutput, calls=%fused_computation.13 | convolution fusion | flops 572506112 | bytes 34840576 | tf_op jit(solution)/shard_map/dot_general | solution.py:19
  59.3 0.2 reduce_max.53
  59.4 0.2 reduce_max.55
  59.6 0.2 reduce_max.57
  59.8 0.1 copy.20
  59.9 0.1 copy.23
  60.0 0.1 copy.17
  60.1 11.3 %fusion.7 = (f32[4096]{0:T(1024)S(1)}, f32[4096]{0:T(1024)S(1)}, f32[4096]{0:T(1024)S(1)}) fusion(f32[4096,512]{0,1:T(8,128)} %get-tuple-element.33, f32[4096]{0:T(1024)S(1)} %get-tuple-element.29, s32[4096]{0:T(1024)S(1)} %le.21, s32[512]{0:T(512)S(1)} %get-tuple-element.34, f32[4096]{0:T(1024)S(1)} %get-tuple-element.27, f32[4096,512]{0,1:T(8,128)} %fusion.38, ...), kind=kLoop, calls=%fused_computation.15 | loop fusion | flops 31444992 | bytes 25286656 | tf_op jit(solution)/shard_map/reduce_sum | solution.py:28
  71.4 0.2 reduce_sum.113
  71.6 0.1 copy.22
  71.6 0.2 reduce_sum.116
  71.8 0.1 copy.24
  71.9 0.2 reduce_sum.119
  72.1 0.1 copy.26
  72.2 0.2 reduce_sum.110
  72.4 0.1 copy.18
  72.5 0.1 copy.25
  72.6 0.6 copy.28
  73.2 8.2 %all-to-all-start.1 = ((f32[1,512,8]{1,0,2:T(1,128)}), f32[1,512,8]{1,0,2:T(1,128)S(1)}, u32[]{:S(2)}, u32[]{:S(2)}) async-start(f32[1,512,8]{1,0,2:T(1,128)} %copy.28), calls=%async_computation.1 | async-start | bytes 32768 | tf_op jit(solution)/shard_map/all_to_all | solution.py:88
  81.5 24.7 %all_gather.7 = bf16[1,2048,128]{2,1,0:T(8,128)(2,1)S(1)} all-gather(bf16[1,64,128]{2,1,0:T(8,128)(2,1)S(1)} %copy-done), channel_id=1, replica_groups=mesh['pb'=32,'ka'=8] {'pb'}, dimensions={1}, use_global_device_ids=true | all-gather | bytes 540672 | tf_op jit(solution)/shard_map/all_gather | solution.py:59
  106.2 5.6 %fusion.14 = f32[4096,128]{1,0:T(8,128)S(1)} fusion(f32[4096,512]{0,1:T(8,128)} %get-tuple-element.32, f32[4096]{0:T(1024)S(1)} %broadcast_maximum_fusion, s32[4096]{0:T(1024)S(1)} %le.21, s32[512]{0:T(512)S(1)} %get-tuple-element.37, f32[4096]{0:T(1024)S(1)} %get-tuple-element.26, f32[4096]{0:T(1024)S(1)} %get-tuple-element.30, ...), kind=kOutput, calls=%fused_computation.26 | convolution fusion | flops 548405248 | bytes 10684416 | tf_op jit(solution)/shard_map/dot_general | solution.py:29
  111.8 2.5 %fusion.13 = f32[4096,128]{1,0:T(8,128)S(1)} fusion(f32[4096,128]{1,0:T(8,128)S(1)} %fusion.14, f32[4096,512]{0,1:T(8,128)S(1)} %bitcast.78, f32[4096]{0:T(1024)S(1)} %get-tuple-element.29, s32[4096]{0:T(1024)S(1)} %le.21, s32[512]{0:T(512)S(1)} %get-tuple-element.34, f32[4096]{0:T(1024)S(1)} %get-tuple-element.25, bf16[1,2048,128]{2,1,0:T(8,128)(2,1)S(1)} %all_gather.7), kind=kOutput, calls=%fused_computation.24 | convolution fusion | flops 548405248 | bytes 12765184 | tf_op jit(solution)/shard_map/dot_general | solution.py:29
  114.3 0.9 slice-done.1
  115.3 3.9 %fusion.12 = f32[4096,128]{1,0:T(8,128)} fusion(f32[4096,128]{1,0:T(8,128)S(1)} %fusion.13, f32[4096,512]{0,1:T(8,128)S(1)} %bitcast.75, f32[4096]{0:T(1024)S(1)} %get-tuple-element.28, s32[4096]{0:T(1024)S(1)} %le.21, s32[512]{0:T(512)S(1)} %get-tuple-element.35, f32[4096]{0:T(1024)S(1)} %get-tuple-element.24, bf16[1,2048,128]{2,1,0:T(8,128)(2,1)S(1)} %all_gather.7), kind=kOutput, calls=%fused_computation.22 | convolution fusion | flops 548405248 | bytes 12765184 | tf_op jit(solution)/shard_map/dot_general | solution.py:29
  119.1 0.6 copy.27
  119.8 6.9 %all-to-all-start = ((f32[1,512,8]{1,0,2:T(1,128)}), f32[1,512,8]{1,0,2:T(1,128)S(1)}, u32[]{:S(2)}, u32[]{:S(2)}) async-start(f32[1,512,8]{1,0,2:T(1,128)} %copy.27), calls=%async_computation | async-start | bytes 32768 | tf_op jit(solution)/shard_map/all_to_all | solution.py:89
  126.7 6.5 %fusion.16 = bf16[4096,128]{1,0:T(8,128)(2,1)S(1)} fusion(f32[4096,128]{1,0:T(8,128)} %fusion.12, f32[4096,512]{0,1:T(8,128)} %fusion.38, f32[4096]{0:T(1024)S(1)} %get-tuple-element.27, s32[4096]{0:T(1024)S(1)} %le.21, s32[512]{0:T(512)S(1)} %get-tuple-element.36, f32[4096]{0:T(1024)S(1)} %get-tuple-element.23, bf16[1,2048,128]{2,1,0:T(8,128)(2,1)S(1)} %all_gather.7), kind=kOutput, calls=%fused_computation.28 | convolution fusion | flops 548929536 | bytes 11716608 | tf_op jit(solution)/shard_map/dot_general | solution.py:29
  133.2 0.5 reshape_reshape.2
  133.7 1.8 copy.29
  135.5 0.5 broadcast.448
  136.0 7.0 %reduce.6 = bf16[1024,512]{1,0:T(8,128)(2,1)S(1)} reduce(bf16[1024,1,512]{2,1,0:T(2,128)(2,1)S(1)} %bitcast.79, bf16[]{:T(256)} %broadcast.448), dimensions={1}, to_apply=%bitcast.64.reduce_sub_computation | reduce | bytes 2097154
  143.1 1.6 reshape.523
  144.7 6.6 %all-to-all-start.2 = ((bf16[8,2,32768]{2,1,0:T(2,128)(2,1)}), bf16[8,2,32768]{2,1,0:T(2,128)(2,1)S(1)}, u32[]{:S(2)}, u32[]{:S(2)}) async-start(bf16[8,2,32768]{2,1,0:T(2,128)(2,1)} %reshape.523), calls=%async_computation.2 | async-start | bytes 2097152 | tf_op jit(solution)/shard_map/all_to_all | solution.py:84
  151.4 0.6 log_add_fusion
  152.0 28.6 %all-to-all-done.2 = bf16[8,2,32768]{2,1,0:T(2,128)(2,1)S(1)} async-done(((bf16[8,2,32768]{2,1,0:T(2,128)(2,1)}), bf16[8,2,32768]{2,1,0:T(2,128)(2,1)S(1)}, u32[]{:S(2)}, u32[]{:S(2)}) %all-to-all-start.2) | async-done | bytes 1048608 | tf_op jit(solution)/shard_map/all_to_all | solution.py:84
  180.6 1.0 reshape.524
  181.6 2.7 %fusion.37 = f32[512,128]{0,1:T(8,128)S(1)} fusion(bf16[1,512,8,128]{1,0,3,2:T(2,128)(2,1)S(1)} %bitcast.76, f32[8,512]{1,0:T(8,128)S(1)} %fusion.43), kind=kLoop, calls=%fused_computation.46 | loop fusion | flops 1507328 | bytes 1327104 | tf_op jit(solution)/shard_map/reduce_sum | solution.py:97
  184.3 0.8 copy.30
  (34 shorter events, 0.4 us)
Async XLA Ops:
  33.1 4.5 %copy-start.1 = (s32[64]{0:T(128)S(1)}, s32[64]{0:T(128)}, u32[]{:S(2)}) copy-start(s32[64]{0:T(128)} %param.7) | copy-start | bytes 772
  60.1 21.4 %copy-start = (bf16[1,64,128]{2,1,0:T(8,128)(2,1)S(1)}, bf16[1,64,128]{2,1,0:T(8,128)(2,1)}, u32[]{:S(2)}) copy-start(bf16[1,64,128]{2,1,0:T(8,128)(2,1)} %param.6) | copy-start | bytes 49156
  73.2 46.5 %all-to-all-start.1 = ((f32[1,512,8]{1,0,2:T(1,128)}), f32[1,512,8]{1,0,2:T(1,128)S(1)}, u32[]{:S(2)}, u32[]{:S(2)}) async-start(f32[1,512,8]{1,0,2:T(1,128)} %copy.28), calls=%async_computation.1 | async-start | bytes 32768 | tf_op jit(solution)/shard_map/all_to_all | solution.py:88
  81.4 30.4 %slice-start.2 = ((s8[8388608]{0:T(1024)(128)(4,1)}), s8[4194304]{0:T(1024)(128)(4,1)S(1)}, s32[]{:S(2)}) async-start(s8[8388608]{0:T(1024)(128)(4,1)} %bitcast.77), calls=%async_computation.5 | async-start | bytes 8388608
  106.2 5.7 %slice-start.3 = ((s8[8388608]{0:T(1024)(128)(4,1)}), s8[4194304]{0:T(1024)(128)(4,1)S(1)}, s32[]{:S(2)}) async-start(s8[8388608]{0:T(1024)(128)(4,1)} %bitcast.77), calls=%async_computation.6 | async-start | bytes 8388608
  111.8 2.5 %slice-start = ((s8[8388608]{0:T(1024)(128)(4,1)}), s8[4194304]{0:T(1024)(128)(4,1)S(1)}, s32[]{:S(2)}) async-start(s8[8388608]{0:T(1024)(128)(4,1)} %bitcast.74), calls=%async_computation.3 | async-start | bytes 8388608
  111.8 3.4 %slice-start.1 = ((s8[8388608]{0:T(1024)(128)(4,1)}), s8[4194304]{0:T(1024)(128)(4,1)S(1)}, s32[]{:S(2)}) async-start(s8[8388608]{0:T(1024)(128)(4,1)} %bitcast.74), calls=%async_computation.4 | async-start | bytes 8388608
  119.8 24.9 %all-to-all-start = ((f32[1,512,8]{1,0,2:T(1,128)}), f32[1,512,8]{1,0,2:T(1,128)S(1)}, u32[]{:S(2)}, u32[]{:S(2)}) async-start(f32[1,512,8]{1,0,2:T(1,128)} %copy.27), calls=%async_computation | async-start | bytes 32768 | tf_op jit(solution)/shard_map/all_to_all | solution.py:89
  144.7 35.9 %all-to-all-start.2 = ((bf16[8,2,32768]{2,1,0:T(2,128)(2,1)}), bf16[8,2,32768]{2,1,0:T(2,128)(2,1)S(1)}, u32[]{:S(2)}, u32[]{:S(2)}) async-start(bf16[8,2,32768]{2,1,0:T(2,128)(2,1)} %reshape.523), calls=%async_computation.2 | async-start | bytes 2097152 | tf_op jit(solution)/shard_map/all_to_all | solution.py:84
where the time goes:
time: 185 us
  blocking collectives  51.1 us (28%)
  matrix products  48.1 us (26%)
  waiting for transfers between devices  28.6 us (15%)
  other arithmetic  22.3 us (12%)
  starting transfers between devices  21.8 us (12%)
  local copies, waits for them, and re-layouts  12.3 us (7%)
    dot_general x4, matrix products, update(): lax.dot_general(query_flat, block_keys, (((1,), (1,)), ((), ())), preferr...  29.7 us
    all_to_all x1, waiting for transfers between devices, local(): lax.all_to_all(partial_value.reshape(1, rows, width), 'ka', split_axis=2,...  28.6 us
    all_gather x1, blocking collectives, local(): piece_keys = lax.all_gather(keys, 'pb', axis=1, tiled=True)[0]  26.4 us
    all_gather x1, blocking collectives, local(): piece_values = lax.all_gather(values, 'pb', axis=1, tiled=True)[0]  24.7 us
    dot_general x4, matrix products, update(): jnp.dot(weights.astype(jnp.bfloat16), block_values, preferred_element_typ...  18.4 us
    reduce_sum x1, other arithmetic, update(): total = total * factor + jnp.sum(weights, axis=1)  11.3 us
    all_to_all x1, starting transfers between devices, local(): lax.all_to_all(best.reshape(1, rows, heads), 'ka', split_axis=2, concat_a...  8.19 us
    unnamed x4, other arithmetic  7.12 us
  transfers between devices with their start and end apart: 3, of which 1 were waited for; matrix products, arithmetic and copies ran while one was open for 17% of the time, Pallas kernels for 0%

commit v1 on v0

v1 whole, which is shorter than its diff:
```python
import functools
import math

import jax
import jax.numpy as jnp
from jax import lax
from jax.experimental import pallas as pl
from jax.experimental.pallas import tpu as pltpu
from jax.sharding import PartitionSpec as P

AXES = ("pb", "ka")
NEG = -1e30
FAR = 3e30
LN2 = math.log(2.0)
PARTS = 4
ROWS = 256
HEAD = 128
LINES = 144


def pairs(move):
    out = []
    for y in range(4):
        for x in range(4):
            for c in range(2):
                for z in range(8):
                    ty, tx, tc, tz = move(y, x, c, z)
                    out.append((((y * 4 + x) * 2 + c) * 8 + z, ((ty * 4 + tx) * 2 + tc) * 8 + tz))
    return out


def flip(core, which):
    return (1, 3)[which ^ core]


def send(value, axis, which=0):
    moves = {
        "x": lambda y, x, c, z: (y, x ^ flip(c, which), c, z),
        "y": lambda y, x, c, z: (y ^ flip(c, which), x, c, z),
        "z": lambda y, x, c, z: (y, x, c, z ^ (2 * flip(c, which))),
        "core": lambda y, x, c, z: (y, x, 1 - c, z),
        "team": lambda y, x, c, z: (y, x, c, z ^ 1),
    }
    return lax.ppermute(value, AXES, pairs(moves[axis]))


def double(value, axis):
    held = jnp.concatenate([value, send(value, axis, 0)], axis=0)
    return jnp.concatenate([held, send(held, axis, 1)], axis=0)


def spread(value, axis):
    near = send(value, axis, 0)
    far = send(value, axis, 1)
    return [value, near, far, send(near, axis, 1)]


def prepare(span, place, own, other, high, low):
    pb = place[0]
    for q, ref in enumerate((own, other)):
        p = pb ^ q
        flag = (span[2 * p] >= 32).astype(jnp.int32)
        for out, slot in ((low, flag), (high, 1 - flag)):
            rows = ref[pl.ds(pl.multiple_of(slot * ROWS, ROWS), ROWS), :]
            for h in range(2):
                block = rows[:, h * HEAD : (h + 1) * HEAD].astype(jnp.float32)
                at = (q * 2 + h) * ROWS
                out[:, at : at + ROWS] = block.T.astype(jnp.bfloat16)


def absorb(part, scale, span, place, first_half, second_half, high, low, *refs):
    start = part == 0
    if start:
        olds = (None, None, None)
        acc_high, acc_low, stats, keys, values, lines = refs
    else:
        olds = refs[:3]
        acc_high, acc_low, stats, keys, values, lines = refs[3:]
    pb, z = place[0], place[1]
    core = pb % 2
    y, x = pb // 8, pb // 2 % 4
    near, far = 1 + 2 * core, 3 - 2 * core

    def lowest(p):
        s = span[2 * p]
        return jnp.minimum(s, 63 - s)

    mine = (lowest(pb), lowest(pb ^ 1))
    seen_low, seen_high = [], []
    for e in range(8):
        half, i = e // 4, e % 4
        src = (first_half, second_half)[half]
        inner = (near if i & 1 else 0) ^ (far if i & 2 else 0)
        outer = (near if part & 1 else 0) ^ (far if part & 2 else 0)
        ty, tx = (y ^ outer, x ^ inner) if half == 0 else (y ^ inner, x ^ outer)
        p = (ty * 4 + tx) * 2 + core
        flag = (span[2 * p] >= 32).astype(jnp.int32)
        s = lowest(p)
        seen_low.append([s < c for c in mine])
        seen_high.append([s > c for c in mine])
        for at, slot in ((0, flag), (512, 1 - flag)):
            for g in range(2):
                row = at + e * 64 + g * 32
                keys[row : row + 32, :] = src[i * 2 + g, 0, slot]
                values[row : row + 32, :] = src[i * 2 + g, 1, slot]
    lines[0:HEAD, :] = values[...].astype(jnp.float32).T.astype(jnp.bfloat16)
    lines[HEAD:LINES, :] = jnp.ones((LINES - HEAD, 1024), jnp.bfloat16)
    if start:
        row = lax.broadcasted_iota(jnp.int32, (64, ROWS), 0)
        column = lax.broadcasted_iota(jnp.int32, (64, ROWS), 1)
        edges = []
        for a, b in ((z, z ^ (2 * near)), (z ^ (2 * far), z ^ (2 * far) ^ (2 * near))):
            edges.append(row % 32 * 8 + jnp.where(row < 32, a, b) <= column)

    def update(which, q, at, old_acc, acc, s, free, seen):
        blocks = [s[free + 64 * e : free + 64 * e + 64] for e in range(8)]
        diagonal = start and q == 0
        if diagonal:
            for half in range(2):
                blocks[4 * half] = jnp.where(edges[half], blocks[4 * half], -FAR)
        tops = []
        for e, block in enumerate(blocks):
            best = jnp.max(block, axis=0, keepdims=True)
            if not (diagonal and e % 4 == 0):
                best = jnp.where(seen[e][q], best, NEG)
            tops.append(best)
        if free:
            tops.append(jnp.max(s[:free], axis=0, keepdims=True))
        top = functools.reduce(jnp.maximum, tops)
        old_top = jnp.full((1, ROWS), NEG, jnp.float32) if start else olds[2][2 * which : 2 * which + 1, at : at + ROWS]
        top = jnp.maximum(jnp.maximum(top, old_top), NEG)
        base = top * scale
        weights = []
        if free:
            weights.append(jnp.exp2(s[:free] * scale - base).astype(jnp.bfloat16))
        for e, block in enumerate(blocks):
            if diagonal and e % 4 == 0:
                mine_base = base
            else:
                mine_base = jnp.where(seen[e][q], base, base + FAR)
            weights.append(jnp.exp2(block * scale - mine_base).astype(jnp.bfloat16))
        weights = jnp.concatenate(weights, axis=0)
        sums = jnp.dot(lines[:, : free + 512] if free else lines[:, :512], weights, preferred_element_type=jnp.float32)
        if start:
            acc[:, at : at + ROWS] = sums[:HEAD]
            total = sums[HEAD : HEAD + 1]
        else:
            factor = jnp.exp2(old_top * scale - base)
            acc[:, at : at + ROWS] = old_acc[:, at : at + ROWS] * factor + sums[:HEAD]
            total = olds[2][2 * which + 1 : 2 * which + 2, at : at + ROWS] * factor + sums[HEAD : HEAD + 1]
        stats[2 * which : 2 * which + 1, at : at + ROWS] = top
        stats[2 * which + 1 : 2 * which + 2, at : at + ROWS] = total

    for q in range(2):
        for h in range(2):
            at = (q * 2 + h) * ROWS
            s = jnp.dot(keys[...], high[:, at : at + ROWS], preferred_element_type=jnp.float32)
            update(0, q, at, olds[0], acc_high, s, 512, seen_high)
            s = jnp.dot(keys[0:512, :], low[:, at : at + ROWS], preferred_element_type=jnp.float32)
            update(1, q, at, olds[1], acc_low, s, 0, seen_low)


def pack(out, at, values, norms):
    out[0:HEAD, at : at + ROWS] = values.astype(jnp.bfloat16)
    one = norms.astype(jnp.bfloat16)
    rest = norms - one.astype(jnp.float32)
    two = rest.astype(jnp.bfloat16)
    three = (rest - two.astype(jnp.float32)).astype(jnp.bfloat16)
    row = lax.broadcasted_iota(jnp.int32, (LINES - HEAD, ROWS), 0)
    tail = jnp.where(row == 0, one.astype(jnp.float32), 0.0)
    tail = jnp.where(row == 1, two.astype(jnp.float32), tail)
    tail = jnp.where(row == 2, three.astype(jnp.float32), tail)
    out[HEAD:LINES, at : at + ROWS] = tail.astype(jnp.bfloat16)


def unpack(ref, at):
    tail = ref[HEAD:LINES, at : at + ROWS].astype(jnp.float32)
    return ref[0:HEAD, at : at + ROWS].astype(jnp.float32), tail[0:1] + tail[1:2] + tail[2:3]


def finish(scale, acc_high, acc_low, stats, own, own_norm, out):
    for part, acc in enumerate((acc_high, acc_low)):
        for q in range(2):
            for h in range(2):
                at = (q * 2 + h) * ROWS
                to = (part * 2 + h) * ROWS
                top = stats[2 * part : 2 * part + 1, at : at + ROWS]
                total = stats[2 * part + 1 : 2 * part + 2, at : at + ROWS]
                some = total > 0
                total = jnp.where(some, total, 1.0)
                value = acc[:, at : at + ROWS] / total
                norm = jnp.where(some, top * (scale * LN2) + jnp.log(total), NEG)
                if q == 0:
                    own[:, to : to + ROWS] = value
                    own_norm[0:1, to : to + ROWS] = norm
                else:
                    pack(out, to, value, norm)


def merge(value_a, norm_a, value_b, norm_b):
    top = jnp.maximum(norm_a, norm_b)
    a, b = jnp.exp(norm_a - top), jnp.exp(norm_b - top)
    total = a + b
    return (a * value_a + b * value_b) / total, top + jnp.log(total)


def join(place, own, own_norm, received, mine, mine_norm, out):
    head = place[1] % 2
    for part in range(2):
        for h in range(2):
            at = (part * 2 + h) * ROWS
            value, norm = unpack(received, at)
            value, norm = merge(own[:, at : at + ROWS], own_norm[0:1, at : at + ROWS], value, norm)

            @pl.when(head == h)
            def _():
                mine[:, part * ROWS : (part + 1) * ROWS] = value
                mine_norm[0:1, part * ROWS : (part + 1) * ROWS] = norm

            @pl.when(head != h)
            def _():
                pack(out, part * ROWS, value, norm)


def close(span, place, mine, mine_norm, received, attended, log_norm):
    flag = (span[2 * place[0]] >= 32).astype(jnp.int32)
    for part in range(2):
        at = part * ROWS
        value, norm = unpack(received, at)
        value, norm = merge(mine[:, at : at + ROWS], mine_norm[0:1, at : at + ROWS], value, norm)
        slot = 1 - flag if part == 0 else flag
        to = pl.ds(pl.multiple_of(slot * ROWS, ROWS), ROWS)
        attended[to, :] = value.T.astype(jnp.bfloat16)
        log_norm[:, to] = norm


def call(body, outs, n_scalars, n_arrays, scratch=(), aliases=None, flops=0, moved=0, exps=0):
    return pl.pallas_call(
        body,
        out_shape=outs,
        in_specs=[pl.BlockSpec(memory_space=pltpu.SMEM)] * n_scalars
        + [pl.BlockSpec(memory_space=pltpu.VMEM)] * n_arrays,
        out_specs=jax.tree.map(lambda _: pl.BlockSpec(memory_space=pltpu.VMEM), outs),
        scratch_shapes=list(scratch),
        input_output_aliases=aliases or {},
        compiler_params=pltpu.CompilerParams(vmem_limit_bytes=40 * 2**20),
        cost_estimate=pl.CostEstimate(flops=flops, bytes_accessed=moved, transcendentals=exps),
    )


def shape(*dims, dtype=jnp.float32):
    return jax.ShapeDtypeStruct(dims, dtype)


def local(queries, keys, values, span_of):
    bf16 = jnp.bfloat16
    pb, z = lax.axis_index("pb"), lax.axis_index("ka")
    place = jnp.stack([pb, z]).astype(jnp.int32)
    scale = 1.0 / (math.sqrt(HEAD) * LN2)

    block = jnp.stack([keys[0], values[0]]).reshape(1, 2, 2, 32, HEAD)
    held = jnp.concatenate([block, send(block, "z", 0)], axis=0)
    first = spread(double(held, "x"), "y")
    second = spread(double(send(held, "z", 1), "y"), "x")

    own = lax.dynamic_slice_in_dim(queries, z // 2 * 2 * HEAD, 2 * HEAD, 1)
    other = send(own, "core")
    wide = 4 * ROWS
    high, low = call(prepare, [shape(HEAD, wide, dtype=bf16)] * 2, 2, 2, moved=2**20)(span_of, place, own, other)

    state_shape = [shape(HEAD, wide), shape(HEAD, wide), shape(8, wide)]
    state = []
    for part in range(PARTS):
        state = call(
            functools.partial(absorb, part, scale),
            state_shape,
            2,
            4 + len(state),
            scratch=[
                pltpu.VMEM((1024, HEAD), bf16),
                pltpu.VMEM((1024, HEAD), bf16),
                pltpu.VMEM((LINES, 1024), bf16),
            ],
            aliases={6 + i: i for i in range(len(state))},
            flops=4 * 1024 * 1536 * HEAD,
            moved=3 * 2**20,
            exps=1024 * 1536,
        )(span_of, place, first[part], second[part], high, low, *state)

    own_part, own_norm, message = call(
        functools.partial(finish, scale),
        [shape(HEAD, wide), shape(8, wide), shape(LINES, wide, dtype=bf16)],
        0,
        3,
        moved=2**20,
    )(*state)
    received = send(message, "core")
    half = 2 * ROWS
    mine, mine_norm, message = call(
        join, [shape(HEAD, half), shape(8, half), shape(LINES, half, dtype=bf16)], 1, 3, moved=2**20
    )(place, own_part, own_norm, received)
    received = send(message, "team")
    return tuple(
        call(close, [shape(half, HEAD, dtype=bf16), shape(1, half)], 2, 3, moved=2**20)(
            span_of, place, mine, mine_norm, received
        )
    )


def solution(mesh):
    placed = (P("pb", None), P("ka", "pb", None), P("ka", "pb", None), P())
    return jax.shard_map(
        local, mesh=mesh, in_specs=placed, out_specs=(P("pb", "ka"), P("ka", "pb")), check_vma=False
    )
```

time: 185 us -> 67.8 us (0.37)
  blocking collectives: 51.1 us -> 0 us
  matrix products: 48.1 us -> 0 us
  other arithmetic: 22.3 us -> 0.97 us
  Pallas kernels: 0 us -> 21 us
  waiting for transfers between devices: 28.6 us -> 13.5 us
  local copies, waits for them, and re-layouts: 12.3 us -> 0.67 us
  starting transfers between devices: 21.8 us -> 30.2 us
    all_gather x2 -> x0, blocking collectives: 51.1 us -> none  [the longest x1 26.4 us: local(): piece_keys = lax.all_gather(keys, 'pb', axis=1, tiled=True)[0]]
    dot_general x8 -> x0, matrix products: 48.1 us -> none  [the longest x4 29.7 us: update(): lax.dot_general(query_flat, block_keys, (((1,), (1,)), ((), ())), preferr...]
    ppermute x0 -> x15, starting transfers between devices: none -> 30.2 us  [send(): return lax.ppermute(value, AXES, pairs(moves[axis]))]
    all_to_all x3 -> x0, waiting for transfers between devices: 28.6 us -> none  [the longest x1 28.6 us: local(): lax.all_to_all(partial_value.reshape(1, rows, width), 'ka', split_axis=2,...]
    all_to_all x3 -> x0, starting transfers between devices: 21.8 us -> none  [the longest x1 8.19 us: local(): lax.all_to_all(best.reshape(1, rows, heads), 'ka', split_axis=2, concat_a...]
    pallas_call x0 -> x8, Pallas kernels: none -> 21 us  [the longest x4 18 us: local(): call(functools.partial(absorb, part, scale), state_shape, 2, 4 + len(stat...]
    reduce_sum x5 -> x0, other arithmetic: 14.4 us -> none  [the longest x1 11.3 us: update(): total = total * factor + jnp.sum(weights, axis=1)]
    ppermute x0 -> x15, waiting for transfers between devices: none -> 13.5 us  [send(): return lax.ppermute(value, AXES, pairs(moves[axis]))]
  transfers between devices with their start and end apart: 3 -> 15, of which waited for: 1 -> 7; matrix products, arithmetic and copies ran while one was open for 17% -> 0% of each run, Pallas kernels for 0% -> 21%
where the time goes in v1:
time: 67.8 us; the launch traced here: 67.2 us
  starting transfers between devices  30.2 us (45%)
  Pallas kernels  21 us (31%)
  waiting for transfers between devices  13.5 us (20%)
  other arithmetic  0.97 us (1%)
  between operations  0.78 us (1%)
    ppermute x15, starting transfers between devices, send(): return lax.ppermute(value, AXES, pairs(moves[axis]))  30.2 us
    pallas_call x4, Pallas kernels, local(): call(functools.partial(absorb, part, scale), state_shape, 2, 4 + len(stat...  18 us
    ppermute x15, waiting for transfers between devices, send(): return lax.ppermute(value, AXES, pairs(moves[axis]))  13.5 us
  transfers between devices with their start and end apart: 15, of which 7 were waited for; matrix products, arithmetic and copies ran while one was open for 0% of the time, Pallas kernels for 21%

profile of v1, /device:TPU:1, one launch (start us, length us, event | category | flops | bytes accessed | tf_op | source)
XLA Modules:
  0.0 67.2 jit_solution(5965402924444243925)
XLA Ops:
  0.6 0.0 copy-start
  0.6 0.8 %pad_maximum_fusion.4 = bf16[2,64,128]{2,1,0:T(8,128)(2,1)S(1)} fusion(bf16[1,64,128]{2,1,0:T(8,128)(2,1)} %param.6, bf16[1,64,128]{2,1,0:T(8,128)(2,1)} %param.5), kind=kLoop, calls=%fused_computation.4 | loop fusion | flops 16384 | bytes 65536 | tf_op jit(solution)/shard_map/stack | solution.py:261
  1.5 6.8 %collective-permute-start = (bf16[1,2,2,32,128]{4,3,2,1,0:T(8,128)(2,1)S(1)}, bf16[1,2,2,32,128]{4,3,2,1,0:T(8,128)(2,1)S(1)}, u32[]{:S(2)}, u32[]{:S(2)}) collective-permute-start(bf16[1,2,2,32,128]{4,3,2,1,0:T(8,128)(2,1)S(1)} %bitcast.3), channel_id=1, source_target_pairs={{0,2},{1,3},{2,0},{3,1},{4,6},{5,7},{6,4},{7,5},{8,14},{9,15},{10,... | collective-permute-start | bytes 98312 | tf_op jit(solution)/shard_map/ppermute | solution.py:44
  8.3 1.3 %collective-permute-done = bf16[1,2,2,32,128]{4,3,2,1,0:T(8,128)(2,1)S(1)} collective-permute-done((bf16[1,2,2,32,128]{4,3,2,1,0:T(8,128)(2,1)S(1)}, bf16[1,2,2,32,128]{4,3,2,1,0:T(8,128)(2,1)S(1)}, u32[]{:S(2)}, u32[]{:S(2)}) %collective-permute-start) | collective-permute-done | bytes 32800 | tf_op jit(solution)/shard_map/ppermute | solution.py:44
  9.6 2.6 %collective-permute-start.1 = (bf16[2,2,2,32,128]{4,3,2,1,0:T(8,128)(2,1)S(1)}, bf16[2,2,2,32,128]{4,3,2,1,0:T(8,128)(2,1)S(1)}, u32[]{:S(2)}, u32[]{:S(2)}) collective-permute-start(bf16[2,2,2,32,128]{4,3,2,1,0:T(8,128)(2,1)S(1)} %pad_maximum_fusion.3), channel_id=1, source_target_pairs={{0,16},{1,17},{2,18},{3,19},{4,20},{5,21},{6,22},{7,23},{8,56},{9,... | collective-permute-start | bytes 196616 | tf_op jit(solution)/shard_map/ppermute | solution.py:44
  12.2 1.2 %collective-permute-start.5 = (bf16[2,2,2,32,128]{4,3,2,1,0:T(8,128)(2,1)S(1)}, bf16[2,2,2,32,128]{4,3,2,1,0:T(8,128)(2,1)S(1)}, u32[]{:S(2)}, u32[]{:S(2)}) collective-permute-start(bf16[2,2,2,32,128]{4,3,2,1,0:T(8,128)(2,1)S(1)} %pad_maximum_fusion.3), channel_id=1, source_target_pairs={{0,6},{1,7},{2,4},{3,5},{4,2},{5,3},{6,0},{7,1},{8,10},{9,11},{10,... | collective-permute-start | bytes 196616 | tf_op jit(solution)/shard_map/ppermute | solution.py:44
  13.4 0.7 %collective-permute-done.1 = bf16[2,2,2,32,128]{4,3,2,1,0:T(8,128)(2,1)S(1)} collective-permute-done((bf16[2,2,2,32,128]{4,3,2,1,0:T(8,128)(2,1)S(1)}, bf16[2,2,2,32,128]{4,3,2,1,0:T(8,128)(2,1)S(1)}, u32[]{:S(2)}, u32[]{:S(2)}) %collective-permute-start.1) | collective-permute-done | bytes 65568 | tf_op jit(solution)/shard_map/ppermute | solution.py:44
  14.1 0.1 collective-permute-start.2
  14.2 3.0 %collective-permute-done.5 = bf16[2,2,2,32,128]{4,3,2,1,0:T(8,128)(2,1)S(1)} collective-permute-done((bf16[2,2,2,32,128]{4,3,2,1,0:T(8,128)(2,1)S(1)}, bf16[2,2,2,32,128]{4,3,2,1,0:T(8,128)(2,1)S(1)}, u32[]{:S(2)}, u32[]{:S(2)}) %collective-permute-start.5) | collective-permute-done | bytes 65568 | tf_op jit(solution)/shard_map/ppermute | solution.py:44
  17.2 2.7 %collective-permute-start.6 = (bf16[2,2,2,32,128]{4,3,2,1,0:T(8,128)(2,1)S(1)}, bf16[2,2,2,32,128]{4,3,2,1,0:T(8,128)(2,1)S(1)}, u32[]{:S(2)}, u32[]{:S(2)}) collective-permute-start(bf16[2,2,2,32,128]{4,3,2,1,0:T(8,128)(2,1)S(1)} %collective-permute-done.5), channel_id=1, source_target_pairs={{0,64},{1,65},{2,66},{3,67},{4,68},{5,69},{6,70},{7,71},{8,200},{9... | collective-permute-start | bytes 196616 | tf_op jit(solution)/shard_map/ppermute | solution.py:44
  20.0 1.6 %collective-permute-done.6 = bf16[2,2,2,32,128]{4,3,2,1,0:T(8,128)(2,1)S(1)} collective-permute-done((bf16[2,2,2,32,128]{4,3,2,1,0:T(8,128)(2,1)S(1)}, bf16[2,2,2,32,128]{4,3,2,1,0:T(8,128)(2,1)S(1)}, u32[]{:S(2)}, u32[]{:S(2)}) %collective-permute-start.6) | collective-permute-done | bytes 65568 | tf_op jit(solution)/shard_map/ppermute | solution.py:44
  21.6 0.4 collective-permute-start.7
  22.0 0.0 collective-permute-done.2
  22.1 2.5 %collective-permute-start.3 = (bf16[8,2,2,32,128]{4,3,2,1,0:T(8,128)(2,1)S(1)}, bf16[8,2,2,32,128]{4,3,2,1,0:T(8,128)(2,1)S(1)}, u32[]{:S(2)}, u32[]{:S(2)}) collective-permute-start(bf16[8,2,2,32,128]{4,3,2,1,0:T(8,128)(2,1)S(1)} %pad_maximum_fusion.first_half), channel_id=1, source_target_pairs={{0,64},{1,65},{2,66},{3,67},{4,68},{5,69},{6,70},{7,71},{8,200},{9... | collective-permute-start | bytes 786440 | tf_op jit(solution)/shard_map/ppermute | solution.py:44
  24.6 0.9 %collective-permute-done.7 = bf16[4,2,2,32,128]{4,3,2,1,0:T(8,128)(2,1)S(1)} collective-permute-done((bf16[4,2,2,32,128]{4,3,2,1,0:T(8,128)(2,1)S(1)}, bf16[4,2,2,32,128]{4,3,2,1,0:T(8,128)(2,1)S(1)}, u32[]{:S(2)}, u32[]{:S(2)}) %collective-permute-start.7) | collective-permute-done | bytes 131104 | tf_op jit(solution)/shard_map/ppermute | solution.py:44
  25.5 0.1 collective-permute-start.8
  25.6 0.0 copy-done
  25.7 5.0 %collective-permute-start.10 = (bf16[512,256]{1,0:T(8,128)(2,1)S(1)}, bf16[512,256]{1,0:T(8,128)(2,1)S(1)}, u32[]{:S(2)}, u32[]{:S(2)}) collective-permute-start(bf16[512,256]{1,0:T(8,128)(2,1)S(1)} %constant_dynamic-slice_fusion.own), channel_id=1, source_target_pairs={{0,8},{1,9},{2,10},{3,11},{4,12},{5,13},{6,14},{7,15},{8,0},{9,1},... | collective-permute-start | bytes 786440 | tf_op jit(solution)/shard_map/ppermute | solution.py:44
  30.7 0.0 collective-permute-start.11
  30.8 1.3 %collective-permute-start.12 = (bf16[8,2,2,32,128]{4,3,2,1,0:T(8,128)(2,1)S(1)}, bf16[8,2,2,32,128]{4,3,2,1,0:T(8,128)(2,1)S(1)}, u32[]{:S(2)}, u32[]{:S(2)}) collective-permute-start(bf16[8,2,2,32,128]{4,3,2,1,0:T(8,128)(2,1)S(1)} %constant_dynamic-update-slice_fusion.second_half), channel_id=1, source_target_pairs={{0,48},{1,49},{2,50},{3,51},{4,52},{5,53},{6,54},{7,55},{8,24},{9,... | collective-permute-start | bytes 786440 | tf_op jit(solution)/shard_map/ppermute | solution.py:44
  32.1 0.0 collective-permute-done.3.first_half
  32.1 1.3 %collective-permute-start.4 = (bf16[8,2,2,32,128]{4,3,2,1,0:T(8,128)(2,1)S(1)}, bf16[8,2,2,32,128]{4,3,2,1,0:T(8,128)(2,1)S(1)}, u32[]{:S(2)}, u32[]{:S(2)}) collective-permute-start(bf16[8,2,2,32,128]{4,3,2,1,0:T(8,128)(2,1)S(1)} %collective-permute-done.3.first_half), channel_id=1, source_target_pairs={{0,192},{1,193},{2,194},{3,195},{4,196},{5,197},{6,198},{7,199},{8... | collective-permute-start | bytes 786440 | tf_op jit(solution)/shard_map/ppermute | solution.py:44
  33.4 0.0 collective-permute-done.8.second_half
  33.4 0.3 collective-permute-start.9
  33.7 0.0 copy-start.1
  33.7 0.1 pad_add_fusion.place
  33.8 0.0 collective-permute-done.10.other
  33.8 0.6 copy-done.1
  34.3 0.8 %shard_map.59 = (bf16[128,1024]{1,0:T(8,128)(2,1)S(1)}, bf16[128,1024]{1,0:T(8,128)(2,1)S(1)}) custom-call(s32[64]{0:T(128)S(1)} %copy-done.1, s32[2]{0:T(128)S(1)} %pad_add_fusion.place, bf16[512,256]{1,0:T(8,128)(2,1)S(1)} %constant_dynamic-slice_fusion.own, bf16[512,256]{1,0:T(8,128)(2,1)S(1)} %collective-permute-done.10.other), custom_call_target="tpu_custom_call" | custom-call | bytes 1048576 | tf_op jit(solution)/shard_map/pallas_call | solution.py:269
  35.1 4.6 %shard_map.60 = (f32[128,1024]{1,0:T(8,128)S(1)}, f32[128,1024]{1,0:T(8,128)S(1)}, f32[8,1024]{1,0:T(8,128)S(1)}) custom-call(s32[64]{0:T(128)S(1)} %copy-done.1, s32[2]{0:T(128)S(1)} %pad_add_fusion.place, bf16[8,2,2,32,128]{4,3,2,1,0:T(8,128)(2,1)S(1)} %pad_maximum_fusion.first_half, ...), custom_call_target="tpu_custom_call" | custom-call | flops 805306368 | bytes 3145728 | tf_op jit(solution)/shard_map/pallas_call | solution.py:274
  39.7 4.4 %shard_map.61 = (f32[128,1024]{1,0:T(8,128)S(1)}, f32[128,1024]{1,0:T(8,128)S(1)}, f32[8,1024]{1,0:T(8,128)S(1)}) custom-call(s32[64]{0:T(128)S(1)} %copy-done.1, s32[2]{0:T(128)S(1)} %pad_add_fusion.place, bf16[8,2,2,32,128]{4,3,2,1,0:T(8,128)(2,1)S(1)} %collective-permute-done.3.first_half, ...), custom_call_target="tpu_custom_call", output_to_operand_aliasing={{0}: (6, {}), {1}: (7, {}), {2}: (8, {})} | custom-call | flops 805306368 | bytes 3145728 | tf_op jit(solution)/shard_map/pallas_call | solution.py:274
  44.1 0.0 collective-permute-done.11.first_half
  44.1 0.0 collective-permute-done.12.second_half
  44.1 4.4 %shard_map.62 = (f32[128,1024]{1,0:T(8,128)S(1)}, f32[128,1024]{1,0:T(8,128)S(1)}, f32[8,1024]{1,0:T(8,128)S(1)}) custom-call(s32[64]{0:T(128)S(1)} %copy-done.1, s32[2]{0:T(128)S(1)} %pad_add_fusion.place, bf16[8,2,2,32,128]{4,3,2,1,0:T(8,128)(2,1)S(1)} %collective-permute-done.11.first_half, ...), custom_call_target="tpu_custom_call", output_to_operand_aliasing={{0}: (6, {}), {1}: (7, {}), {2}: (8, {})} | custom-call | flops 805306368 | bytes 3145728 | tf_op jit(solution)/shard_map/pallas_call | solution.py:274
  48.5 0.0 collective-permute-done.4.first_half
  48.6 0.0 collective-permute-done.9.second_half
  48.6 4.6 %shard_map.63 = (f32[128,1024]{1,0:T(8,128)S(1)}, f32[128,1024]{1,0:T(8,128)S(1)}, f32[8,1024]{1,0:T(8,128)S(1)}) custom-call(s32[64]{0:T(128)S(1)} %copy-done.1, s32[2]{0:T(128)S(1)} %pad_add_fusion.place, bf16[8,2,2,32,128]{4,3,2,1,0:T(8,128)(2,1)S(1)} %collective-permute-done.4.first_half, ...), custom_call_target="tpu_custom_call", output_to_operand_aliasing={{0}: (6, {}), {1}: (7, {}), {2}: (8, {})} | custom-call | flops 805306368 | bytes 3145728 | tf_op jit(solution)/shard_map/pallas_call | solution.py:274
  53.2 0.1 shard_map.64
  53.3 5.4 %collective-permute-start.13 = (bf16[144,1024]{1,0:T(8,128)(2,1)S(1)}, bf16[144,1024]{1,0:T(8,128)(2,1)S(1)}, u32[]{:S(2)}, u32[]{:S(2)}) collective-permute-start(bf16[144,1024]{1,0:T(8,128)(2,1)S(1)} %get-tuple-element.38), channel_id=1, source_target_pairs={{0,8},{1,9},{2,10},{3,11},{4,12},{5,13},{6,14},{7,15},{8,0},{9,1},... | collective-permute-start | bytes 884744 | tf_op jit(solution)/shard_map/ppermute | solution.py:44
  58.7 1.2 %collective-permute-done.13.received = bf16[144,1024]{1,0:T(8,128)(2,1)S(1)} collective-permute-done((bf16[144,1024]{1,0:T(8,128)(2,1)S(1)}, bf16[144,1024]{1,0:T(8,128)(2,1)S(1)}, u32[]{:S(2)}, u32[]{:S(2)}) %collective-permute-start.13) | collective-permute-done | bytes 294944 | tf_op jit(solution)/shard_map/ppermute | solution.py:44
  59.9 0.8 %shard_map.65 = (f32[128,512]{1,0:T(8,128)S(1)}, f32[8,512]{1,0:T(8,128)S(1)}, bf16[144,512]{1,0:T(8,128)(2,1)S(1)}) custom-call(s32[2]{0:T(128)S(1)} %pad_add_fusion.place, f32[128,1024]{1,0:T(8,128)S(1)} %get-tuple-element.36.own, f32[8,1024]{1,0:T(8,128)S(1)} %get-tuple-element.37.own_norm, bf16[144,1024]{1,0:T(8,128)(2,1)S(1)} %collective-permute-done.13.received), custom_call_target="tpu_custom_call" | custom-call | bytes 1048576 | tf_op jit(solution)/shard_map/pallas_call | solution.py:299
  60.7 0.5 collective-permute-start.14
  61.2 4.6 %collective-permute-done.14.received = bf16[144,512]{1,0:T(8,128)(2,1)S(1)} collective-permute-done((bf16[144,512]{1,0:T(8,128)(2,1)S(1)}, bf16[144,512]{1,0:T(8,128)(2,1)S(1)}, u32[]{:S(2)}, u32[]{:S(2)}) %collective-permute-start.14) | collective-permute-done | bytes 147488 | tf_op jit(solution)/shard_map/ppermute | solution.py:44
  65.8 1.3 %shard_map.66 = (bf16[512,128]{1,0:T(8,128)(2,1)}, f32[1,512]{1,0:T(1,128)}) custom-call(s32[64]{0:T(128)S(1)} %copy-done.1, s32[2]{0:T(128)S(1)} %pad_add_fusion.place, f32[128,512]{1,0:T(8,128)S(1)} %get-tuple-element.39.mine, f32[8,512]{1,0:T(8,128)S(1)} %get-tuple-element.40.mine_norm, bf16[144,512]{1,0:T(8,128)(2,1)S(1)} %collective-permute-done.14.received), custom_call_target="tpu_custom_call" | custom-call | bytes 1048576 | tf_op jit(solution)/shard_map/pallas_call | solution.py:304
  (8 shorter events, 0.1 us)
Async XLA Ops:
  0.6 25.0 %copy-start = (bf16[512,1024]{1,0:T(8,128)(2,1)S(1)}, bf16[512,1024]{1,0:T(8,128)(2,1)}, u32[]{:S(2)}) copy-start(bf16[512,1024]{1,0:T(8,128)(2,1)} %param.4) | copy-start | bytes 3145732
  1.5 8.2 %collective-permute-start = (bf16[1,2,2,32,128]{4,3,2,1,0:T(8,128)(2,1)S(1)}, bf16[1,2,2,32,128]{4,3,2,1,0:T(8,128)(2,1)S(1)}, u32[]{:S(2)}, u32[]{:S(2)}) collective-permute-start(bf16[1,2,2,32,128]{4,3,2,1,0:T(8,128)(2,1)S(1)} %bitcast.3), channel_id=1, source_target_pairs={{0,2},{1,3},{2,0},{3,1},{4,6},{5,7},{6,4},{7,5},{8,14},{9,15},{10,... | collective-permute-start | bytes 98312 | tf_op jit(solution)/shard_map/ppermute | solution.py:44
  9.6 4.4 %collective-permute-start.1 = (bf16[2,2,2,32,128]{4,3,2,1,0:T(8,128)(2,1)S(1)}, bf16[2,2,2,32,128]{4,3,2,1,0:T(8,128)(2,1)S(1)}, u32[]{:S(2)}, u32[]{:S(2)}) collective-permute-start(bf16[2,2,2,32,128]{4,3,2,1,0:T(8,128)(2,1)S(1)} %pad_maximum_fusion.3), channel_id=1, source_target_pairs={{0,16},{1,17},{2,18},{3,19},{4,20},{5,21},{6,22},{7,23},{8,56},{9,... | collective-permute-start | bytes 196616 | tf_op jit(solution)/shard_map/ppermute | solution.py:44
  12.2 5.0 %collective-permute-start.5 = (bf16[2,2,2,32,128]{4,3,2,1,0:T(8,128)(2,1)S(1)}, bf16[2,2,2,32,128]{4,3,2,1,0:T(8,128)(2,1)S(1)}, u32[]{:S(2)}, u32[]{:S(2)}) collective-permute-start(bf16[2,2,2,32,128]{4,3,2,1,0:T(8,128)(2,1)S(1)} %pad_maximum_fusion.3), channel_id=1, source_target_pairs={{0,6},{1,7},{2,4},{3,5},{4,2},{5,3},{6,0},{7,1},{8,10},{9,11},{10,... | collective-permute-start | bytes 196616 | tf_op jit(solution)/shard_map/ppermute | solution.py:44
  14.1 8.0 %collective-permute-start.2 = (bf16[4,2,2,32,128]{4,3,2,1,0:T(8,128)(2,1)S(1)}, bf16[4,2,2,32,128]{4,3,2,1,0:T(8,128)(2,1)S(1)}, u32[]{:S(2)}, u32[]{:S(2)}) collective-permute-start(bf16[4,2,2,32,128]{4,3,2,1,0:T(8,128)(2,1)S(1)} %pad_maximum_fusion.1), channel_id=1, source_target_pairs={{0,48},{1,49},{2,50},{3,51},{4,52},{5,53},{6,54},{7,55},{8,24},{9,... | collective-permute-start | bytes 393224 | tf_op jit(solution)/shard_map/ppermute | solution.py:44
  17.2 4.4 %collective-permute-start.6 = (bf16[2,2,2,32,128]{4,3,2,1,0:T(8,128)(2,1)S(1)}, bf16[2,2,2,32,128]{4,3,2,1,0:T(8,128)(2,1)S(1)}, u32[]{:S(2)}, u32[]{:S(2)}) collective-permute-start(bf16[2,2,2,32,128]{4,3,2,1,0:T(8,128)(2,1)S(1)} %collective-permute-done.5), channel_id=1, source_target_pairs={{0,64},{1,65},{2,66},{3,67},{4,68},{5,69},{6,70},{7,71},{8,200},{9... | collective-permute-start | bytes 196616 | tf_op jit(solution)/shard_map/ppermute | solution.py:44
  21.6 3.9 %collective-permute-start.7 = (bf16[4,2,2,32,128]{4,3,2,1,0:T(8,128)(2,1)S(1)}, bf16[4,2,2,32,128]{4,3,2,1,0:T(8,128)(2,1)S(1)}, u32[]{:S(2)}, u32[]{:S(2)}) collective-permute-start(bf16[4,2,2,32,128]{4,3,2,1,0:T(8,128)(2,1)S(1)} %pad_maximum_fusion.2), channel_id=1, source_target_pairs={{0,192},{1,193},{2,194},{3,195},{4,196},{5,197},{6,198},{7,199},{8... | collective-permute-start | bytes 393224 | tf_op jit(solution)/shard_map/ppermute | solution.py:44
  22.1 10.0 %collective-permute-start.3 = (bf16[8,2,2,32,128]{4,3,2,1,0:T(8,128)(2,1)S(1)}, bf16[8,2,2,32,128]{4,3,2,1,0:T(8,128)(2,1)S(1)}, u32[]{:S(2)}, u32[]{:S(2)}) collective-permute-start(bf16[8,2,2,32,128]{4,3,2,1,0:T(8,128)(2,1)S(1)} %pad_maximum_fusion.first_half), channel_id=1, source_target_pairs={{0,64},{1,65},{2,66},{3,67},{4,68},{5,69},{6,70},{7,71},{8,200},{9... | collective-permute-start | bytes 786440 | tf_op jit(solution)/shard_map/ppermute | solution.py:44
  25.5 7.8 %collective-permute-start.8 = (bf16[8,2,2,32,128]{4,3,2,1,0:T(8,128)(2,1)S(1)}, bf16[8,2,2,32,128]{4,3,2,1,0:T(8,128)(2,1)S(1)}, u32[]{:S(2)}, u32[]{:S(2)}) collective-permute-start(bf16[8,2,2,32,128]{4,3,2,1,0:T(8,128)(2,1)S(1)} %constant_dynamic-update-slice_fusion.second_half), channel_id=1, source_target_pairs={{0,16},{1,17},{2,18},{3,19},{4,20},{5,21},{6,22},{7,23},{8,56},{9,... | collective-permute-start | bytes 786440 | tf_op jit(solution)/shard_map/ppermute | solution.py:44
  25.7 8.1 %collective-permute-start.10 = (bf16[512,256]{1,0:T(8,128)(2,1)S(1)}, bf16[512,256]{1,0:T(8,128)(2,1)S(1)}, u32[]{:S(2)}, u32[]{:S(2)}) collective-permute-start(bf16[512,256]{1,0:T(8,128)(2,1)S(1)} %constant_dynamic-slice_fusion.own), channel_id=1, source_target_pairs={{0,8},{1,9},{2,10},{3,11},{4,12},{5,13},{6,14},{7,15},{8,0},{9,1},... | collective-permute-start | bytes 786440 | tf_op jit(solution)/shard_map/ppermute | solution.py:44
  30.7 13.4 %collective-permute-start.11 = (bf16[8,2,2,32,128]{4,3,2,1,0:T(8,128)(2,1)S(1)}, bf16[8,2,2,32,128]{4,3,2,1,0:T(8,128)(2,1)S(1)}, u32[]{:S(2)}, u32[]{:S(2)}) collective-permute-start(bf16[8,2,2,32,128]{4,3,2,1,0:T(8,128)(2,1)S(1)} %pad_maximum_fusion.first_half), channel_id=1, source_target_pairs={{0,192},{1,193},{2,194},{3,195},{4,196},{5,197},{6,198},{7,199},{8... | collective-permute-start | bytes 786440 | tf_op jit(solution)/shard_map/ppermute | solution.py:44
  30.8 13.3 %collective-permute-start.12 = (bf16[8,2,2,32,128]{4,3,2,1,0:T(8,128)(2,1)S(1)}, bf16[8,2,2,32,128]{4,3,2,1,0:T(8,128)(2,1)S(1)}, u32[]{:S(2)}, u32[]{:S(2)}) collective-permute-start(bf16[8,2,2,32,128]{4,3,2,1,0:T(8,128)(2,1)S(1)} %constant_dynamic-update-slice_fusion.second_half), channel_id=1, source_target_pairs={{0,48},{1,49},{2,50},{3,51},{4,52},{5,53},{6,54},{7,55},{8,24},{9,... | collective-permute-start | bytes 786440 | tf_op jit(solution)/shard_map/ppermute | solution.py:44
  32.1 16.5 %collective-permute-start.4 = (bf16[8,2,2,32,128]{4,3,2,1,0:T(8,128)(2,1)S(1)}, bf16[8,2,2,32,128]{4,3,2,1,0:T(8,128)(2,1)S(1)}, u32[]{:S(2)}, u32[]{:S(2)}) collective-permute-start(bf16[8,2,2,32,128]{4,3,2,1,0:T(8,128)(2,1)S(1)} %collective-permute-done.3.first_half), channel_id=1, source_target_pairs={{0,192},{1,193},{2,194},{3,195},{4,196},{5,197},{6,198},{7,199},{8... | collective-permute-start | bytes 786440 | tf_op jit(solution)/shard_map/ppermute | solution.py:44
  33.4 15.2 %collective-permute-start.9 = (bf16[8,2,2,32,128]{4,3,2,1,0:T(8,128)(2,1)S(1)}, bf16[8,2,2,32,128]{4,3,2,1,0:T(8,128)(2,1)S(1)}, u32[]{:S(2)}, u32[]{:S(2)}) collective-permute-start(bf16[8,2,2,32,128]{4,3,2,1,0:T(8,128)(2,1)S(1)} %collective-permute-done.8.second_half), channel_id=1, source_target_pairs={{0,48},{1,49},{2,50},{3,51},{4,52},{5,53},{6,54},{7,55},{8,24},{9,... | collective-permute-start | bytes 786440 | tf_op jit(solution)/shard_map/ppermute | solution.py:44
  33.7 0.7 copy-start.1
  53.3 6.6 %collective-permute-start.13 = (bf16[144,1024]{1,0:T(8,128)(2,1)S(1)}, bf16[144,1024]{1,0:T(8,128)(2,1)S(1)}, u32[]{:S(2)}, u32[]{:S(2)}) collective-permute-start(bf16[144,1024]{1,0:T(8,128)(2,1)S(1)} %get-tuple-element.38), channel_id=1, source_target_pairs={{0,8},{1,9},{2,10},{3,11},{4,12},{5,13},{6,14},{7,15},{8,0},{9,1},... | collective-permute-start | bytes 884744 | tf_op jit(solution)/shard_map/ppermute | solution.py:44
  60.7 5.1 %collective-permute-start.14 = (bf16[144,512]{1,0:T(8,128)(2,1)S(1)}, bf16[144,512]{1,0:T(8,128)(2,1)S(1)}, u32[]{:S(2)}, u32[]{:S(2)}) collective-permute-start(bf16[144,512]{1,0:T(8,128)(2,1)S(1)} %get-tuple-element.41), channel_id=1, source_target_pairs={{0,1},{1,0},{2,3},{3,2},{4,5},{5,4},{6,7},{7,6},{8,9},{9,8},{10,11... | collective-permute-start | bytes 442376 | tf_op jit(solution)/shard_map/ppermute | solution.py:44

commit v2 on v0

v2 whole, which is shorter than its diff:
```python
import functools
import math

import jax
import jax.numpy as jnp
from jax import lax
from jax.experimental import pallas as pl
from jax.experimental.pallas import tpu as pltpu
from jax.sharding import PartitionSpec as P

AXES = ("pb", "ka")
NEG = -1e29
FAR = 3e30
STEPS = (0, 1, 3, 2)
ROWS = 256
HEAD = 128
BF16 = jnp.bfloat16
F32 = jnp.float32
SCALE = 1.0 / (math.sqrt(HEAD) * math.log(2.0))


def send(value, move):
    pairs = []
    for y in range(4):
        for x in range(4):
            for c in range(2):
                for z in range(8):
                    ty, tx, tc, tz = move(y, x, c, z)
                    pairs.append((((y * 4 + x) * 2 + c) * 8 + z, ((ty * 4 + tx) * 2 + tc) * 8 + tz))
    return lax.ppermute(value, AXES, pairs)


def along_z(step):
    return lambda y, x, c, z: (y, x, c, z ^ (2 * step))


def along_first(step):
    return lambda y, x, c, z: (y, x ^ step, c, z) if c == 0 else (y ^ step, x, c, z)


def along_second(step):
    return lambda y, x, c, z: (y ^ step, x, c, z) if c == 0 else (y, x ^ step, c, z)


def spread(value, along):
    return [value] + [send(value, along(step)) for step in STEPS[1:]]


def partner(c, z):
    return z ^ 1 if c == 0 else (z + 8 + (1 if z % 2 else -1)) % 8


def lowest(span, p):
    s = span[2 * p]
    return jnp.minimum(s, 63 - s)


def pieces(norms):
    one = norms.astype(BF16).astype(F32)
    two = (norms - one).astype(BF16).astype(F32)
    return one, two, norms - one - two


def eye():
    return lax.broadcasted_iota(jnp.int32, (HEAD, HEAD), 0) == lax.broadcasted_iota(jnp.int32, (HEAD, HEAD), 1)


def to_lanes(wide):
    mask = eye()
    n = wide.shape[0] // HEAD
    return [jnp.sum(jnp.where(mask, wide[i * HEAD : (i + 1) * HEAD], 0.0), axis=0, keepdims=True) for i in range(n)]


def pack(out, at, norms):
    terms = [t for row in to_lanes(norms) for t in pieces(row)]
    room = out.shape[0] - at
    rows = jnp.concatenate(terms + [jnp.zeros((room - len(terms), HEAD), F32)], axis=0)
    out[at:, :] = rows.astype(BF16)


def unpack(ref, at, block):
    terms = ref[at:, :].astype(F32)
    mask = eye()
    parts = [jnp.where(mask, terms[3 * block + i : 3 * block + i + 1], 0.0).astype(BF16) for i in range(3)]
    return jnp.dot(jnp.concatenate(parts, axis=1), jnp.ones((3 * HEAD, HEAD), BF16), preferred_element_type=F32)


def prepare(span, place, own, other, both, flags, tables):
    pb, z = place[0], place[1]
    core = pb % 2
    y, x = pb // 8, pb // 2 % 4
    mine = (lowest(span, pb), lowest(span, pb ^ 1))
    for q, ref in enumerate((own, other)):
        flag = (span[2 * (pb ^ q)] >= 32).astype(jnp.int32)
        for half, slot in ((0, flag), (1, 1 - flag)):
            rows = ref[pl.ds(pl.multiple_of(slot * ROWS, ROWS), ROWS), :]
            for h in range(2):
                both[q, h * ROWS : (h + 1) * ROWS, half * HEAD : (half + 1) * HEAD] = rows[:, h * HEAD : (h + 1) * HEAD]
    for part in range(4):
        for i in range(4):
            ty = jnp.where(core == 0, y ^ STEPS[part], y ^ STEPS[i])
            tx = jnp.where(core == 0, x ^ STEPS[i], x ^ STEPS[part])
            p = (ty * 4 + tx) * 2 + core
            flags[part, i] = jnp.full((16, HEAD), jnp.where(span[2 * p] >= 32, 1.0, 0.0), F32).astype(BF16)
            for q in range(2):
                value = jnp.where(lowest(span, p) < mine[q], 1.0, 0.0)
                if part == 0 and q == 0 and i == 0:
                    value = jnp.float32(1.0)
                flags[part, 4 + 4 * q + i] = jnp.full((16, HEAD), value, F32).astype(BF16)
                tables[part, 4 * q + i] = jnp.full((8, HEAD), value, F32)
    lane = lax.broadcasted_iota(jnp.int32, (8, HEAD), 1)
    group = z ^ (2 * jnp.where(lane < 64, jnp.where(lane < 32, 0, STEPS[1]), jnp.where(lane < 96, STEPS[2], STEPS[3])))
    tables[0, 8] = (lane % 32 * 8 + group).astype(F32)
    tables[0, 9] = jnp.full((8, HEAD), jnp.where(span[2 * pb] >= 32, 1.0, 0.0), F32)


def spread_rows(tile, n):
    return jnp.broadcast_to(tile[None], (n // 8, 8, HEAD)).reshape(n, HEAD)


def absorb(chips, which, n_blocks, *refs):
    start, last = chips[0][2] == 0, chips[0][2] == 3
    blocks, (both, flags, tables), refs = refs[:n_blocks], refs[n_blocks : n_blocks + 3], refs[n_blocks + 3 :]
    n_chips = len(chips)
    n_old = 0 if start else 3 * len(which)
    olds = [refs[3 * j : 3 * j + 3] for j in range(n_old // 3)]
    refs = refs[n_old:]
    rows = 2 * ROWS
    low_keys, low_values, keys, values = refs[-4:]
    outs = refs[:-4]

    def times(data, tile):
        return (data.reshape(HEAD // 16, 16, HEAD) * tile[None]).reshape(HEAD, HEAD)

    low_values[:, HEAD:] = jnp.ones((n_chips * HEAD, HEAD), BF16)
    kinds, tiles = [], []
    for j, q in enumerate(which):
        kinds.append([tables[part, 4 * q + i] for _, _, part, i in chips])
        if start and q == 0:
            kinds[j].append(jnp.zeros((8, HEAD), F32))
        tiles.append(len(kinds[j]))
    for at, (which_block, place, part, i) in enumerate(chips):
        to = slice(at * HEAD, (at + 1) * HEAD)
        flag = flags[part, i]
        block = blocks[which_block]
        for kv, low_ref, fold_ref in ((0, low_keys, keys), (1, low_values, values)):
            first = block[4 * place : 4 * place + 4, kv, 0].reshape(HEAD, HEAD)
            second = block[4 * place : 4 * place + 4, kv, 1].reshape(HEAD, HEAD)
            low = times(first, 1 - flag) + times(second, flag)
            high = times(first, flag) + times(second, 1 - flag)
            low_ref[to, 0:HEAD] = low
            for j, q in enumerate(which):
                kind = flags[part, 4 + 4 * q + i]
                fold_ref[j, to, 0:HEAD] = times(low, kind)
                fold_ref[j, to, HEAD:] = times(high, 1 - kind)
                if tiles[j] == 5 and i == 0:
                    fold_ref[j, 4 * HEAD :, 0:HEAD] = jnp.zeros((HEAD, HEAD), BF16)
                    fold_ref[j, 4 * HEAD :, HEAD:] = high

    contract = (((1,), (1,)), ((), ()))
    scores = []
    for j, q in enumerate(which):
        free = lax.dot_general(both[q, :, HEAD:], low_keys[...], contract, preferred_element_type=F32)
        fold = lax.dot_general(both[q], keys[j, : tiles[j] * HEAD, :], contract, preferred_element_type=F32)
        tile = [fold[:, i * HEAD : (i + 1) * HEAD] for i in range(tiles[j])]
        if tiles[j] == 5:
            row = lax.broadcasted_iota(jnp.int32, (rows, HEAD), 0) % ROWS
            edge = spread_rows(tables[0, 8], rows) <= row.astype(F32)
            tile[0] = jnp.where(edge, tile[0], -FAR)
            tile[4] = jnp.where(edge, tile[4], -FAR)
        scores.append(([free[:, i * HEAD : (i + 1) * HEAD] for i in range(n_chips)], tile))
    for j, q in enumerate(which):
        free, tile = scores[j]
        kind = kinds[j]
        bests = (
            [t + spread_rows((k - 1.0) * FAR, rows) for t, k in zip(tile, kind)],
            [t - spread_rows(k * FAR, rows) for t, k in zip(tile, kind)] + free,
        )
        bases, factors = [], []
        for k in range(2):
            at = slice(k * rows, (k + 1) * rows)
            top = jnp.max(functools.reduce(jnp.maximum, bests[k]), axis=1, keepdims=True) * SCALE
            if start:
                top = jnp.broadcast_to(jnp.maximum(top, NEG), (rows, HEAD))
            else:
                old = olds[j][1][at, :]
                top = jnp.maximum(top, old)
                factors.append(jnp.exp2(old - top))
            bases.append(top)
        low_sum = jnp.zeros((rows, HEAD), F32)
        high_sum = jnp.zeros((rows, HEAD), F32)
        weights = []
        for t, k in zip(tile, kind):
            base = jnp.where(spread_rows(k, rows) > 0, bases[0], bases[1])
            w = jnp.exp2(t * SCALE - base)
            low_sum = low_sum + w * spread_rows(k, rows)
            high_sum = high_sum + w * spread_rows(1.0 - k, rows)
            weights.append(w.astype(BF16))
        fold = jnp.dot(
            jnp.concatenate(weights, axis=1), values[j, : tiles[j] * HEAD, :], preferred_element_type=F32
        )
        weights = [jnp.exp2(t * SCALE - bases[1]).astype(BF16) for t in free]
        free = jnp.dot(jnp.concatenate(weights, axis=1), low_values[...], preferred_element_type=F32)
        parts = (fold[:, :HEAD], fold[:, HEAD:] + free[:, :HEAD])
        totals = (
            jnp.broadcast_to(jnp.sum(low_sum, axis=1, keepdims=True), (rows, HEAD)),
            jnp.sum(high_sum, axis=1, keepdims=True) + free[:, HEAD:],
        )
        norms = []
        for k in range(2):
            at = slice(k * rows, (k + 1) * rows)
            value, total = parts[k], totals[k]
            if not start:
                value = olds[j][0][at, :] * factors[k] + value
                total = olds[j][2][at, :] * factors[k] + total
            if last and q == 1:
                some = total > 0
                total = jnp.where(some, total, 1.0)
                outs[0][at, :] = (value / total).astype(BF16)
                norms.append(jnp.where(some, bases[k] + jnp.log2(total), NEG))
            else:
                outs[3 * j][at, :] = value
                outs[3 * j + 1][at, :] = bases[k]
                outs[3 * j + 2][at, :] = total
        if last and q == 1:
            pack(outs[0], 2 * rows, jnp.concatenate(norms, axis=0))


def merge(value, top, total, other, norm):
    best = jnp.maximum(top, norm)
    a, b = jnp.exp2(top - best), jnp.exp2(norm - best)
    return value * a + other * b, best, total * a + b


def join(head, acc, tops, sums, received, *outs):
    norms = []
    for kind in range(2):
        for j in range(2):
            block = kind * 4 + head * 2 + j
            rows = slice(block * HEAD, (block + 1) * HEAD)
            to = slice((kind * 2 + j) * HEAD, (kind * 2 + j + 1) * HEAD)
            norm = unpack(received, 4 * ROWS, block)
            value, top, total = merge(acc[rows, :], tops[rows, :], sums[rows, :], received[rows, :].astype(F32), norm)
            if head == 0:
                outs[0][to, :], outs[1][to, :], outs[2][to, :] = value, top, total
            else:
                some = total > 0
                total = jnp.where(some, total, 1.0)
                outs[0][to, :] = (value / total).astype(BF16)
                norms.append(jnp.where(some, top + jnp.log2(total), NEG))
    if head == 1:
        pack(outs[0], 2 * ROWS, jnp.concatenate(norms, axis=0))


def close(tables, mine, mine_tops, mine_sums, received, attended, log_norm):
    flag = tables[0, 9]
    values, norms = [], []
    for block in range(4):
        rows = slice(block * HEAD, (block + 1) * HEAD)
        value, top, total = merge(
            mine[rows, :],
            mine_tops[rows, :],
            mine_sums[rows, :],
            received[rows, :].astype(F32),
            unpack(received, 2 * ROWS, block),
        )
        values.append(value / total)
        norms += to_lanes((top + jnp.log2(total)) * math.log(2.0))
    for slot in range(2):
        for j in range(2):
            low, high = values[j], values[2 + j]
            swap = spread_rows(flag, HEAD) > 0
            pair = (high, low) if slot == 0 else (low, high)
            rows = slice((slot * 2 + j) * HEAD, (slot * 2 + j + 1) * HEAD)
            attended[rows, :] = jnp.where(swap, *pair).astype(BF16)
            pair = (norms[2 + j], norms[j]) if slot == 0 else (norms[j], norms[2 + j])
            log_norm[:, rows] = jnp.where(flag[0:1] > 0, *pair)


def call(body, outs, *args, scalars=0, scratch=(), aliases=None, flops=0, moved=2**20, exps=0):
    return pl.pallas_call(
        body,
        out_shape=outs,
        in_specs=[pl.BlockSpec(memory_space=pltpu.SMEM if i < scalars else pltpu.VMEM) for i in range(len(args))],
        out_specs=jax.tree.map(lambda _: pl.BlockSpec(memory_space=pltpu.VMEM), outs),
        scratch_shapes=list(scratch),
        input_output_aliases=aliases or {},
        compiler_params=pltpu.CompilerParams(vmem_limit_bytes=40 * 2**20),
        cost_estimate=pl.CostEstimate(flops=flops, bytes_accessed=moved, transcendentals=exps),
    )(*args)


def shape(*dims, dtype=F32):
    return jax.ShapeDtypeStruct(dims, dtype)


def attend(chips, which, blocks, ready, state):
    n, n_chips = len(which), len(chips)
    start = chips[0][2] == 0
    message = chips[0][2] == 3 and which == (1,)
    outs = [shape(4 * ROWS + 32, HEAD, dtype=BF16)] if message else [shape(4 * ROWS, HEAD)] * (3 * n)
    wide = n_chips + 1 if start else n_chips
    return call(
        functools.partial(absorb, chips, which, len(blocks)),
        outs,
        *blocks,
        *ready,
        *state,
        scratch=[
            pltpu.VMEM((n_chips * HEAD, HEAD), BF16),
            pltpu.VMEM((n_chips * HEAD, 2 * HEAD), BF16),
            pltpu.VMEM((n, wide * HEAD, 2 * HEAD), BF16),
            pltpu.VMEM((n, wide * HEAD, 2 * HEAD), BF16),
        ],
        aliases={} if start or message else {len(blocks) + 3 + i: i for i in range(3 * n)},
        flops=n * n_chips * 1024 * 1024 * HEAD,
        moved=n * 2 * 2**20,
        exps=n * n_chips * 128 * 1024,
    )


def get_ready(span_of, place, own, other):
    return call(
        prepare,
        [shape(2, 2 * ROWS, 2 * HEAD, dtype=BF16), shape(4, 12, 16, HEAD, dtype=BF16), shape(4, 10, 8, HEAD)],
        span_of,
        place,
        own,
        other,
        scalars=2,
    )


def swap_cores(y, x, c, z):
    return (y, x, 1 - c, z)


def local(queries, keys, values, span_of):
    pb, z = lax.axis_index("pb"), lax.axis_index("ka")
    place = jnp.stack([pb, z]).astype(jnp.int32)

    block = jnp.stack([keys[0], values[0]]).reshape(1, 2, 2, 32, HEAD)
    held = spread(block, along_z)
    held[1], queries = lax.optimization_barrier((held[1], queries))
    shared = jnp.where(pb % 2 == 0, z ^ 1, (z + 7 + 2 * (z % 2)) % 8)
    own = jnp.concatenate([lax.dynamic_slice_in_dim(queries, h * HEAD, HEAD, 1) for h in (z, shared)], axis=1)
    other = send(own, swap_cores)
    ready = get_ready(span_of, place, own, other)
    rows = spread(jnp.concatenate(held, axis=0), along_first)
    rows = [jnp.concatenate(rows[:2], axis=0), jnp.concatenate(rows[2:], axis=0)]
    *rows, both, flags, tables = lax.optimization_barrier((*rows, *ready))
    ready = (both, flags, tables)

    near = [send(half, along_second(STEPS[1])) for half in rows]
    far = [send(half, along_second(STEPS[2])) for half in rows]
    state = attend([(i // 2, i % 2, 0, i) for i in range(4)], (0, 1), rows, ready, ())
    near[0], far[1], *state = lax.optimization_barrier((near[0], far[1], *state))
    across = [send(near[0], along_second(STEPS[2])), send(far[1], along_second(STEPS[1]))]
    first = [(0, 0, 1, 0), (0, 1, 1, 1), (1, 0, 2, 2), (1, 1, 2, 3)]
    state = attend(first, (0, 1), [near[0], far[1]], ready, state)
    second = [(0, 0, 1, 2), (0, 1, 1, 3), (1, 0, 2, 0), (1, 1, 2, 1)]
    state = attend(second, (0, 1), [near[1], far[0]], ready, state)
    last = [(i // 2, i % 2, 3, i) for i in range(4)]
    (message,) = attend(last, (1,), across, ready, state[3:])
    received = send(message, swap_cores)
    state = attend(last, (0,), across, ready, state[:3])
    half = 2 * ROWS
    (message,) = call(
        functools.partial(join, 1), [shape(half + 16, HEAD, dtype=BF16)], *state, received
    )
    mine = call(functools.partial(join, 0), [shape(half, HEAD)] * 3, *state, received)
    received = send(message, lambda y, x, c, z: (y, x, c, partner(c, z)))
    return tuple(call(close, [shape(half, HEAD, dtype=BF16), shape(1, half)], ready[2], *mine, received))


def solution(mesh):
    placed = (P("pb", None), P("ka", "pb", None), P("ka", "pb", None), P())
    return jax.shard_map(
        local, mesh=mesh, in_specs=placed, out_specs=(P("pb", "ka"), P("ka", "pb")), check_vma=False
    )
```

time: 185 us -> 54.9 us (0.30)
  blocking collectives: 51.1 us -> 0 us
  matrix products: 48.1 us -> 0 us
  other arithmetic: 22.3 us -> 0.89 us
  waiting for transfers between devices: 28.6 us -> 8.88 us
  Pallas kernels: 0 us -> 13.7 us
  local copies, waits for them, and re-layouts: 12.3 us -> 1.05 us
  starting transfers between devices: 21.8 us -> 29.3 us
    all_gather x2 -> x0, blocking collectives: 51.1 us -> none  [the longest x1 26.4 us: local(): piece_keys = lax.all_gather(keys, 'pb', axis=1, tiled=True)[0]]
    dot_general x8 -> x0, matrix products: 48.1 us -> none  [the longest x4 29.7 us: update(): lax.dot_general(query_flat, block_keys, (((1,), (1,)), ((), ())), preferr...]
    ppermute x0 -> x15, starting transfers between devices: none -> 29.3 us  [send(): return lax.ppermute(value, AXES, pairs)]
    all_to_all x3 -> x0, waiting for transfers between devices: 28.6 us -> none  [the longest x1 28.6 us: local(): lax.all_to_all(partial_value.reshape(1, rows, width), 'ka', split_axis=2,...]
    all_to_all x3 -> x0, starting transfers between devices: 21.8 us -> none  [the longest x1 8.19 us: local(): lax.all_to_all(best.reshape(1, rows, heads), 'ka', split_axis=2, concat_a...]
    reduce_sum x5 -> x0, other arithmetic: 14.4 us -> none  [the longest x1 11.3 us: update(): total = total * factor + jnp.sum(weights, axis=1)]
    pallas_call x0 -> x9, Pallas kernels: none -> 13.7 us  [call(): pl.pallas_call(body, out_shape=outs, in_specs=[pl.BlockSpec(memory_space=...]
    ppermute x0 -> x15, waiting for transfers between devices: none -> 8.88 us  [send(): return lax.ppermute(value, AXES, pairs)]
  transfers between devices with their start and end apart: 3 -> 15, of which waited for: 1 -> 6; matrix products, arithmetic and copies ran while one was open for 17% -> 2% of each run, Pallas kernels for 0% -> 18%
where the time goes in v2:
time: 54.9 us; the launch traced here: 54.6 us
  starting transfers between devices  29.3 us (53%)
  Pallas kernels  13.7 us (25%)
  waiting for transfers between devices  8.88 us (16%)
  local copies, waits for them, and re-layouts  1.05 us (2%)
  other arithmetic  0.89 us (2%)
  between operations  0.77 us (1%)
    ppermute x15, starting transfers between devices, send(): return lax.ppermute(value, AXES, pairs)  29.3 us
    pallas_call x9, Pallas kernels, call(): pl.pallas_call(body, out_shape=outs, in_specs=[pl.BlockSpec(memory_space=...  13.7 us
    ppermute x15, waiting for transfers between devices, send(): return lax.ppermute(value, AXES, pairs)  8.88 us
  transfers between devices with their start and end apart: 15, of which 6 were waited for; matrix products, arithmetic and copies ran while one was open for 2% of the time, Pallas kernels for 18%

profile of v2, /device:TPU:1, one launch (start us, length us, event | category | flops | bytes accessed | tf_op | source)
XLA Modules:
  0.0 54.6 jit_solution(4881904616732778624)
XLA Ops:
  0.6 0.7 %pad_maximum_fusion.3 = bf16[2,64,128]{2,1,0:T(8,128)(2,1)S(1)} fusion(bf16[1,64,128]{2,1,0:T(8,128)(2,1)} %param.6, bf16[1,64,128]{2,1,0:T(8,128)(2,1)} %param.5), kind=kLoop, calls=%fused_computation.3 | loop fusion | flops 16384 | bytes 65536 | tf_op jit(solution)/shard_map/stack | solution.py:342
  1.4 7.7 %collective-permute-start.2 = (bf16[1,2,2,32,128]{4,3,2,1,0:T(8,128)(2,1)S(1)}, bf16[1,2,2,32,128]{4,3,2,1,0:T(8,128)(2,1)S(1)}, u32[]{:S(2)}, u32[]{:S(2)}) collective-permute-start(bf16[1,2,2,32,128]{4,3,2,1,0:T(8,128)(2,1)S(1)} %bitcast.3), channel_id=1, source_target_pairs={{0,4},{1,5},{2,6},{3,7},{4,0},{5,1},{6,2},{7,3},{8,12},{9,13},{10,... | collective-permute-start | bytes 98312 | tf_op jit(solution)/shard_map/ppermute | solution.py:30
  9.1 0.0 collective-permute-start.1
  9.1 1.2 %collective-permute-start = (bf16[1,2,2,32,128]{4,3,2,1,0:T(8,128)(2,1)S(1)}, bf16[1,2,2,32,128]{4,3,2,1,0:T(8,128)(2,1)S(1)}, u32[]{:S(2)}, u32[]{:S(2)}) collective-permute-start(bf16[1,2,2,32,128]{4,3,2,1,0:T(8,128)(2,1)S(1)} %bitcast.5), channel_id=1, source_target_pairs={{0,2},{1,3},{2,0},{3,1},{4,6},{5,7},{6,4},{7,5},{8,10},{9,11},{10,... | collective-permute-start | bytes 98312 | tf_op jit(solution)/shard_map/ppermute | solution.py:30
  10.3 0.1 pad_add_fusion.place
  10.4 2.4 %collective-permute-done = bf16[1,2,2,32,128]{4,3,2,1,0:T(8,128)(2,1)S(1)} collective-permute-done((bf16[1,2,2,32,128]{4,3,2,1,0:T(8,128)(2,1)S(1)}, bf16[1,2,2,32,128]{4,3,2,1,0:T(8,128)(2,1)S(1)}, u32[]{:S(2)}, u32[]{:S(2)}) %collective-permute-start) | collective-permute-done | bytes 32800 | tf_op jit(solution)/shard_map/ppermute | solution.py:30
  12.8 0.0 collective-permute-done.2
  12.8 1.2 %collective-permute-done.1 = bf16[1,2,2,32,128]{4,3,2,1,0:T(8,128)(2,1)S(1)} collective-permute-done((bf16[1,2,2,32,128]{4,3,2,1,0:T(8,128)(2,1)S(1)}, bf16[1,2,2,32,128]{4,3,2,1,0:T(8,128)(2,1)S(1)}, u32[]{:S(2)}, u32[]{:S(2)}) %collective-permute-start.1) | collective-permute-done | bytes 32800 | tf_op jit(solution)/shard_map/ppermute | solution.py:30
  14.0 3.0 %collective-permute-start.5 = (bf16[4,2,2,32,128]{4,3,2,1,0:T(8,128)(2,1)S(1)}, bf16[4,2,2,32,128]{4,3,2,1,0:T(8,128)(2,1)S(1)}, u32[]{:S(2)}, u32[]{:S(2)}) collective-permute-start(bf16[4,2,2,32,128]{4,3,2,1,0:T(8,128)(2,1)S(1)} %pad_maximum_fusion.2), channel_id=1, source_target_pairs={{0,32},{1,33},{2,34},{3,35},{4,36},{5,37},{6,38},{7,39},{8,136},{9... | collective-permute-start | bytes 393224 | tf_op jit(solution)/shard_map/ppermute | solution.py:30
  17.0 0.8 %collective-permute-start.4 = (bf16[4,2,2,32,128]{4,3,2,1,0:T(8,128)(2,1)S(1)}, bf16[4,2,2,32,128]{4,3,2,1,0:T(8,128)(2,1)S(1)}, u32[]{:S(2)}, u32[]{:S(2)}) collective-permute-start(bf16[4,2,2,32,128]{4,3,2,1,0:T(8,128)(2,1)S(1)} %pad_maximum_fusion.2), channel_id=1, source_target_pairs={{0,48},{1,49},{2,50},{3,51},{4,52},{5,53},{6,54},{7,55},{8,200},{9... | collective-permute-start | bytes 393224 | tf_op jit(solution)/shard_map/ppermute | solution.py:30
  17.8 0.0 collective-permute-start.3
  17.8 1.0 %constant_dynamic-slice_fusion.1 = (bf16[512,128]{1,0:T(8,128)(2,1)S(1)}, bf16[512,128]{1,0:T(8,128)(2,1)S(1)}) fusion(bf16[512,1024]{1,0:T(8,128)(2,1)} %param.4, s32[]{:T(128)S(6)} %select_n.24, s32[]{:T(128)S(6)} %select_n.29), kind=kLoop, calls=%fused_computation.11 | loop fusion | bytes 524296 | tf_op jit(solution)/shard_map/dynamic_slice | solution.py:346
  18.8 3.0 %collective-permute-start.6 = (bf16[512,256]{1,0:T(8,128)(2,1)S(1)}, bf16[512,256]{1,0:T(8,128)(2,1)S(1)}, u32[]{:S(2)}, u32[]{:S(2)}) collective-permute-start(bf16[512,256]{1,0:T(8,128)(2,1)S(1)} %pad_maximum_fusion.1.own), channel_id=1, source_target_pairs={{0,8},{1,9},{2,10},{3,11},{4,12},{5,13},{6,14},{7,15},{8,0},{9,1},... | collective-permute-start | bytes 786440 | tf_op jit(solution)/shard_map/ppermute | solution.py:30
  21.9 0.0 collective-permute-done.3
  21.9 0.0 copy-start
  21.9 0.0 collective-permute-done.5
  21.9 0.4 collective-permute-done.4
  22.4 0.7 %collective-permute-done.6.other = bf16[512,256]{1,0:T(8,128)(2,1)S(1)} collective-permute-done((bf16[512,256]{1,0:T(8,128)(2,1)S(1)}, bf16[512,256]{1,0:T(8,128)(2,1)S(1)}, u32[]{:S(2)}, u32[]{:S(2)}) %collective-permute-start.6) | collective-permute-done | bytes 262176 | tf_op jit(solution)/shard_map/ppermute | solution.py:30
  23.0 0.0 copy-done
  23.0 0.7 %shard_map.59 = (bf16[2,512,256]{2,1,0:T(8,128)(2,1)S(1)}, bf16[4,12,16,128]{3,2,1,0:T(8,128)(2,1)S(1)}, f32[4,10,8,128]{3,2,1,0:T(8,128)S(1)}) custom-call(s32[64]{0:T(128)S(1)} %copy-done, s32[2]{0:T(128)S(1)} %pad_add_fusion.place, bf16[512,256]{1,0:T(8,128)(2,1)S(1)} %pad_maximum_fusion.1.own, bf16[512,256]{1,0:T(8,128)(2,1)S(1)} %collective-permute-done.6.other), custom_call_target="tpu_custom_call" | custom-call | bytes 1048576 | tf_op jit(solution)/shard_map/pallas_call | solution.py:281
  23.8 1.8 %collective-permute-start.7 = (bf16[8,2,2,32,128]{4,3,2,1,0:T(8,128)(2,1)S(1)}, bf16[8,2,2,32,128]{4,3,2,1,0:T(8,128)(2,1)S(1)}, u32[]{:S(2)}, u32[]{:S(2)}) collective-permute-start(bf16[8,2,2,32,128]{4,3,2,1,0:T(8,128)(2,1)S(1)} %constant_dynamic-update-slice_fusion.refs_0_), channel_id=1, source_target_pairs={{0,64},{1,65},{2,66},{3,67},{4,68},{5,69},{6,70},{7,71},{8,24},{9,... | collective-permute-start | bytes 786440 | tf_op jit(solution)/shard_map/ppermute | solution.py:30
  25.6 1.8 %collective-permute-start.8 = (bf16[8,2,2,32,128]{4,3,2,1,0:T(8,128)(2,1)S(1)}, bf16[8,2,2,32,128]{4,3,2,1,0:T(8,128)(2,1)S(1)}, u32[]{:S(2)}, u32[]{:S(2)}) collective-permute-start(bf16[8,2,2,32,128]{4,3,2,1,0:T(8,128)(2,1)S(1)} %pad_maximum_fusion.refs_1_), channel_id=1, source_target_pairs={{0,192},{1,193},{2,194},{3,195},{4,196},{5,197},{6,198},{7,199},{8... | collective-permute-start | bytes 786440 | tf_op jit(solution)/shard_map/ppermute | solution.py:30
  27.4 0.9 %collective-permute-start.12 = (bf16[8,2,2,32,128]{4,3,2,1,0:T(8,128)(2,1)S(1)}, bf16[8,2,2,32,128]{4,3,2,1,0:T(8,128)(2,1)S(1)}, u32[]{:S(2)}, u32[]{:S(2)}) collective-permute-start(bf16[8,2,2,32,128]{4,3,2,1,0:T(8,128)(2,1)S(1)} %constant_dynamic-update-slice_fusion.refs_0_), channel_id=1, source_target_pairs={{0,192},{1,193},{2,194},{3,195},{4,196},{5,197},{6,198},{7,199},{8... | collective-permute-start | bytes 786440 | tf_op jit(solution)/shard_map/ppermute | solution.py:30
  28.3 0.0 collective-permute-start.11
  28.3 2.5 %shard_map.60 = (f32[1024,128]{1,0:T(8,128)S(1)}, f32[1024,128]{1,0:T(8,128)S(1)}, f32[1024,128]{1,0:T(8,128)S(1)}, f32[1024,128]{1,0:T(8,128)S(1)}, f32[1024,128]{1,0:T(8,128)S(1)}, /*index=5*/f32[1024,128]{1,0:T(8,128)S(1)}) custom-call(bf16[8,2,2,32,128]{4,3,2,1,0:T(8,128)(2,1)S(1)} %constant_dynamic-update-slice_fusion.refs_0_, ...), custom_call_target="tpu_custom_call" | custom-call | flops 1073741824 | bytes 4194304 | tf_op jit(solution)/shard_map/pallas_call | solution.py:281
  30.8 0.0 collective-permute-done.7.refs_0_
  30.8 1.3 %collective-permute-done.8.refs_1_ = bf16[8,2,2,32,128]{4,3,2,1,0:T(8,128)(2,1)S(1)} collective-permute-done((bf16[8,2,2,32,128]{4,3,2,1,0:T(8,128)(2,1)S(1)}, bf16[8,2,2,32,128]{4,3,2,1,0:T(8,128)(2,1)S(1)}, u32[]{:S(2)}, u32[]{:S(2)}) %collective-permute-start.8) | collective-permute-done | bytes 262176 | tf_op jit(solution)/shard_map/ppermute | solution.py:30
  32.0 1.8 %collective-permute-start.9 = (bf16[8,2,2,32,128]{4,3,2,1,0:T(8,128)(2,1)S(1)}, bf16[8,2,2,32,128]{4,3,2,1,0:T(8,128)(2,1)S(1)}, u32[]{:S(2)}, u32[]{:S(2)}) collective-permute-start(bf16[8,2,2,32,128]{4,3,2,1,0:T(8,128)(2,1)S(1)} %collective-permute-done.7.refs_0_), channel_id=1, source_target_pairs={{0,192},{1,193},{2,194},{3,195},{4,196},{5,197},{6,198},{7,199},{8... | collective-permute-start | bytes 786440 | tf_op jit(solution)/shard_map/ppermute | solution.py:30
  33.8 0.0 collective-permute-start.10
  33.8 2.9 %shard_map.61 = (f32[1024,128]{1,0:T(8,128)S(1)}, f32[1024,128]{1,0:T(8,128)S(1)}, f32[1024,128]{1,0:T(8,128)S(1)}, f32[1024,128]{1,0:T(8,128)S(1)}, f32[1024,128]{1,0:T(8,128)S(1)}, /*index=5*/f32[1024,128]{1,0:T(8,128)S(1)}) custom-call(bf16[8,2,2,32,128]{4,3,2,1,0:T(8,128)(2,1)S(1)} %collect, ...), custom_call_target="tpu_custom_call", output_to_operand_aliasing={{0}: (5, {}), {1}: (6, {}), {2}: (7, {}), {3}: (8, {}), {4}... | custom-call | flops 1073741824 | bytes 4194304 | tf_op jit(solution)/shard_map/pallas_call | solution.py:281
  36.7 0.0 collective-permute-done.12.refs_1_
  36.7 0.0 collective-permute-done.11.refs_0_
  36.8 2.9 %shard_map.62 = (f32[1024,128]{1,0:T(8,128)S(1)}, f32[1024,128]{1,0:T(8,128)S(1)}, f32[1024,128]{1,0:T(8,128)S(1)}, f32[1024,128]{1,0:T(8,128)S(1)}, f32[1024,128]{1,0:T(8,128)S(1)}, /*index=5*/f32[1024,128]{1,0:T(8,128)S(1)}) custom-call(bf16[8,2,2,32,128]{4,3,2,1,0:T(8,128)(2,1)S(1)} %collect, ...), custom_call_target="tpu_custom_call", output_to_operand_aliasing={{0}: (5, {}), {1}: (6, {}), {2}: (7, {}), {3}: (8, {}), {4}... | custom-call | flops 1073741824 | bytes 4194304 | tf_op jit(solution)/shard_map/pallas_call | solution.py:281
  39.7 0.0 collective-permute-done.9.refs_0_
  39.7 0.0 collective-permute-done.10.refs_1_
  39.7 1.5 %shard_map.64 = bf16[1056,128]{1,0:T(8,128)(2,1)S(1)} custom-call(bf16[8,2,2,32,128]{4,3,2,1,0:T(8,128)(2,1)S(1)} %collective-permute-done.9.refs_0_, bf16[8,2,2,32,128]{4,3,2,1,0:T(8,128)(2,1)S(1)} %collective-permute-done.10.refs_1_, bf16[2,512,256]{2,1,0:T(8,128)(2,1)S(1)} %get-tuple-element.52.refs_2_, ...), custom_call_target="tpu_custom_call" | custom-call | flops 536870912 | bytes 2097152 | tf_op jit(solution)/shard_map/pallas_call | solution.py:281
  41.2 5.3 %collective-permute-start.13 = (bf16[1056,128]{1,0:T(8,128)(2,1)S(1)}, bf16[1056,128]{1,0:T(8,128)(2,1)S(1)}, u32[]{:S(2)}, u32[]{:S(2)}) collective-permute-start(bf16[1056,128]{1,0:T(8,128)(2,1)S(1)} %shard_map.64), channel_id=1, source_target_pairs={{0,8},{1,9},{2,10},{3,11},{4,12},{5,13},{6,14},{7,15},{8,0},{9,1},... | collective-permute-start | bytes 811016 | tf_op jit(solution)/shard_map/ppermute | solution.py:30
  46.5 1.5 %shard_map.63 = (f32[1024,128]{1,0:T(8,128)S(1)}, f32[1024,128]{1,0:T(8,128)S(1)}, f32[1024,128]{1,0:T(8,128)S(1)}) custom-call(bf16[8,2,2,32,128]{4,3,2,1,0:T(8,128)(2,1)S(1)} %collective-permute-done.9.refs_0_, bf16[8,2,2,32,128]{4,3,2,1,0:T(8,128)(2,1)S(1)} %collective-permute-done.10.refs_1_, ...), custom_call_target="tpu_custom_call", output_to_operand_aliasing={{0}: (5, {}), {1}: (6, {}), {2}: (7, {})} | custom-call | flops 536870912 | bytes 2097152 | tf_op jit(solution)/shard_map/pallas_call | solution.py:281
  48.0 0.0 collective-permute-done.13.received
  48.0 0.4 shard_map.66
  48.4 1.9 %collective-permute-start.14 = (bf16[528,128]{1,0:T(8,128)(2,1)S(1)}, bf16[528,128]{1,0:T(8,128)(2,1)S(1)}, u32[]{:S(2)}, u32[]{:S(2)}) collective-permute-start(bf16[528,128]{1,0:T(8,128)(2,1)S(1)} %shard_map.66), channel_id=1, source_target_pairs={{0,1},{1,0},{2,3},{3,2},{4,5},{5,4},{6,7},{7,6},{8,15},{9,10},{10,... | collective-permute-start | bytes 405512 | tf_op jit(solution)/shard_map/ppermute | solution.py:30
  50.3 0.3 shard_map.65
  50.6 2.9 %collective-permute-done.14.received = bf16[528,128]{1,0:T(8,128)(2,1)S(1)} collective-permute-done((bf16[528,128]{1,0:T(8,128)(2,1)S(1)}, bf16[528,128]{1,0:T(8,128)(2,1)S(1)}, u32[]{:S(2)}, u32[]{:S(2)}) %collective-permute-start.14) | collective-permute-done | bytes 135200 | tf_op jit(solution)/shard_map/ppermute | solution.py:30
  53.6 1.0 %shard_map.67 = (bf16[512,128]{1,0:T(8,128)(2,1)}, f32[1,512]{1,0:T(1,128)}) custom-call(f32[4,10,8,128]{3,2,1,0:T(8,128)S(1)} %get-tuple-element.49.refs_4_.tables, f32[512,128]{1,0:T(8,128)S(1)} %get-tuple-element.83.mine, f32[512,128]{1,0:T(8,128)S(1)} %get-tuple-element.84.mine_tops, f32[512,128]{1,0:T(8,128)S(1)} %get-tuple-element.85.mine_sums, ...), custom_call_target="tpu_custom_call" | custom-call | bytes 1048576 | tf_op jit(solution)/shard_map/pallas_call | solution.py:281
  (8 shorter events, 0.1 us)
Async XLA Ops:
  1.4 11.4 %collective-permute-start.2 = (bf16[1,2,2,32,128]{4,3,2,1,0:T(8,128)(2,1)S(1)}, bf16[1,2,2,32,128]{4,3,2,1,0:T(8,128)(2,1)S(1)}, u32[]{:S(2)}, u32[]{:S(2)}) collective-permute-start(bf16[1,2,2,32,128]{4,3,2,1,0:T(8,128)(2,1)S(1)} %bitcast.3), channel_id=1, source_target_pairs={{0,4},{1,5},{2,6},{3,7},{4,0},{5,1},{6,2},{7,3},{8,12},{9,13},{10,... | collective-permute-start | bytes 98312 | tf_op jit(solution)/shard_map/ppermute | solution.py:30
  9.1 4.9 %collective-permute-start.1 = (bf16[1,2,2,32,128]{4,3,2,1,0:T(8,128)(2,1)S(1)}, bf16[1,2,2,32,128]{4,3,2,1,0:T(8,128)(2,1)S(1)}, u32[]{:S(2)}, u32[]{:S(2)}) collective-permute-start(bf16[1,2,2,32,128]{4,3,2,1,0:T(8,128)(2,1)S(1)} %bitcast.4), channel_id=1, source_target_pairs={{0,6},{1,7},{2,4},{3,5},{4,2},{5,3},{6,0},{7,1},{8,14},{9,15},{10,... | collective-permute-start | bytes 98312 | tf_op jit(solution)/shard_map/ppermute | solution.py:30
  9.1 3.7 %collective-permute-start = (bf16[1,2,2,32,128]{4,3,2,1,0:T(8,128)(2,1)S(1)}, bf16[1,2,2,32,128]{4,3,2,1,0:T(8,128)(2,1)S(1)}, u32[]{:S(2)}, u32[]{:S(2)}) collective-permute-start(bf16[1,2,2,32,128]{4,3,2,1,0:T(8,128)(2,1)S(1)} %bitcast.5), channel_id=1, source_target_pairs={{0,2},{1,3},{2,0},{3,1},{4,6},{5,7},{6,4},{7,5},{8,10},{9,11},{10,... | collective-permute-start | bytes 98312 | tf_op jit(solution)/shard_map/ppermute | solution.py:30
  14.0 7.9 %collective-permute-start.5 = (bf16[4,2,2,32,128]{4,3,2,1,0:T(8,128)(2,1)S(1)}, bf16[4,2,2,32,128]{4,3,2,1,0:T(8,128)(2,1)S(1)}, u32[]{:S(2)}, u32[]{:S(2)}) collective-permute-start(bf16[4,2,2,32,128]{4,3,2,1,0:T(8,128)(2,1)S(1)} %pad_maximum_fusion.2), channel_id=1, source_target_pairs={{0,32},{1,33},{2,34},{3,35},{4,36},{5,37},{6,38},{7,39},{8,136},{9... | collective-permute-start | bytes 393224 | tf_op jit(solution)/shard_map/ppermute | solution.py:30
  17.0 5.3 %collective-permute-start.4 = (bf16[4,2,2,32,128]{4,3,2,1,0:T(8,128)(2,1)S(1)}, bf16[4,2,2,32,128]{4,3,2,1,0:T(8,128)(2,1)S(1)}, u32[]{:S(2)}, u32[]{:S(2)}) collective-permute-start(bf16[4,2,2,32,128]{4,3,2,1,0:T(8,128)(2,1)S(1)} %pad_maximum_fusion.2), channel_id=1, source_target_pairs={{0,48},{1,49},{2,50},{3,51},{4,52},{5,53},{6,54},{7,55},{8,200},{9... | collective-permute-start | bytes 393224 | tf_op jit(solution)/shard_map/ppermute | solution.py:30
  17.8 4.1 %collective-permute-start.3 = (bf16[4,2,2,32,128]{4,3,2,1,0:T(8,128)(2,1)S(1)}, bf16[4,2,2,32,128]{4,3,2,1,0:T(8,128)(2,1)S(1)}, u32[]{:S(2)}, u32[]{:S(2)}) collective-permute-start(bf16[4,2,2,32,128]{4,3,2,1,0:T(8,128)(2,1)S(1)} %pad_maximum_fusion.2), channel_id=1, source_target_pairs={{0,16},{1,17},{2,18},{3,19},{4,20},{5,21},{6,22},{7,23},{8,72},{9,... | collective-permute-start | bytes 393224 | tf_op jit(solution)/shard_map/ppermute | solution.py:30
  18.8 4.2 %collective-permute-start.6 = (bf16[512,256]{1,0:T(8,128)(2,1)S(1)}, bf16[512,256]{1,0:T(8,128)(2,1)S(1)}, u32[]{:S(2)}, u32[]{:S(2)}) collective-permute-start(bf16[512,256]{1,0:T(8,128)(2,1)S(1)} %pad_maximum_fusion.1.own), channel_id=1, source_target_pairs={{0,8},{1,9},{2,10},{3,11},{4,12},{5,13},{6,14},{7,15},{8,0},{9,1},... | collective-permute-start | bytes 786440 | tf_op jit(solution)/shard_map/ppermute | solution.py:30
  21.9 1.1 %copy-start = (s32[64]{0:T(128)S(1)}, s32[64]{0:T(128)}, u32[]{:S(2)}) copy-start(s32[64]{0:T(128)} %span.1) | copy-start | bytes 772
  23.8 7.0 %collective-permute-start.7 = (bf16[8,2,2,32,128]{4,3,2,1,0:T(8,128)(2,1)S(1)}, bf16[8,2,2,32,128]{4,3,2,1,0:T(8,128)(2,1)S(1)}, u32[]{:S(2)}, u32[]{:S(2)}) collective-permute-start(bf16[8,2,2,32,128]{4,3,2,1,0:T(8,128)(2,1)S(1)} %constant_dynamic-update-slice_fusion.refs_0_), channel_id=1, source_target_pairs={{0,64},{1,65},{2,66},{3,67},{4,68},{5,69},{6,70},{7,71},{8,24},{9,... | collective-permute-start | bytes 786440 | tf_op jit(solution)/shard_map/ppermute | solution.py:30
  25.6 6.4 %collective-permute-start.8 = (bf16[8,2,2,32,128]{4,3,2,1,0:T(8,128)(2,1)S(1)}, bf16[8,2,2,32,128]{4,3,2,1,0:T(8,128)(2,1)S(1)}, u32[]{:S(2)}, u32[]{:S(2)}) collective-permute-start(bf16[8,2,2,32,128]{4,3,2,1,0:T(8,128)(2,1)S(1)} %pad_maximum_fusion.refs_1_), channel_id=1, source_target_pairs={{0,192},{1,193},{2,194},{3,195},{4,196},{5,197},{6,198},{7,199},{8... | collective-permute-start | bytes 786440 | tf_op jit(solution)/shard_map/ppermute | solution.py:30
  27.4 9.3 %collective-permute-start.12 = (bf16[8,2,2,32,128]{4,3,2,1,0:T(8,128)(2,1)S(1)}, bf16[8,2,2,32,128]{4,3,2,1,0:T(8,128)(2,1)S(1)}, u32[]{:S(2)}, u32[]{:S(2)}) collective-permute-start(bf16[8,2,2,32,128]{4,3,2,1,0:T(8,128)(2,1)S(1)} %constant_dynamic-update-slice_fusion.refs_0_), channel_id=1, source_target_pairs={{0,192},{1,193},{2,194},{3,195},{4,196},{5,197},{6,198},{7,199},{8... | collective-permute-start | bytes 786440 | tf_op jit(solution)/shard_map/ppermute | solution.py:30
  28.3 8.5 %collective-permute-start.11 = (bf16[8,2,2,32,128]{4,3,2,1,0:T(8,128)(2,1)S(1)}, bf16[8,2,2,32,128]{4,3,2,1,0:T(8,128)(2,1)S(1)}, u32[]{:S(2)}, u32[]{:S(2)}) collective-permute-start(bf16[8,2,2,32,128]{4,3,2,1,0:T(8,128)(2,1)S(1)} %pad_maximum_fusion.refs_1_), channel_id=1, source_target_pairs={{0,64},{1,65},{2,66},{3,67},{4,68},{5,69},{6,70},{7,71},{8,24},{9,... | collective-permute-start | bytes 786440 | tf_op jit(solution)/shard_map/ppermute | solution.py:30
  32.0 7.6 %collective-permute-start.9 = (bf16[8,2,2,32,128]{4,3,2,1,0:T(8,128)(2,1)S(1)}, bf16[8,2,2,32,128]{4,3,2,1,0:T(8,128)(2,1)S(1)}, u32[]{:S(2)}, u32[]{:S(2)}) collective-permute-start(bf16[8,2,2,32,128]{4,3,2,1,0:T(8,128)(2,1)S(1)} %collective-permute-done.7.refs_0_), channel_id=1, source_target_pairs={{0,192},{1,193},{2,194},{3,195},{4,196},{5,197},{6,198},{7,199},{8... | collective-permute-start | bytes 786440 | tf_op jit(solution)/shard_map/ppermute | solution.py:30
  33.8 5.8 %collective-permute-start.10 = (bf16[8,2,2,32,128]{4,3,2,1,0:T(8,128)(2,1)S(1)}, bf16[8,2,2,32,128]{4,3,2,1,0:T(8,128)(2,1)S(1)}, u32[]{:S(2)}, u32[]{:S(2)}) collective-permute-start(bf16[8,2,2,32,128]{4,3,2,1,0:T(8,128)(2,1)S(1)} %collective-permute-done.8.refs_1_), channel_id=1, source_target_pairs={{0,64},{1,65},{2,66},{3,67},{4,68},{5,69},{6,70},{7,71},{8,24},{9,... | collective-permute-start | bytes 786440 | tf_op jit(solution)/shard_map/ppermute | solution.py:30
  41.2 6.8 %collective-permute-start.13 = (bf16[1056,128]{1,0:T(8,128)(2,1)S(1)}, bf16[1056,128]{1,0:T(8,128)(2,1)S(1)}, u32[]{:S(2)}, u32[]{:S(2)}) collective-permute-start(bf16[1056,128]{1,0:T(8,128)(2,1)S(1)} %shard_map.64), channel_id=1, source_target_pairs={{0,8},{1,9},{2,10},{3,11},{4,12},{5,13},{6,14},{7,15},{8,0},{9,1},... | collective-permute-start | bytes 811016 | tf_op jit(solution)/shard_map/ppermute | solution.py:30
  48.4 5.2 %collective-permute-start.14 = (bf16[528,128]{1,0:T(8,128)(2,1)S(1)}, bf16[528,128]{1,0:T(8,128)(2,1)S(1)}, u32[]{:S(2)}, u32[]{:S(2)}) collective-permute-start(bf16[528,128]{1,0:T(8,128)(2,1)S(1)} %shard_map.66), channel_id=1, source_target_pairs={{0,1},{1,0},{2,3},{3,2},{4,5},{5,4},{6,7},{7,6},{8,15},{9,10},{10,... | collective-permute-start | bytes 405512 | tf_op jit(solution)/shard_map/ppermute | solution.py:30

commit v3 on v2

--- a/solution.py
+++ b/solution.py
@@ -85,17 +85,11 @@
     return jnp.dot(jnp.concatenate(parts, axis=1), jnp.ones((3 * HEAD, HEAD), BF16), preferred_element_type=F32)
 
 
-def prepare(span, place, own, other, both, flags, tables):
+def tabulate(span, place, flags, tables):
     pb, z = place[0], place[1]
     core = pb % 2
     y, x = pb // 8, pb // 2 % 4
     mine = (lowest(span, pb), lowest(span, pb ^ 1))
-    for q, ref in enumerate((own, other)):
-        flag = (span[2 * (pb ^ q)] >= 32).astype(jnp.int32)
-        for half, slot in ((0, flag), (1, 1 - flag)):
-            rows = ref[pl.ds(pl.multiple_of(slot * ROWS, ROWS), ROWS), :]
-            for h in range(2):
-                both[q, h * ROWS : (h + 1) * ROWS, half * HEAD : (half + 1) * HEAD] = rows[:, h * HEAD : (h + 1) * HEAD]
     for part in range(4):
         for i in range(4):
             ty = jnp.where(core == 0, y ^ STEPS[part], y ^ STEPS[i])
@@ -111,38 +105,56 @@
     lane = lax.broadcasted_iota(jnp.int32, (8, HEAD), 1)
     group = z ^ (2 * jnp.where(lane < 64, jnp.where(lane < 32, 0, STEPS[1]), jnp.where(lane < 96, STEPS[2], STEPS[3])))
     tables[0, 8] = (lane % 32 * 8 + group).astype(F32)
-    tables[0, 9] = jnp.full((8, HEAD), jnp.where(span[2 * pb] >= 32, 1.0, 0.0), F32)
+    for q in range(2):
+        value = jnp.full((16, HEAD), jnp.where(span[2 * (pb ^ q)] >= 32, 1.0, 0.0), F32)
+        tables[0, 9 + q] = value[:8]
+        flags[0, 12 + q] = value.astype(BF16)
+
+
+def times(data, tile):
+    n = data.shape[0]
+    return (data.reshape(n // 16, 16, HEAD) * tile[None]).reshape(n, HEAD)
+
+
+def arrange(flags, own, other, both):
+    for q, ref in enumerate((own, other)):
+        flag = flags[0, 12 + q]
+        for h in range(2):
+            lanes = slice(h * HEAD, (h + 1) * HEAD)
+            first, second = ref[:ROWS, lanes], ref[ROWS:, lanes]
+            rows = slice(h * ROWS, (h + 1) * ROWS)
+            both[q, rows, :HEAD] = times(first, 1 - flag) + times(second, flag)
+            both[q, rows, HEAD:] = times(first, flag) + times(second, 1 - flag)
 
 
 def spread_rows(tile, n):
     return jnp.broadcast_to(tile[None], (n // 8, 8, HEAD)).reshape(n, HEAD)
 
 
-def absorb(chips, which, n_blocks, *refs):
+def absorb(chips, which, heads, *refs):
     start, last = chips[0][2] == 0, chips[0][2] == 3
+    n_blocks = 1 + max(c[0] for c in chips)
     blocks, (both, flags, tables), refs = refs[:n_blocks], refs[n_blocks : n_blocks + 3], refs[n_blocks + 3 :]
-    n_chips = len(chips)
     n_old = 0 if start else 3 * len(which)
     olds = [refs[3 * j : 3 * j + 3] for j in range(n_old // 3)]
     refs = refs[n_old:]
-    rows = 2 * ROWS
+    rows = len(heads) * ROWS
     low_keys, low_values, keys, values = refs[-4:]
     outs = refs[:-4]
-
-    def times(data, tile):
-        return (data.reshape(HEAD // 16, 16, HEAD) * tile[None]).reshape(HEAD, HEAD)
-
-    low_values[:, HEAD:] = jnp.ones((n_chips * HEAD, HEAD), BF16)
+    n_chips = len(chips)
+
     kinds, tiles = [], []
     for j, q in enumerate(which):
         kinds.append([tables[part, 4 * q + i] for _, _, part, i in chips])
         if start and q == 0:
             kinds[j].append(jnp.zeros((8, HEAD), F32))
         tiles.append(len(kinds[j]))
+    first_lane = lax.broadcasted_iota(jnp.int32, (HEAD, HEAD), 1) == 0
     for at, (which_block, place, part, i) in enumerate(chips):
         to = slice(at * HEAD, (at + 1) * HEAD)
         flag = flags[part, i]
         block = blocks[which_block]
+        low_values[to, HEAD:] = jnp.where(first_lane, 1.0, 0.0).astype(BF16)
         for kv, low_ref, fold_ref in ((0, low_keys, keys), (1, low_values, values)):
             first = block[4 * place : 4 * place + 4, kv, 0].reshape(HEAD, HEAD)
             second = block[4 * place : 4 * place + 4, kv, 1].reshape(HEAD, HEAD)
@@ -153,32 +165,32 @@
                 kind = flags[part, 4 + 4 * q + i]
                 fold_ref[j, to, 0:HEAD] = times(low, kind)
                 fold_ref[j, to, HEAD:] = times(high, 1 - kind)
-                if tiles[j] == 5 and i == 0:
-                    fold_ref[j, 4 * HEAD :, 0:HEAD] = jnp.zeros((HEAD, HEAD), BF16)
-                    fold_ref[j, 4 * HEAD :, HEAD:] = high
+                if tiles[j] > n_chips and at == 0:
+                    fold_ref[j, n_chips * HEAD :, 0:HEAD] = jnp.zeros((HEAD, HEAD), BF16)
+                    fold_ref[j, n_chips * HEAD :, HEAD:] = high
 
     contract = (((1,), (1,)), ((), ()))
-    scores = []
+    mine = slice(heads[0] * ROWS, heads[0] * ROWS + rows)
     for j, q in enumerate(which):
-        free = lax.dot_general(both[q, :, HEAD:], low_keys[...], contract, preferred_element_type=F32)
-        fold = lax.dot_general(both[q], keys[j, : tiles[j] * HEAD, :], contract, preferred_element_type=F32)
+        kind = kinds[j]
+        free = lax.dot_general(both[q, mine, HEAD:], low_keys[...], contract, preferred_element_type=F32)
+        free = [free[:, i * HEAD : (i + 1) * HEAD] for i in range(n_chips)]
+        fold = lax.dot_general(
+            both[q, mine, :], keys[j, : tiles[j] * HEAD, :], contract, preferred_element_type=F32
+        )
         tile = [fold[:, i * HEAD : (i + 1) * HEAD] for i in range(tiles[j])]
-        if tiles[j] == 5:
+        if tiles[j] > n_chips:
             row = lax.broadcasted_iota(jnp.int32, (rows, HEAD), 0) % ROWS
             edge = spread_rows(tables[0, 8], rows) <= row.astype(F32)
             tile[0] = jnp.where(edge, tile[0], -FAR)
-            tile[4] = jnp.where(edge, tile[4], -FAR)
-        scores.append(([free[:, i * HEAD : (i + 1) * HEAD] for i in range(n_chips)], tile))
-    for j, q in enumerate(which):
-        free, tile = scores[j]
-        kind = kinds[j]
+            tile[-1] = jnp.where(edge, tile[-1], -FAR)
         bests = (
             [t + spread_rows((k - 1.0) * FAR, rows) for t, k in zip(tile, kind)],
             [t - spread_rows(k * FAR, rows) for t, k in zip(tile, kind)] + free,
         )
         bases, factors = [], []
         for k in range(2):
-            at = slice(k * rows, (k + 1) * rows)
+            at = slice(k * 2 * ROWS + mine.start, k * 2 * ROWS + mine.stop)
             top = jnp.max(functools.reduce(jnp.maximum, bests[k]), axis=1, keepdims=True) * SCALE
             if start:
                 top = jnp.broadcast_to(jnp.maximum(top, NEG), (rows, HEAD))
@@ -202,27 +214,27 @@
         weights = [jnp.exp2(t * SCALE - bases[1]).astype(BF16) for t in free]
         free = jnp.dot(jnp.concatenate(weights, axis=1), low_values[...], preferred_element_type=F32)
         parts = (fold[:, :HEAD], fold[:, HEAD:] + free[:, :HEAD])
-        totals = (
-            jnp.broadcast_to(jnp.sum(low_sum, axis=1, keepdims=True), (rows, HEAD)),
-            jnp.sum(high_sum, axis=1, keepdims=True) + free[:, HEAD:],
-        )
+        totals = (low_sum, high_sum + free[:, HEAD:])
         norms = []
         for k in range(2):
-            at = slice(k * rows, (k + 1) * rows)
+            at = slice(k * 2 * ROWS + mine.start, k * 2 * ROWS + mine.stop)
+            to = slice(k * rows, (k + 1) * rows)
             value, total = parts[k], totals[k]
             if not start:
                 value = olds[j][0][at, :] * factors[k] + value
                 total = olds[j][2][at, :] * factors[k] + total
-            if last and q == 1:
+            if last:
+                total = jnp.broadcast_to(jnp.sum(total, axis=1, keepdims=True), (rows, HEAD))
+            if len(outs) == 1:
                 some = total > 0
                 total = jnp.where(some, total, 1.0)
-                outs[0][at, :] = (value / total).astype(BF16)
+                outs[0][to, :] = (value / total).astype(BF16)
                 norms.append(jnp.where(some, bases[k] + jnp.log2(total), NEG))
             else:
-                outs[3 * j][at, :] = value
-                outs[3 * j + 1][at, :] = bases[k]
-                outs[3 * j + 2][at, :] = total
-        if last and q == 1:
+                outs[3 * j][to, :] = value
+                outs[3 * j + 1][to, :] = bases[k]
+                outs[3 * j + 2][to, :] = total
+        if len(outs) == 1:
             pack(outs[0], 2 * rows, jnp.concatenate(norms, axis=0))
 
 
@@ -232,24 +244,12 @@
     return value * a + other * b, best, total * a + b
 
 
-def join(head, acc, tops, sums, received, *outs):
-    norms = []
-    for kind in range(2):
-        for j in range(2):
-            block = kind * 4 + head * 2 + j
-            rows = slice(block * HEAD, (block + 1) * HEAD)
-            to = slice((kind * 2 + j) * HEAD, (kind * 2 + j + 1) * HEAD)
-            norm = unpack(received, 4 * ROWS, block)
-            value, top, total = merge(acc[rows, :], tops[rows, :], sums[rows, :], received[rows, :].astype(F32), norm)
-            if head == 0:
-                outs[0][to, :], outs[1][to, :], outs[2][to, :] = value, top, total
-            else:
-                some = total > 0
-                total = jnp.where(some, total, 1.0)
-                outs[0][to, :] = (value / total).astype(BF16)
-                norms.append(jnp.where(some, top + jnp.log2(total), NEG))
-    if head == 1:
-        pack(outs[0], 2 * ROWS, jnp.concatenate(norms, axis=0))
+def join(acc, tops, sums, received, *outs):
+    for block in range(4):
+        rows = slice(block * HEAD, (block + 1) * HEAD)
+        norm = unpack(received, 2 * ROWS, block)
+        state = merge(acc[rows, :], tops[rows, :], sums[rows, :], received[rows, :].astype(F32), norm)
+        outs[0][rows, :], outs[1][rows, :], outs[2][rows, :] = state
 
 
 def close(tables, mine, mine_tops, mine_sums, received, attended, log_norm):
@@ -277,7 +277,7 @@
             log_norm[:, rows] = jnp.where(flag[0:1] > 0, *pair)
 
 
-def call(body, outs, *args, scalars=0, scratch=(), aliases=None, flops=0, moved=2**20, exps=0):
+def call(body, outs, *args, scalars=0, scratch=(), aliases=None):
     return pl.pallas_call(
         body,
         out_shape=outs,
@@ -286,7 +286,7 @@
         scratch_shapes=list(scratch),
         input_output_aliases=aliases or {},
         compiler_params=pltpu.CompilerParams(vmem_limit_bytes=40 * 2**20),
-        cost_estimate=pl.CostEstimate(flops=flops, bytes_accessed=moved, transcendentals=exps),
+        cost_estimate=pl.CostEstimate(flops=1024, bytes_accessed=1024, transcendentals=0),
     )(*args)
 
 
@@ -294,14 +294,13 @@
     return jax.ShapeDtypeStruct(dims, dtype)
 
 
-def attend(chips, which, blocks, ready, state):
+def attend(chips, which, blocks, ready, state, heads=(0, 1), message=False):
     n, n_chips = len(which), len(chips)
-    start = chips[0][2] == 0
-    message = chips[0][2] == 3 and which == (1,)
-    outs = [shape(4 * ROWS + 32, HEAD, dtype=BF16)] if message else [shape(4 * ROWS, HEAD)] * (3 * n)
-    wide = n_chips + 1 if start else n_chips
+    rows = 2 * len(heads) * ROWS
+    outs = [shape(rows + 16, HEAD, dtype=BF16)] if message else [shape(rows, HEAD)] * (3 * n)
+    wide = n_chips + 1 if chips[0][2] == 0 else n_chips
     return call(
-        functools.partial(absorb, chips, which, len(blocks)),
+        functools.partial(absorb, chips, which, heads),
         outs,
         *blocks,
         *ready,
@@ -312,23 +311,14 @@
             pltpu.VMEM((n, wide * HEAD, 2 * HEAD), BF16),
             pltpu.VMEM((n, wide * HEAD, 2 * HEAD), BF16),
         ],
-        aliases={} if start or message else {len(blocks) + 3 + i: i for i in range(3 * n)},
-        flops=n * n_chips * 1024 * 1024 * HEAD,
-        moved=n * 2 * 2**20,
-        exps=n * n_chips * 128 * 1024,
+        aliases={len(blocks) + 3 + i: i for i in range(3 * n)} if state and len(heads) == 2 else {},
     )
 
 
 def get_ready(span_of, place, own, other):
-    return call(
-        prepare,
-        [shape(2, 2 * ROWS, 2 * HEAD, dtype=BF16), shape(4, 12, 16, HEAD, dtype=BF16), shape(4, 10, 8, HEAD)],
-        span_of,
-        place,
-        own,
-        other,
-        scalars=2,
-    )
+    flags, tables = call(tabulate, [shape(4, 14, 16, HEAD, dtype=BF16), shape(4, 11, 8, HEAD)], span_of, place, scalars=2)
+    (both,) = call(arrange, [shape(2, 2 * ROWS, 2 * HEAD, dtype=BF16)], flags, own, other)
+    return both, flags, tables
 
 
 def swap_cores(y, x, c, z):
@@ -356,21 +346,22 @@
     state = attend([(i // 2, i % 2, 0, i) for i in range(4)], (0, 1), rows, ready, ())
     near[0], far[1], *state = lax.optimization_barrier((near[0], far[1], *state))
     across = [send(near[0], along_second(STEPS[2])), send(far[1], along_second(STEPS[1]))]
-    first = [(0, 0, 1, 0), (0, 1, 1, 1), (1, 0, 2, 2), (1, 1, 2, 3)]
-    state = attend(first, (0, 1), [near[0], far[1]], ready, state)
-    second = [(0, 0, 1, 2), (0, 1, 1, 3), (1, 0, 2, 0), (1, 1, 2, 1)]
-    state = attend(second, (0, 1), [near[1], far[0]], ready, state)
-    last = [(i // 2, i % 2, 3, i) for i in range(4)]
-    (message,) = attend(last, (1,), across, ready, state[3:])
-    received = send(message, swap_cores)
-    state = attend(last, (0,), across, ready, state[:3])
+    chips = [(2 * part + i // 2, i % 2, 1 + part, i) for part in range(2) for i in range(4)]
+    state = attend(chips, (0, 1), near + far, ready, state)
+
+    chips = [(i // 2, i % 2, 3, i) for i in range(4)]
+    (message,) = attend(chips, (1,), across, ready, state[3:], (1,), True)
+    cross = send(message, lambda y, x, c, z: (y, x, 1 - c, partner(1 - c, z)))
+    (message,) = attend(chips, (0,), across, ready, state[:3], (1,), True)
+    message, *state = lax.optimization_barrier((message, *state))
+    side = send(message, lambda y, x, c, z: (y, x, c, partner(c, z)))
+    (message,) = attend(chips, (1,), across, ready, state[3:], (0,), True)
+    mate = send(message, swap_cores)
+    state = attend(chips, (0,), across, ready, state[:3], (0,))
     half = 2 * ROWS
-    (message,) = call(
-        functools.partial(join, 1), [shape(half + 16, HEAD, dtype=BF16)], *state, received
-    )
-    mine = call(functools.partial(join, 0), [shape(half, HEAD)] * 3, *state, received)
-    received = send(message, lambda y, x, c, z: (y, x, c, partner(c, z)))
-    return tuple(call(close, [shape(half, HEAD, dtype=BF16), shape(1, half)], ready[2], *mine, received))
+    for message in (cross, side):
+        state = call(join, [shape(half, HEAD)] * 3, *state, message)
+    return tuple(call(close, [shape(half, HEAD, dtype=BF16), shape(1, half)], tables, *state, mate))
 
 
 def solution(mesh):

time: 54.9 us -> 52.7 us (0.960)
  waiting for transfers between devices: 8.88 us -> 6.58 us
  Pallas kernels: 13.7 us -> 12.9 us
  local copies, waits for them, and re-layouts: 1.05 us -> 1.63 us
    ppermute x15 -> x16, waiting for transfers between devices: 8.88 us -> 6.58 us  [send(): return lax.ppermute(value, AXES, pairs)]
    pallas_call x9 -> x11, Pallas kernels: 13.7 us -> 12.9 us  [call(): pl.pallas_call(body, out_shape=outs, in_specs=[pl.BlockSpec(memory_space=...]
    unnamed x6, local copies, waits for them, and re-layouts: 0.04 us -> 0.61 us
    ppermute x15 -> x16, starting transfers between devices: 29.3 us -> 29.7 us  [send(): return lax.ppermute(value, AXES, pairs)]
  transfers between devices with their start and end apart: 15 -> 16, of which waited for: 6 -> 7; matrix products, arithmetic and copies ran while one was open for 2% -> 2% of each run, Pallas kernels for 18% -> 21%
where the time goes in v3:
time: 52.7 us; the launch traced here: 52.4 us
  starting transfers between devices  29.7 us (56%)
  Pallas kernels  12.9 us (24%)
  waiting for transfers between devices  6.58 us (12%)
  local copies, waits for them, and re-layouts  1.63 us (3%)
  other arithmetic  0.89 us (2%)
  between operations  0.8 us (2%)
    ppermute x16, starting transfers between devices, send(): return lax.ppermute(value, AXES, pairs)  29.7 us
    pallas_call x11, Pallas kernels, call(): pl.pallas_call(body, out_shape=outs, in_specs=[pl.BlockSpec(memory_space=...  12.9 us
    ppermute x16, waiting for transfers between devices, send(): return lax.ppermute(value, AXES, pairs)  6.58 us
  transfers between devices with their start and end apart: 16, of which 7 were waited for; matrix products, arithmetic and copies ran while one was open for 2% of the time, Pallas kernels for 21%

profile of v3, /device:TPU:1, one launch (start us, length us, event | category | flops | bytes accessed | tf_op | source)
XLA Modules:
  0.0 52.4 jit_solution(11105942866351174467)
XLA Ops:
  0.6 0.7 %pad_maximum_fusion.3 = bf16[2,64,128]{2,1,0:T(8,128)(2,1)S(1)} fusion(bf16[1,64,128]{2,1,0:T(8,128)(2,1)} %param.6, bf16[1,64,128]{2,1,0:T(8,128)(2,1)} %param.5), kind=kLoop, calls=%fused_computation.3 | loop fusion | flops 16384 | bytes 65536 | tf_op jit(solution)/shard_map/stack | solution.py:332
  1.4 7.7 %collective-permute-start.2 = (bf16[1,2,2,32,128]{4,3,2,1,0:T(8,128)(2,1)S(1)}, bf16[1,2,2,32,128]{4,3,2,1,0:T(8,128)(2,1)S(1)}, u32[]{:S(2)}, u32[]{:S(2)}) collective-permute-start(bf16[1,2,2,32,128]{4,3,2,1,0:T(8,128)(2,1)S(1)} %bitcast.3), channel_id=1, source_target_pairs={{0,4},{1,5},{2,6},{3,7},{4,0},{5,1},{6,2},{7,3},{8,12},{9,13},{10,... | collective-permute-start | bytes 98312 | tf_op jit(solution)/shard_map/ppermute | solution.py:30
  9.1 0.0 collective-permute-start.1
  9.1 1.2 %collective-permute-start = (bf16[1,2,2,32,128]{4,3,2,1,0:T(8,128)(2,1)S(1)}, bf16[1,2,2,32,128]{4,3,2,1,0:T(8,128)(2,1)S(1)}, u32[]{:S(2)}, u32[]{:S(2)}) collective-permute-start(bf16[1,2,2,32,128]{4,3,2,1,0:T(8,128)(2,1)S(1)} %bitcast.5), channel_id=1, source_target_pairs={{0,2},{1,3},{2,0},{3,1},{4,6},{5,7},{6,4},{7,5},{8,10},{9,11},{10,... | collective-permute-start | bytes 98312 | tf_op jit(solution)/shard_map/ppermute | solution.py:30
  10.3 0.0 copy-start
  10.3 0.1 pad_add_fusion.place
  10.4 0.6 %copy-done = s32[64]{0:T(128)S(1)} copy-done((s32[64]{0:T(128)S(1)}, s32[64]{0:T(128)}, u32[]{:S(2)}) %copy-start) | copy-done | bytes 280
  11.0 0.7 %shard_map.59 = (bf16[4,14,16,128]{3,2,1,0:T(8,128)(2,1)S(1)}, f32[4,11,8,128]{3,2,1,0:T(8,128)S(1)}) custom-call(s32[64]{0:T(128)S(1)} %copy-done, s32[2]{0:T(128)S(1)} %pad_add_fusion.place), custom_call_target="tpu_custom_call" | custom-call | flops 1024 | bytes 1024 | tf_op jit(solution)/shard_map/pallas_call | solution.py:281
  11.7 1.1 %collective-permute-done = bf16[1,2,2,32,128]{4,3,2,1,0:T(8,128)(2,1)S(1)} collective-permute-done((bf16[1,2,2,32,128]{4,3,2,1,0:T(8,128)(2,1)S(1)}, bf16[1,2,2,32,128]{4,3,2,1,0:T(8,128)(2,1)S(1)}, u32[]{:S(2)}, u32[]{:S(2)}) %collective-permute-start) | collective-permute-done | bytes 32800 | tf_op jit(solution)/shard_map/ppermute | solution.py:30
  12.8 0.0 collective-permute-done.2
  12.8 1.2 %collective-permute-done.1 = bf16[1,2,2,32,128]{4,3,2,1,0:T(8,128)(2,1)S(1)} collective-permute-done((bf16[1,2,2,32,128]{4,3,2,1,0:T(8,128)(2,1)S(1)}, bf16[1,2,2,32,128]{4,3,2,1,0:T(8,128)(2,1)S(1)}, u32[]{:S(2)}, u32[]{:S(2)}) %collective-permute-start.1) | collective-permute-done | bytes 32800 | tf_op jit(solution)/shard_map/ppermute | solution.py:30
  14.0 3.0 %collective-permute-start.5 = (bf16[4,2,2,32,128]{4,3,2,1,0:T(8,128)(2,1)S(1)}, bf16[4,2,2,32,128]{4,3,2,1,0:T(8,128)(2,1)S(1)}, u32[]{:S(2)}, u32[]{:S(2)}) collective-permute-start(bf16[4,2,2,32,128]{4,3,2,1,0:T(8,128)(2,1)S(1)} %pad_maximum_fusion.2), channel_id=1, source_target_pairs={{0,32},{1,33},{2,34},{3,35},{4,36},{5,37},{6,38},{7,39},{8,136},{9... | collective-permute-start | bytes 393224 | tf_op jit(solution)/shard_map/ppermute | solution.py:30
  17.0 0.8 %collective-permute-start.4 = (bf16[4,2,2,32,128]{4,3,2,1,0:T(8,128)(2,1)S(1)}, bf16[4,2,2,32,128]{4,3,2,1,0:T(8,128)(2,1)S(1)}, u32[]{:S(2)}, u32[]{:S(2)}) collective-permute-start(bf16[4,2,2,32,128]{4,3,2,1,0:T(8,128)(2,1)S(1)} %pad_maximum_fusion.2), channel_id=1, source_target_pairs={{0,48},{1,49},{2,50},{3,51},{4,52},{5,53},{6,54},{7,55},{8,200},{9... | collective-permute-start | bytes 393224 | tf_op jit(solution)/shard_map/ppermute | solution.py:30
  17.8 0.0 collective-permute-start.3
  17.8 1.0 %constant_dynamic-slice_fusion.1 = (bf16[512,128]{1,0:T(8,128)(2,1)S(1)}, bf16[512,128]{1,0:T(8,128)(2,1)S(1)}) fusion(bf16[512,1024]{1,0:T(8,128)(2,1)} %param.4, s32[]{:T(128)S(6)} %select_n.24, s32[]{:T(128)S(6)} %select_n.29), kind=kLoop, calls=%fused_computation.11 | loop fusion | bytes 524296 | tf_op jit(solution)/shard_map/dynamic_slice | solution.py:336
  18.8 3.0 %collective-permute-start.6 = (bf16[512,256]{1,0:T(8,128)(2,1)S(1)}, bf16[512,256]{1,0:T(8,128)(2,1)S(1)}, u32[]{:S(2)}, u32[]{:S(2)}) collective-permute-start(bf16[512,256]{1,0:T(8,128)(2,1)S(1)} %pad_maximum_fusion.1.own), channel_id=1, source_target_pairs={{0,8},{1,9},{2,10},{3,11},{4,12},{5,13},{6,14},{7,15},{8,0},{9,1},... | collective-permute-start | bytes 786440 | tf_op jit(solution)/shard_map/ppermute | solution.py:30
  21.9 0.0 collective-permute-done.3
  21.9 0.0 collective-permute-done.5
  21.9 0.4 collective-permute-done.4
  22.4 0.7 %collective-permute-done.6.other = bf16[512,256]{1,0:T(8,128)(2,1)S(1)} collective-permute-done((bf16[512,256]{1,0:T(8,128)(2,1)S(1)}, bf16[512,256]{1,0:T(8,128)(2,1)S(1)}, u32[]{:S(2)}, u32[]{:S(2)}) %collective-permute-start.6) | collective-permute-done | bytes 262176 | tf_op jit(solution)/shard_map/ppermute | solution.py:30
  23.0 0.1 shard_map.60.refs_2_.refs_4_
  23.1 1.8 %collective-permute-start.7 = (bf16[8,2,2,32,128]{4,3,2,1,0:T(8,128)(2,1)S(1)}, bf16[8,2,2,32,128]{4,3,2,1,0:T(8,128)(2,1)S(1)}, u32[]{:S(2)}, u32[]{:S(2)}) collective-permute-start(bf16[8,2,2,32,128]{4,3,2,1,0:T(8,128)(2,1)S(1)} %constant_dynamic-update-slice_fusion.refs_0_), channel_id=1, source_target_pairs={{0,64},{1,65},{2,66},{3,67},{4,68},{5,69},{6,70},{7,71},{8,24},{9,... | collective-permute-start | bytes 786440 | tf_op jit(solution)/shard_map/ppermute | solution.py:30
  25.0 1.8 %collective-permute-start.8 = (bf16[8,2,2,32,128]{4,3,2,1,0:T(8,128)(2,1)S(1)}, bf16[8,2,2,32,128]{4,3,2,1,0:T(8,128)(2,1)S(1)}, u32[]{:S(2)}, u32[]{:S(2)}) collective-permute-start(bf16[8,2,2,32,128]{4,3,2,1,0:T(8,128)(2,1)S(1)} %pad_maximum_fusion.refs_1_), channel_id=1, source_target_pairs={{0,192},{1,193},{2,194},{3,195},{4,196},{5,197},{6,198},{7,199},{8... | collective-permute-start | bytes 786440 | tf_op jit(solution)/shard_map/ppermute | solution.py:30
  26.8 0.9 %collective-permute-start.12 = (bf16[8,2,2,32,128]{4,3,2,1,0:T(8,128)(2,1)S(1)}, bf16[8,2,2,32,128]{4,3,2,1,0:T(8,128)(2,1)S(1)}, u32[]{:S(2)}, u32[]{:S(2)}) collective-permute-start(bf16[8,2,2,32,128]{4,3,2,1,0:T(8,128)(2,1)S(1)} %constant_dynamic-update-slice_fusion.refs_0_), channel_id=1, source_target_pairs={{0,192},{1,193},{2,194},{3,195},{4,196},{5,197},{6,198},{7,199},{8... | collective-permute-start | bytes 786440 | tf_op jit(solution)/shard_map/ppermute | solution.py:30
  27.6 0.0 collective-permute-start.11
  27.7 2.4 %shard_map.61 = (f32[1024,128]{1,0:T(8,128)S(1)}, f32[1024,128]{1,0:T(8,128)S(1)}, f32[1024,128]{1,0:T(8,128)S(1)}, f32[1024,128]{1,0:T(8,128)S(1)}, f32[1024,128]{1,0:T(8,128)S(1)}, /*index=5*/f32[1024,128]{1,0:T(8,128)S(1)}) custom-call(bf16[8,2,2,32,128]{4,3,2,1,0:T(8,128)(2,1)S(1)} %constant_dynamic-update-slice_fusion.refs_0_, ...), custom_call_target="tpu_custom_call" | custom-call | flops 1024 | bytes 1024 | tf_op jit(solution)/shard_map/pallas_call | solution.py:281
  30.1 0.0 collective-permute-done.7.refs_0_
  30.1 1.3 %collective-permute-done.8.refs_3_ = bf16[8,2,2,32,128]{4,3,2,1,0:T(8,128)(2,1)S(1)} collective-permute-done((bf16[8,2,2,32,128]{4,3,2,1,0:T(8,128)(2,1)S(1)}, bf16[8,2,2,32,128]{4,3,2,1,0:T(8,128)(2,1)S(1)}, u32[]{:S(2)}, u32[]{:S(2)}) %collective-permute-start.8) | collective-permute-done | bytes 262176 | tf_op jit(solution)/shard_map/ppermute | solution.py:30
  31.4 1.8 %collective-permute-start.9 = (bf16[8,2,2,32,128]{4,3,2,1,0:T(8,128)(2,1)S(1)}, bf16[8,2,2,32,128]{4,3,2,1,0:T(8,128)(2,1)S(1)}, u32[]{:S(2)}, u32[]{:S(2)}) collective-permute-start(bf16[8,2,2,32,128]{4,3,2,1,0:T(8,128)(2,1)S(1)} %collective-permute-done.7.refs_0_), channel_id=1, source_target_pairs={{0,192},{1,193},{2,194},{3,195},{4,196},{5,197},{6,198},{7,199},{8... | collective-permute-start | bytes 786440 | tf_op jit(solution)/shard_map/ppermute | solution.py:30
  33.2 0.0 collective-permute-start.10
  33.2 1.3 %collective-permute-done.12.refs_2_ = bf16[8,2,2,32,128]{4,3,2,1,0:T(8,128)(2,1)S(1)} collective-permute-done((bf16[8,2,2,32,128]{4,3,2,1,0:T(8,128)(2,1)S(1)}, bf16[8,2,2,32,128]{4,3,2,1,0:T(8,128)(2,1)S(1)}, u32[]{:S(2)}, u32[]{:S(2)}) %collective-permute-start.12) | collective-permute-done | bytes 262176 | tf_op jit(solution)/shard_map/ppermute | solution.py:30
  34.5 0.0 collective-permute-done.11.refs_1_
  34.5 4.3 %shard_map.62 = (f32[1024,128]{1,0:T(8,128)S(1)}, f32[1024,128]{1,0:T(8,128)S(1)}, f32[1024,128]{1,0:T(8,128)S(1)}, f32[1024,128]{1,0:T(8,128)S(1)}, f32[1024,128]{1,0:T(8,128)S(1)}, /*index=5*/f32[1024,128]{1,0:T(8,128)S(1)}) custom-call(bf16[8,2,2,32,128]{4,3,2,1,0:T(8,128)(2,1)S(1)} %collect, ...), custom_call_target="tpu_custom_call", output_to_operand_aliasing={{0}: (7, {}), {1}: (8, {}), {2}: (9, {}), {3}: (10, {}), {4... | custom-call | flops 1024 | bytes 1024 | tf_op jit(solution)/shard_map/pallas_call | solution.py:281
  38.8 0.0 collective-permute-done.9.refs_0_
  38.8 0.0 collective-permute-done.10.refs_1_
  38.8 0.9 %shard_map.65 = bf16[528,128]{1,0:T(8,128)(2,1)S(1)} custom-call(bf16[8,2,2,32,128]{4,3,2,1,0:T(8,128)(2,1)S(1)} %collective-permute-done.9.refs_0_, bf16[8,2,2,32,128]{4,3,2,1,0:T(8,128)(2,1)S(1)} %collective-permute-done.10.refs_1_, bf16[2,512,256]{2,1,0:T(8,128)(2,1)S(1)} %shard_map.60.refs_2_.refs_4_, ...), custom_call_target="tpu_custom_call" | custom-call | flops 1024 | bytes 1024 | tf_op jit(solution)/shard_map/pallas_call | solution.py:281
  39.8 5.3 %collective-permute-start.13 = (bf16[528,128]{1,0:T(8,128)(2,1)S(1)}, bf16[528,128]{1,0:T(8,128)(2,1)S(1)}, u32[]{:S(2)}, u32[]{:S(2)}) collective-permute-start(bf16[528,128]{1,0:T(8,128)(2,1)S(1)} %shard_map.65), channel_id=1, source_target_pairs={{0,15},{1,10},{2,9},{3,12},{4,11},{5,14},{6,13},{7,8},{8,1},{9,0},... | collective-permute-start | bytes 405512 | tf_op jit(solution)/shard_map/ppermute | solution.py:30
  45.0 0.9 %shard_map.63 = bf16[528,128]{1,0:T(8,128)(2,1)S(1)} custom-call(bf16[8,2,2,32,128]{4,3,2,1,0:T(8,128)(2,1)S(1)} %collective-permute-done.9.refs_0_, bf16[8,2,2,32,128]{4,3,2,1,0:T(8,128)(2,1)S(1)} %collective-permute-done.10.refs_1_, bf16[2,512,256]{2,1,0:T(8,128)(2,1)S(1)} %shard_map.60.refs_2_.refs_4_, ...), custom_call_target="tpu_custom_call" | custom-call | flops 1024 | bytes 1024 | tf_op jit(solution)/shard_map/pallas_call | solution.py:281
  46.0 2.3 %collective-permute-start.14 = (bf16[528,128]{1,0:T(8,128)(2,1)S(1)}, bf16[528,128]{1,0:T(8,128)(2,1)S(1)}, u32[]{:S(2)}, u32[]{:S(2)}) collective-permute-start(bf16[528,128]{1,0:T(8,128)(2,1)S(1)} %shard_map.63), channel_id=1, source_target_pairs={{0,1},{1,0},{2,3},{3,2},{4,5},{5,4},{6,7},{7,6},{8,15},{9,10},{10,... | collective-permute-start | bytes 405512 | tf_op jit(solution)/shard_map/ppermute | solution.py:30
  48.2 0.9 %shard_map.68 = bf16[528,128]{1,0:T(8,128)(2,1)S(1)} custom-call(bf16[8,2,2,32,128]{4,3,2,1,0:T(8,128)(2,1)S(1)} %collective-permute-done.9.refs_0_, bf16[8,2,2,32,128]{4,3,2,1,0:T(8,128)(2,1)S(1)} %collective-permute-done.10.refs_1_, bf16[2,512,256]{2,1,0:T(8,128)(2,1)S(1)} %shard_map.60.refs_2_.refs_4_, ...), custom_call_target="tpu_custom_call" | custom-call | flops 1024 | bytes 1024 | tf_op jit(solution)/shard_map/pallas_call | solution.py:281
  49.2 0.1 collective-permute-start.15
  49.3 1.0 %shard_map.64 = (f32[512,128]{1,0:T(8,128)S(1)}, f32[512,128]{1,0:T(8,128)S(1)}, f32[512,128]{1,0:T(8,128)S(1)}) custom-call(bf16[8,2,2,32,128]{4,3,2,1,0:T(8,128)(2,1)S(1)} %collective-permute-done.9.refs_0_, bf16[8,2,2,32,128]{4,3,2,1,0:T(8,128)(2,1)S(1)} %collective-permute-done.10.refs_1_, bf16[2,512,256]{2,1,0:T(8,128)(2,1)S(1)} %shard_map.60.refs_2_.refs_4_, ...), custom_call_target="tpu_custom_call" | custom-call | flops 1024 | bytes 1024 | tf_op jit(solution)/shard_map/pallas_call | solution.py:281
  50.2 0.0 collective-permute-done.13.received
  50.2 0.3 shard_map.66
  50.5 0.6 %collective-permute-done.14.received = bf16[528,128]{1,0:T(8,128)(2,1)S(1)} collective-permute-done((bf16[528,128]{1,0:T(8,128)(2,1)S(1)}, bf16[528,128]{1,0:T(8,128)(2,1)S(1)}, u32[]{:S(2)}, u32[]{:S(2)}) %collective-permute-start.14) | collective-permute-done | bytes 135200 | tf_op jit(solution)/shard_map/ppermute | solution.py:30
  51.1 0.3 shard_map.67
  51.4 0.0 collective-permute-done.15.received
  51.4 1.0 %shard_map.69 = (bf16[512,128]{1,0:T(8,128)(2,1)}, f32[1,512]{1,0:T(1,128)}) custom-call(f32[4,11,8,128]{3,2,1,0:T(8,128)S(1)} %get-tuple-element.51.refs_4_.refs_6_.tables, f32[512,128]{1,0:T(8,128)S(1)} %get-tuple-element.86.mine, f32[512,128]{1,0:T(8,128)S(1)} %get-tuple-element.87.mine_tops, f32[512,128]{1,0:T(8,128)S(1)} %get-tuple-element.88.mine_sums, ...), custom_call_target="tpu_custom_call" | custom-call | flops 1024 | bytes 1024 | tf_op jit(solution)/shard_map/pallas_call | solution.py:281
  (8 shorter events, 0.1 us)
Async XLA Ops:
  1.4 11.4 %collective-permute-start.2 = (bf16[1,2,2,32,128]{4,3,2,1,0:T(8,128)(2,1)S(1)}, bf16[1,2,2,32,128]{4,3,2,1,0:T(8,128)(2,1)S(1)}, u32[]{:S(2)}, u32[]{:S(2)}) collective-permute-start(bf16[1,2,2,32,128]{4,3,2,1,0:T(8,128)(2,1)S(1)} %bitcast.3), channel_id=1, source_target_pairs={{0,4},{1,5},{2,6},{3,7},{4,0},{5,1},{6,2},{7,3},{8,12},{9,13},{10,... | collective-permute-start | bytes 98312 | tf_op jit(solution)/shard_map/ppermute | solution.py:30
  9.1 4.9 %collective-permute-start.1 = (bf16[1,2,2,32,128]{4,3,2,1,0:T(8,128)(2,1)S(1)}, bf16[1,2,2,32,128]{4,3,2,1,0:T(8,128)(2,1)S(1)}, u32[]{:S(2)}, u32[]{:S(2)}) collective-permute-start(bf16[1,2,2,32,128]{4,3,2,1,0:T(8,128)(2,1)S(1)} %bitcast.4), channel_id=1, source_target_pairs={{0,6},{1,7},{2,4},{3,5},{4,2},{5,3},{6,0},{7,1},{8,14},{9,15},{10,... | collective-permute-start | bytes 98312 | tf_op jit(solution)/shard_map/ppermute | solution.py:30
  9.1 3.7 %collective-permute-start = (bf16[1,2,2,32,128]{4,3,2,1,0:T(8,128)(2,1)S(1)}, bf16[1,2,2,32,128]{4,3,2,1,0:T(8,128)(2,1)S(1)}, u32[]{:S(2)}, u32[]{:S(2)}) collective-permute-start(bf16[1,2,2,32,128]{4,3,2,1,0:T(8,128)(2,1)S(1)} %bitcast.5), channel_id=1, source_target_pairs={{0,2},{1,3},{2,0},{3,1},{4,6},{5,7},{6,4},{7,5},{8,10},{9,11},{10,... | collective-permute-start | bytes 98312 | tf_op jit(solution)/shard_map/ppermute | solution.py:30
  10.3 0.7 %copy-start = (s32[64]{0:T(128)S(1)}, s32[64]{0:T(128)}, u32[]{:S(2)}) copy-start(s32[64]{0:T(128)} %span.1) | copy-start | bytes 772
  14.0 7.9 %collective-permute-start.5 = (bf16[4,2,2,32,128]{4,3,2,1,0:T(8,128)(2,1)S(1)}, bf16[4,2,2,32,128]{4,3,2,1,0:T(8,128)(2,1)S(1)}, u32[]{:S(2)}, u32[]{:S(2)}) collective-permute-start(bf16[4,2,2,32,128]{4,3,2,1,0:T(8,128)(2,1)S(1)} %pad_maximum_fusion.2), channel_id=1, source_target_pairs={{0,32},{1,33},{2,34},{3,35},{4,36},{5,37},{6,38},{7,39},{8,136},{9... | collective-permute-start | bytes 393224 | tf_op jit(solution)/shard_map/ppermute | solution.py:30
  17.0 5.3 %collective-permute-start.4 = (bf16[4,2,2,32,128]{4,3,2,1,0:T(8,128)(2,1)S(1)}, bf16[4,2,2,32,128]{4,3,2,1,0:T(8,128)(2,1)S(1)}, u32[]{:S(2)}, u32[]{:S(2)}) collective-permute-start(bf16[4,2,2,32,128]{4,3,2,1,0:T(8,128)(2,1)S(1)} %pad_maximum_fusion.2), channel_id=1, source_target_pairs={{0,48},{1,49},{2,50},{3,51},{4,52},{5,53},{6,54},{7,55},{8,200},{9... | collective-permute-start | bytes 393224 | tf_op jit(solution)/shard_map/ppermute | solution.py:30
  17.8 4.1 %collective-permute-start.3 = (bf16[4,2,2,32,128]{4,3,2,1,0:T(8,128)(2,1)S(1)}, bf16[4,2,2,32,128]{4,3,2,1,0:T(8,128)(2,1)S(1)}, u32[]{:S(2)}, u32[]{:S(2)}) collective-permute-start(bf16[4,2,2,32,128]{4,3,2,1,0:T(8,128)(2,1)S(1)} %pad_maximum_fusion.2), channel_id=1, source_target_pairs={{0,16},{1,17},{2,18},{3,19},{4,20},{5,21},{6,22},{7,23},{8,72},{9,... | collective-permute-start | bytes 393224 | tf_op jit(solution)/shard_map/ppermute | solution.py:30
  18.8 4.2 %collective-permute-start.6 = (bf16[512,256]{1,0:T(8,128)(2,1)S(1)}, bf16[512,256]{1,0:T(8,128)(2,1)S(1)}, u32[]{:S(2)}, u32[]{:S(2)}) collective-permute-start(bf16[512,256]{1,0:T(8,128)(2,1)S(1)} %pad_maximum_fusion.1.own), channel_id=1, source_target_pairs={{0,8},{1,9},{2,10},{3,11},{4,12},{5,13},{6,14},{7,15},{8,0},{9,1},... | collective-permute-start | bytes 786440 | tf_op jit(solution)/shard_map/ppermute | solution.py:30
  23.1 6.9 %collective-permute-start.7 = (bf16[8,2,2,32,128]{4,3,2,1,0:T(8,128)(2,1)S(1)}, bf16[8,2,2,32,128]{4,3,2,1,0:T(8,128)(2,1)S(1)}, u32[]{:S(2)}, u32[]{:S(2)}) collective-permute-start(bf16[8,2,2,32,128]{4,3,2,1,0:T(8,128)(2,1)S(1)} %constant_dynamic-update-slice_fusion.refs_0_), channel_id=1, source_target_pairs={{0,64},{1,65},{2,66},{3,67},{4,68},{5,69},{6,70},{7,71},{8,24},{9,... | collective-permute-start | bytes 786440 | tf_op jit(solution)/shard_map/ppermute | solution.py:30
  25.0 6.4 %collective-permute-start.8 = (bf16[8,2,2,32,128]{4,3,2,1,0:T(8,128)(2,1)S(1)}, bf16[8,2,2,32,128]{4,3,2,1,0:T(8,128)(2,1)S(1)}, u32[]{:S(2)}, u32[]{:S(2)}) collective-permute-start(bf16[8,2,2,32,128]{4,3,2,1,0:T(8,128)(2,1)S(1)} %pad_maximum_fusion.refs_1_), channel_id=1, source_target_pairs={{0,192},{1,193},{2,194},{3,195},{4,196},{5,197},{6,198},{7,199},{8... | collective-permute-start | bytes 786440 | tf_op jit(solution)/shard_map/ppermute | solution.py:30
  26.8 7.7 %collective-permute-start.12 = (bf16[8,2,2,32,128]{4,3,2,1,0:T(8,128)(2,1)S(1)}, bf16[8,2,2,32,128]{4,3,2,1,0:T(8,128)(2,1)S(1)}, u32[]{:S(2)}, u32[]{:S(2)}) collective-permute-start(bf16[8,2,2,32,128]{4,3,2,1,0:T(8,128)(2,1)S(1)} %constant_dynamic-update-slice_fusion.refs_0_), channel_id=1, source_target_pairs={{0,192},{1,193},{2,194},{3,195},{4,196},{5,197},{6,198},{7,199},{8... | collective-permute-start | bytes 786440 | tf_op jit(solution)/shard_map/ppermute | solution.py:30
  27.6 6.9 %collective-permute-start.11 = (bf16[8,2,2,32,128]{4,3,2,1,0:T(8,128)(2,1)S(1)}, bf16[8,2,2,32,128]{4,3,2,1,0:T(8,128)(2,1)S(1)}, u32[]{:S(2)}, u32[]{:S(2)}) collective-permute-start(bf16[8,2,2,32,128]{4,3,2,1,0:T(8,128)(2,1)S(1)} %pad_maximum_fusion.refs_1_), channel_id=1, source_target_pairs={{0,64},{1,65},{2,66},{3,67},{4,68},{5,69},{6,70},{7,71},{8,24},{9,... | collective-permute-start | bytes 786440 | tf_op jit(solution)/shard_map/ppermute | solution.py:30
  31.4 7.4 %collective-permute-start.9 = (bf16[8,2,2,32,128]{4,3,2,1,0:T(8,128)(2,1)S(1)}, bf16[8,2,2,32,128]{4,3,2,1,0:T(8,128)(2,1)S(1)}, u32[]{:S(2)}, u32[]{:S(2)}) collective-permute-start(bf16[8,2,2,32,128]{4,3,2,1,0:T(8,128)(2,1)S(1)} %collective-permute-done.7.refs_0_), channel_id=1, source_target_pairs={{0,192},{1,193},{2,194},{3,195},{4,196},{5,197},{6,198},{7,199},{8... | collective-permute-start | bytes 786440 | tf_op jit(solution)/shard_map/ppermute | solution.py:30
  33.2 5.6 %collective-permute-start.10 = (bf16[8,2,2,32,128]{4,3,2,1,0:T(8,128)(2,1)S(1)}, bf16[8,2,2,32,128]{4,3,2,1,0:T(8,128)(2,1)S(1)}, u32[]{:S(2)}, u32[]{:S(2)}) collective-permute-start(bf16[8,2,2,32,128]{4,3,2,1,0:T(8,128)(2,1)S(1)} %collective-permute-done.8.refs_3_), channel_id=1, source_target_pairs={{0,64},{1,65},{2,66},{3,67},{4,68},{5,69},{6,70},{7,71},{8,24},{9,... | collective-permute-start | bytes 786440 | tf_op jit(solution)/shard_map/ppermute | solution.py:30
  39.8 10.5 %collective-permute-start.13 = (bf16[528,128]{1,0:T(8,128)(2,1)S(1)}, bf16[528,128]{1,0:T(8,128)(2,1)S(1)}, u32[]{:S(2)}, u32[]{:S(2)}) collective-permute-start(bf16[528,128]{1,0:T(8,128)(2,1)S(1)} %shard_map.65), channel_id=1, source_target_pairs={{0,15},{1,10},{2,9},{3,12},{4,11},{5,14},{6,13},{7,8},{8,1},{9,0},... | collective-permute-start | bytes 405512 | tf_op jit(solution)/shard_map/ppermute | solution.py:30
  46.0 5.2 %collective-permute-start.14 = (bf16[528,128]{1,0:T(8,128)(2,1)S(1)}, bf16[528,128]{1,0:T(8,128)(2,1)S(1)}, u32[]{:S(2)}, u32[]{:S(2)}) collective-permute-start(bf16[528,128]{1,0:T(8,128)(2,1)S(1)} %shard_map.63), channel_id=1, source_target_pairs={{0,1},{1,0},{2,3},{3,2},{4,5},{5,4},{6,7},{7,6},{8,15},{9,10},{10,... | collective-permute-start | bytes 405512 | tf_op jit(solution)/shard_map/ppermute | solution.py:30
  49.2 2.2 %collective-permute-start.15 = (bf16[528,128]{1,0:T(8,128)(2,1)S(1)}, bf16[528,128]{1,0:T(8,128)(2,1)S(1)}, u32[]{:S(2)}, u32[]{:S(2)}) collective-permute-start(bf16[528,128]{1,0:T(8,128)(2,1)S(1)} %shard_map.68), channel_id=1, source_target_pairs={{0,8},{1,9},{2,10},{3,11},{4,12},{5,13},{6,14},{7,15},{8,0},{9,1},... | collective-permute-start | bytes 405512 | tf_op jit(solution)/shard_map/ppermute | solution.py:30

commit v4 on v3

--- a/solution.py
+++ b/solution.py
@@ -131,7 +131,7 @@
     return jnp.broadcast_to(tile[None], (n // 8, 8, HEAD)).reshape(n, HEAD)
 
 
-def absorb(chips, which, heads, *refs):
+def absorb(chips, which, heads, message, *refs):
     start, last = chips[0][2] == 0, chips[0][2] == 3
     n_blocks = 1 + max(c[0] for c in chips)
     blocks, (both, flags, tables), refs = refs[:n_blocks], refs[n_blocks : n_blocks + 3], refs[n_blocks + 3 :]
@@ -158,21 +158,27 @@
         for kv, low_ref, fold_ref in ((0, low_keys, keys), (1, low_values, values)):
             first = block[4 * place : 4 * place + 4, kv, 0].reshape(HEAD, HEAD)
             second = block[4 * place : 4 * place + 4, kv, 1].reshape(HEAD, HEAD)
-            low = times(first, 1 - flag) + times(second, flag)
-            high = times(first, flag) + times(second, 1 - flag)
+            second_low = jnp.broadcast_to(flag[None], (HEAD // 16, 16, HEAD)).reshape(HEAD, HEAD) > 0
+            low = jnp.where(second_low, second, first)
+            high = jnp.where(second_low, first, second)
             low_ref[to, 0:HEAD] = low
             for j, q in enumerate(which):
                 kind = flags[part, 4 + 4 * q + i]
-                fold_ref[j, to, 0:HEAD] = times(low, kind)
-                fold_ref[j, to, HEAD:] = times(high, 1 - kind)
+                sees = jnp.broadcast_to(kind[None], (HEAD // 16, 16, HEAD)).reshape(HEAD, HEAD) > 0
+                fold_ref[j, to, 0:HEAD] = jnp.where(sees, low, jnp.zeros_like(low))
+                fold_ref[j, to, HEAD:] = jnp.where(sees, jnp.zeros_like(low), high)
                 if tiles[j] > n_chips and at == 0:
                     fold_ref[j, n_chips * HEAD :, 0:HEAD] = jnp.zeros((HEAD, HEAD), BF16)
                     fold_ref[j, n_chips * HEAD :, HEAD:] = high
 
     contract = (((1,), (1,)), ((), ()))
-    mine = slice(heads[0] * ROWS, heads[0] * ROWS + rows)
-    for j, q in enumerate(which):
-        kind = kinds[j]
+    units = [(j, q, h) for j, q in enumerate(which) for h in heads]
+    rows = ROWS
+    n_heads = len(heads)
+    norms = [[] for _ in range(2 * len(which))]
+
+    def score(j, q, h):
+        mine = slice(h * ROWS, (h + 1) * ROWS)
         free = lax.dot_general(both[q, mine, HEAD:], low_keys[...], contract, preferred_element_type=F32)
         free = [free[:, i * HEAD : (i + 1) * HEAD] for i in range(n_chips)]
         fold = lax.dot_general(
@@ -184,14 +190,26 @@
             edge = spread_rows(tables[0, 8], rows) <= row.astype(F32)
             tile[0] = jnp.where(edge, tile[0], -FAR)
             tile[-1] = jnp.where(edge, tile[-1], -FAR)
+        return free, tile
+
+    def finish(j, q, h, free, tile):
+        kind = kinds[j]
+        mine = slice(h * ROWS, (h + 1) * ROWS)
+        short = [t.astype(BF16) for t in tile]
+        pens = [jnp.concatenate([(1.0 - k) * FAR, (1.0 - k) * FAR], axis=0).astype(BF16) for k in kind]
+        flips = [jnp.concatenate([k * FAR, k * FAR], axis=0).astype(BF16) for k in kind]
+
+        def lower(t, pen):
+            return (t.reshape(rows // 16, 16, HEAD) - pen[None]).reshape(rows, HEAD)
+
         bests = (
-            [t + spread_rows((k - 1.0) * FAR, rows) for t, k in zip(tile, kind)],
-            [t - spread_rows(k * FAR, rows) for t, k in zip(tile, kind)] + free,
+            [lower(t, p) for t, p in zip(short, pens)],
+            [lower(t, p) for t, p in zip(short, flips)] + [t.astype(BF16) for t in free],
         )
         bases, factors = [], []
         for k in range(2):
             at = slice(k * 2 * ROWS + mine.start, k * 2 * ROWS + mine.stop)
-            top = jnp.max(functools.reduce(jnp.maximum, bests[k]), axis=1, keepdims=True) * SCALE
+            top = jnp.max(functools.reduce(jnp.maximum, bests[k]).astype(F32), axis=1, keepdims=True) * SCALE
             if start:
                 top = jnp.broadcast_to(jnp.maximum(top, NEG), (rows, HEAD))
             else:
@@ -206,7 +224,7 @@
             base = jnp.where(spread_rows(k, rows) > 0, bases[0], bases[1])
             w = jnp.exp2(t * SCALE - base)
             low_sum = low_sum + w * spread_rows(k, rows)
-            high_sum = high_sum + w * spread_rows(1.0 - k, rows)
+            high_sum = high_sum + w
             weights.append(w.astype(BF16))
         fold = jnp.dot(
             jnp.concatenate(weights, axis=1), values[j, : tiles[j] * HEAD, :], preferred_element_type=F32
@@ -214,28 +232,36 @@
         weights = [jnp.exp2(t * SCALE - bases[1]).astype(BF16) for t in free]
         free = jnp.dot(jnp.concatenate(weights, axis=1), low_values[...], preferred_element_type=F32)
         parts = (fold[:, :HEAD], fold[:, HEAD:] + free[:, :HEAD])
-        totals = (low_sum, high_sum + free[:, HEAD:])
-        norms = []
+        totals = (low_sum, high_sum - low_sum + free[:, HEAD:])
         for k in range(2):
             at = slice(k * 2 * ROWS + mine.start, k * 2 * ROWS + mine.stop)
-            to = slice(k * rows, (k + 1) * rows)
+            place = (k * n_heads + heads.index(h)) * ROWS
+            to = slice(place, place + ROWS)
             value, total = parts[k], totals[k]
             if not start:
                 value = olds[j][0][at, :] * factors[k] + value
                 total = olds[j][2][at, :] * factors[k] + total
             if last:
                 total = jnp.broadcast_to(jnp.sum(total, axis=1, keepdims=True), (rows, HEAD))
-            if len(outs) == 1:
+            if message:
                 some = total > 0
                 total = jnp.where(some, total, 1.0)
-                outs[0][to, :] = (value / total).astype(BF16)
-                norms.append(jnp.where(some, bases[k] + jnp.log2(total), NEG))
+                outs[j][to, :] = (value / total).astype(BF16)
+                norms[2 * j + k].append(jnp.where(some, bases[k] + jnp.log2(total), NEG))
             else:
                 outs[3 * j][to, :] = value
                 outs[3 * j + 1][to, :] = bases[k]
                 outs[3 * j + 2][to, :] = total
-        if len(outs) == 1:
-            pack(outs[0], 2 * rows, jnp.concatenate(norms, axis=0))
+
+    ahead = score(*units[0])
+    for n, unit in enumerate(units):
+        now = ahead
+        if n + 1 < len(units):
+            ahead = score(*units[n + 1])
+        finish(*unit, *now)
+    if message:
+        for j in range(len(which)):
+            pack(outs[j], 2 * n_heads * ROWS, jnp.concatenate(norms[2 * j] + norms[2 * j + 1], axis=0))
 
 
 def merge(value, top, total, other, norm):
@@ -297,10 +323,10 @@
 def attend(chips, which, blocks, ready, state, heads=(0, 1), message=False):
     n, n_chips = len(which), len(chips)
     rows = 2 * len(heads) * ROWS
-    outs = [shape(rows + 16, HEAD, dtype=BF16)] if message else [shape(rows, HEAD)] * (3 * n)
+    outs = [shape(rows + 16, HEAD, dtype=BF16)] * n if message else [shape(rows, HEAD)] * (3 * n)
     wide = n_chips + 1 if chips[0][2] == 0 else n_chips
     return call(
-        functools.partial(absorb, chips, which, heads),
+        functools.partial(absorb, chips, which, heads, message),
         outs,
         *blocks,
         *ready,
@@ -350,11 +376,10 @@
     state = attend(chips, (0, 1), near + far, ready, state)
 
     chips = [(i // 2, i % 2, 3, i) for i in range(4)]
-    (message,) = attend(chips, (1,), across, ready, state[3:], (1,), True)
-    cross = send(message, lambda y, x, c, z: (y, x, 1 - c, partner(1 - c, z)))
-    (message,) = attend(chips, (0,), across, ready, state[:3], (1,), True)
-    message, *state = lax.optimization_barrier((message, *state))
-    side = send(message, lambda y, x, c, z: (y, x, c, partner(c, z)))
+    messages = attend(chips, (1, 0), across, ready, state[3:] + state[:3], (1,), True)
+    cross, side, *state = lax.optimization_barrier((*messages, *state))
+    cross = send(cross, lambda y, x, c, z: (y, x, 1 - c, partner(1 - c, z)))
+    side = send(side, lambda y, x, c, z: (y, x, c, partner(c, z)))
     (message,) = attend(chips, (1,), across, ready, state[3:], (0,), True)
     mate = send(message, swap_cores)
     state = attend(chips, (0,), across, ready, state[:3], (0,))

time: 52.7 us -> 52.8 us (level)
  Pallas kernels: 12.9 us -> 11.8 us
  waiting for transfers between devices: 6.58 us -> 7.53 us
    pallas_call x11 -> x10, Pallas kernels: 12.9 us -> 11.8 us  [call(): pl.pallas_call(body, out_shape=outs, in_specs=[pl.BlockSpec(memory_space=...]
    ppermute x16, waiting for transfers between devices: 6.58 us -> 7.53 us  [send(): return lax.ppermute(value, AXES, pairs)]
  transfers between devices with their start and end apart: 16 -> 16, of which waited for: 7 -> 8; matrix products, arithmetic and copies ran while one was open for 2% -> 2% of each run, Pallas kernels for 21% -> 17%
where the time goes in v4:
time: 52.8 us; the launch traced here: 52.5 us
  starting transfers between devices  29.8 us (56%)
  Pallas kernels  11.8 us (22%)
  waiting for transfers between devices  7.53 us (14%)
  local copies, waits for them, and re-layouts  1.63 us (3%)
  other arithmetic  0.89 us (2%)
  between operations  0.8 us (2%)
    ppermute x16, starting transfers between devices, send(): return lax.ppermute(value, AXES, pairs)  29.8 us
    pallas_call x10, Pallas kernels, call(): pl.pallas_call(body, out_shape=outs, in_specs=[pl.BlockSpec(memory_space=...  11.8 us
    ppermute x16, waiting for transfers between devices, send(): return lax.ppermute(value, AXES, pairs)  7.53 us
  transfers between devices with their start and end apart: 16, of which 8 were waited for; matrix products, arithmetic and copies ran while one was open for 2% of the time, Pallas kernels for 17%

profile of v4, /device:TPU:1, one launch (start us, length us, event | category | flops | bytes accessed | tf_op | source)
XLA Modules:
  0.0 52.5 jit_solution(13192467488354325723)
XLA Ops:
  0.6 0.7 %pad_maximum_fusion.3 = bf16[2,64,128]{2,1,0:T(8,128)(2,1)S(1)} fusion(bf16[1,64,128]{2,1,0:T(8,128)(2,1)} %param.6, bf16[1,64,128]{2,1,0:T(8,128)(2,1)} %param.5), kind=kLoop, calls=%fused_computation.3 | loop fusion | flops 16384 | bytes 65536 | tf_op jit(solution)/shard_map/stack | solution.py:358
  1.4 7.7 %collective-permute-start.2 = (bf16[1,2,2,32,128]{4,3,2,1,0:T(8,128)(2,1)S(1)}, bf16[1,2,2,32,128]{4,3,2,1,0:T(8,128)(2,1)S(1)}, u32[]{:S(2)}, u32[]{:S(2)}) collective-permute-start(bf16[1,2,2,32,128]{4,3,2,1,0:T(8,128)(2,1)S(1)} %bitcast.3), channel_id=1, source_target_pairs={{0,4},{1,5},{2,6},{3,7},{4,0},{5,1},{6,2},{7,3},{8,12},{9,13},{10,... | collective-permute-start | bytes 98312 | tf_op jit(solution)/shard_map/ppermute | solution.py:30
  9.1 0.0 collective-permute-start.1
  9.1 1.2 %collective-permute-start = (bf16[1,2,2,32,128]{4,3,2,1,0:T(8,128)(2,1)S(1)}, bf16[1,2,2,32,128]{4,3,2,1,0:T(8,128)(2,1)S(1)}, u32[]{:S(2)}, u32[]{:S(2)}) collective-permute-start(bf16[1,2,2,32,128]{4,3,2,1,0:T(8,128)(2,1)S(1)} %bitcast.5), channel_id=1, source_target_pairs={{0,2},{1,3},{2,0},{3,1},{4,6},{5,7},{6,4},{7,5},{8,10},{9,11},{10,... | collective-permute-start | bytes 98312 | tf_op jit(solution)/shard_map/ppermute | solution.py:30
  10.3 0.0 copy-start
  10.3 0.1 pad_add_fusion.place
  10.4 0.6 %copy-done = s32[64]{0:T(128)S(1)} copy-done((s32[64]{0:T(128)S(1)}, s32[64]{0:T(128)}, u32[]{:S(2)}) %copy-start) | copy-done | bytes 280
  11.0 0.7 %shard_map.59 = (bf16[4,14,16,128]{3,2,1,0:T(8,128)(2,1)S(1)}, f32[4,11,8,128]{3,2,1,0:T(8,128)S(1)}) custom-call(s32[64]{0:T(128)S(1)} %copy-done, s32[2]{0:T(128)S(1)} %pad_add_fusion.place), custom_call_target="tpu_custom_call" | custom-call | flops 1024 | bytes 1024 | tf_op jit(solution)/shard_map/pallas_call | solution.py:307
  11.7 1.1 %collective-permute-done = bf16[1,2,2,32,128]{4,3,2,1,0:T(8,128)(2,1)S(1)} collective-permute-done((bf16[1,2,2,32,128]{4,3,2,1,0:T(8,128)(2,1)S(1)}, bf16[1,2,2,32,128]{4,3,2,1,0:T(8,128)(2,1)S(1)}, u32[]{:S(2)}, u32[]{:S(2)}) %collective-permute-start) | collective-permute-done | bytes 32800 | tf_op jit(solution)/shard_map/ppermute | solution.py:30
  12.8 0.0 collective-permute-done.2
  12.8 1.2 %collective-permute-done.1 = bf16[1,2,2,32,128]{4,3,2,1,0:T(8,128)(2,1)S(1)} collective-permute-done((bf16[1,2,2,32,128]{4,3,2,1,0:T(8,128)(2,1)S(1)}, bf16[1,2,2,32,128]{4,3,2,1,0:T(8,128)(2,1)S(1)}, u32[]{:S(2)}, u32[]{:S(2)}) %collective-permute-start.1) | collective-permute-done | bytes 32800 | tf_op jit(solution)/shard_map/ppermute | solution.py:30
  14.0 3.0 %collective-permute-start.5 = (bf16[4,2,2,32,128]{4,3,2,1,0:T(8,128)(2,1)S(1)}, bf16[4,2,2,32,128]{4,3,2,1,0:T(8,128)(2,1)S(1)}, u32[]{:S(2)}, u32[]{:S(2)}) collective-permute-start(bf16[4,2,2,32,128]{4,3,2,1,0:T(8,128)(2,1)S(1)} %pad_maximum_fusion.2), channel_id=1, source_target_pairs={{0,32},{1,33},{2,34},{3,35},{4,36},{5,37},{6,38},{7,39},{8,136},{9... | collective-permute-start | bytes 393224 | tf_op jit(solution)/shard_map/ppermute | solution.py:30
  17.0 0.8 %collective-permute-start.4 = (bf16[4,2,2,32,128]{4,3,2,1,0:T(8,128)(2,1)S(1)}, bf16[4,2,2,32,128]{4,3,2,1,0:T(8,128)(2,1)S(1)}, u32[]{:S(2)}, u32[]{:S(2)}) collective-permute-start(bf16[4,2,2,32,128]{4,3,2,1,0:T(8,128)(2,1)S(1)} %pad_maximum_fusion.2), channel_id=1, source_target_pairs={{0,48},{1,49},{2,50},{3,51},{4,52},{5,53},{6,54},{7,55},{8,200},{9... | collective-permute-start | bytes 393224 | tf_op jit(solution)/shard_map/ppermute | solution.py:30
  17.8 0.0 collective-permute-start.3
  17.8 1.0 %constant_dynamic-slice_fusion.1 = (bf16[512,128]{1,0:T(8,128)(2,1)S(1)}, bf16[512,128]{1,0:T(8,128)(2,1)S(1)}) fusion(bf16[512,1024]{1,0:T(8,128)(2,1)} %param.4, s32[]{:T(128)S(6)} %select_n.24, s32[]{:T(128)S(6)} %select_n.29), kind=kLoop, calls=%fused_computation.11 | loop fusion | bytes 524296 | tf_op jit(solution)/shard_map/dynamic_slice | solution.py:362
  18.8 3.0 %collective-permute-start.6 = (bf16[512,256]{1,0:T(8,128)(2,1)S(1)}, bf16[512,256]{1,0:T(8,128)(2,1)S(1)}, u32[]{:S(2)}, u32[]{:S(2)}) collective-permute-start(bf16[512,256]{1,0:T(8,128)(2,1)S(1)} %pad_maximum_fusion.1.own), channel_id=1, source_target_pairs={{0,8},{1,9},{2,10},{3,11},{4,12},{5,13},{6,14},{7,15},{8,0},{9,1},... | collective-permute-start | bytes 786440 | tf_op jit(solution)/shard_map/ppermute | solution.py:30
  21.9 0.0 collective-permute-done.3
  21.9 0.0 collective-permute-done.5
  21.9 0.4 collective-permute-done.4
  22.4 0.7 %collective-permute-done.6.other = bf16[512,256]{1,0:T(8,128)(2,1)S(1)} collective-permute-done((bf16[512,256]{1,0:T(8,128)(2,1)S(1)}, bf16[512,256]{1,0:T(8,128)(2,1)S(1)}, u32[]{:S(2)}, u32[]{:S(2)}) %collective-permute-start.6) | collective-permute-done | bytes 262176 | tf_op jit(solution)/shard_map/ppermute | solution.py:30
  23.0 0.1 shard_map.60.refs_2_.refs_4_
  23.1 1.8 %collective-permute-start.7 = (bf16[8,2,2,32,128]{4,3,2,1,0:T(8,128)(2,1)S(1)}, bf16[8,2,2,32,128]{4,3,2,1,0:T(8,128)(2,1)S(1)}, u32[]{:S(2)}, u32[]{:S(2)}) collective-permute-start(bf16[8,2,2,32,128]{4,3,2,1,0:T(8,128)(2,1)S(1)} %constant_dynamic-update-slice_fusion.refs_0_), channel_id=1, source_target_pairs={{0,64},{1,65},{2,66},{3,67},{4,68},{5,69},{6,70},{7,71},{8,24},{9,... | collective-permute-start | bytes 786440 | tf_op jit(solution)/shard_map/ppermute | solution.py:30
  25.0 1.8 %collective-permute-start.8 = (bf16[8,2,2,32,128]{4,3,2,1,0:T(8,128)(2,1)S(1)}, bf16[8,2,2,32,128]{4,3,2,1,0:T(8,128)(2,1)S(1)}, u32[]{:S(2)}, u32[]{:S(2)}) collective-permute-start(bf16[8,2,2,32,128]{4,3,2,1,0:T(8,128)(2,1)S(1)} %pad_maximum_fusion.refs_1_), channel_id=1, source_target_pairs={{0,192},{1,193},{2,194},{3,195},{4,196},{5,197},{6,198},{7,199},{8... | collective-permute-start | bytes 786440 | tf_op jit(solution)/shard_map/ppermute | solution.py:30
  26.8 0.9 %collective-permute-start.12 = (bf16[8,2,2,32,128]{4,3,2,1,0:T(8,128)(2,1)S(1)}, bf16[8,2,2,32,128]{4,3,2,1,0:T(8,128)(2,1)S(1)}, u32[]{:S(2)}, u32[]{:S(2)}) collective-permute-start(bf16[8,2,2,32,128]{4,3,2,1,0:T(8,128)(2,1)S(1)} %constant_dynamic-update-slice_fusion.refs_0_), channel_id=1, source_target_pairs={{0,192},{1,193},{2,194},{3,195},{4,196},{5,197},{6,198},{7,199},{8... | collective-permute-start | bytes 786440 | tf_op jit(solution)/shard_map/ppermute | solution.py:30
  27.6 0.0 collective-permute-start.11
  27.7 2.1 %shard_map.61 = (f32[1024,128]{1,0:T(8,128)S(1)}, f32[1024,128]{1,0:T(8,128)S(1)}, f32[1024,128]{1,0:T(8,128)S(1)}, f32[1024,128]{1,0:T(8,128)S(1)}, f32[1024,128]{1,0:T(8,128)S(1)}, /*index=5*/f32[1024,128]{1,0:T(8,128)S(1)}) custom-call(bf16[8,2,2,32,128]{4,3,2,1,0:T(8,128)(2,1)S(1)} %constant_dynamic-update-slice_fusion.refs_0_, ...), custom_call_target="tpu_custom_call" | custom-call | flops 1024 | bytes 1024 | tf_op jit(solution)/shard_map/pallas_call | solution.py:307
  29.7 0.0 collective-permute-done.7.refs_0_
  29.8 1.6 %collective-permute-done.8.refs_3_ = bf16[8,2,2,32,128]{4,3,2,1,0:T(8,128)(2,1)S(1)} collective-permute-done((bf16[8,2,2,32,128]{4,3,2,1,0:T(8,128)(2,1)S(1)}, bf16[8,2,2,32,128]{4,3,2,1,0:T(8,128)(2,1)S(1)}, u32[]{:S(2)}, u32[]{:S(2)}) %collective-permute-start.8) | collective-permute-done | bytes 262176 | tf_op jit(solution)/shard_map/ppermute | solution.py:30
  31.4 1.8 %collective-permute-start.9 = (bf16[8,2,2,32,128]{4,3,2,1,0:T(8,128)(2,1)S(1)}, bf16[8,2,2,32,128]{4,3,2,1,0:T(8,128)(2,1)S(1)}, u32[]{:S(2)}, u32[]{:S(2)}) collective-permute-start(bf16[8,2,2,32,128]{4,3,2,1,0:T(8,128)(2,1)S(1)} %collective-permute-done.7.refs_0_), channel_id=1, source_target_pairs={{0,192},{1,193},{2,194},{3,195},{4,196},{5,197},{6,198},{7,199},{8... | collective-permute-start | bytes 786440 | tf_op jit(solution)/shard_map/ppermute | solution.py:30
  33.2 0.0 collective-permute-start.10
  33.2 1.3 %collective-permute-done.12.refs_2_ = bf16[8,2,2,32,128]{4,3,2,1,0:T(8,128)(2,1)S(1)} collective-permute-done((bf16[8,2,2,32,128]{4,3,2,1,0:T(8,128)(2,1)S(1)}, bf16[8,2,2,32,128]{4,3,2,1,0:T(8,128)(2,1)S(1)}, u32[]{:S(2)}, u32[]{:S(2)}) %collective-permute-start.12) | collective-permute-done | bytes 262176 | tf_op jit(solution)/shard_map/ppermute | solution.py:30
  34.5 0.0 collective-permute-done.11.refs_1_
  34.5 4.0 %shard_map.62 = (f32[1024,128]{1,0:T(8,128)S(1)}, f32[1024,128]{1,0:T(8,128)S(1)}, f32[1024,128]{1,0:T(8,128)S(1)}, f32[1024,128]{1,0:T(8,128)S(1)}, f32[1024,128]{1,0:T(8,128)S(1)}, /*index=5*/f32[1024,128]{1,0:T(8,128)S(1)}) custom-call(bf16[8,2,2,32,128]{4,3,2,1,0:T(8,128)(2,1)S(1)} %collect, ...), custom_call_target="tpu_custom_call", output_to_operand_aliasing={{0}: (7, {}), {1}: (8, {}), {2}: (9, {}), {3}: (10, {}), {4... | custom-call | flops 1024 | bytes 1024 | tf_op jit(solution)/shard_map/pallas_call | solution.py:307
  38.6 0.0 collective-permute-done.9.refs_0_
  38.6 0.0 collective-permute-done.10.refs_1_
  38.6 1.5 %shard_map.63 = (bf16[528,128]{1,0:T(8,128)(2,1)S(1)}, bf16[528,128]{1,0:T(8,128)(2,1)S(1)}) custom-call(bf16[8,2,2,32,128]{4,3,2,1,0:T(8,128)(2,1)S(1)} %collective-permute-done.9.refs_0_, bf16[8,2,2,32,128]{4,3,2,1,0:T(8,128)(2,1)S(1)} %collective-permute-done.10.refs_1_, bf16[2,512,256]{2,1,0:T(8,128)(2,1)S(1)} %shard_map.60.refs_2_.refs_4_, ...), custom_call_target="tpu_custom_call" | custom-call | flops 1024 | bytes 1024 | tf_op jit(solution)/shard_map/pallas_call | solution.py:307
  40.0 5.5 %collective-permute-start.13 = (bf16[528,128]{1,0:T(8,128)(2,1)S(1)}, bf16[528,128]{1,0:T(8,128)(2,1)S(1)}, u32[]{:S(2)}, u32[]{:S(2)}) collective-permute-start(bf16[528,128]{1,0:T(8,128)(2,1)S(1)} %get-tuple-element.87), channel_id=1, source_target_pairs={{0,15},{1,10},{2,9},{3,12},{4,11},{5,14},{6,13},{7,8},{8,1},{9,0},... | collective-permute-start | bytes 405512 | tf_op jit(solution)/shard_map/ppermute | solution.py:30
  45.5 2.2 %collective-permute-start.14 = (bf16[528,128]{1,0:T(8,128)(2,1)S(1)}, bf16[528,128]{1,0:T(8,128)(2,1)S(1)}, u32[]{:S(2)}, u32[]{:S(2)}) collective-permute-start(bf16[528,128]{1,0:T(8,128)(2,1)S(1)} %get-tuple-element.91), channel_id=1, source_target_pairs={{0,1},{1,0},{2,3},{3,2},{4,5},{5,4},{6,7},{7,6},{8,15},{9,10},{10,... | collective-permute-start | bytes 405512 | tf_op jit(solution)/shard_map/ppermute | solution.py:30
  47.7 0.9 %shard_map.67 = bf16[528,128]{1,0:T(8,128)(2,1)S(1)} custom-call(bf16[8,2,2,32,128]{4,3,2,1,0:T(8,128)(2,1)S(1)} %collective-permute-done.9.refs_0_, bf16[8,2,2,32,128]{4,3,2,1,0:T(8,128)(2,1)S(1)} %collective-permute-done.10.refs_1_, bf16[2,512,256]{2,1,0:T(8,128)(2,1)S(1)} %shard_map.60.refs_2_.refs_4_, ...), custom_call_target="tpu_custom_call" | custom-call | flops 1024 | bytes 1024 | tf_op jit(solution)/shard_map/pallas_call | solution.py:307
  48.6 0.1 collective-permute-start.15
  48.7 0.9 %shard_map.64 = (f32[512,128]{1,0:T(8,128)S(1)}, f32[512,128]{1,0:T(8,128)S(1)}, f32[512,128]{1,0:T(8,128)S(1)}) custom-call(bf16[8,2,2,32,128]{4,3,2,1,0:T(8,128)(2,1)S(1)} %collective-permute-done.9.refs_0_, bf16[8,2,2,32,128]{4,3,2,1,0:T(8,128)(2,1)S(1)} %collective-permute-done.10.refs_1_, bf16[2,512,256]{2,1,0:T(8,128)(2,1)S(1)} %shard_map.60.refs_2_.refs_4_, ...), custom_call_target="tpu_custom_call" | custom-call | flops 1024 | bytes 1024 | tf_op jit(solution)/shard_map/pallas_call | solution.py:307
  49.6 0.6 %collective-permute-done.13.received = bf16[528,128]{1,0:T(8,128)(2,1)S(1)} collective-permute-done((bf16[528,128]{1,0:T(8,128)(2,1)S(1)}, bf16[528,128]{1,0:T(8,128)(2,1)S(1)}, u32[]{:S(2)}, u32[]{:S(2)}) %collective-permute-start.13) | collective-permute-done | bytes 135200 | tf_op jit(solution)/shard_map/ppermute | solution.py:30
  50.3 0.3 shard_map.65
  50.5 0.6 %collective-permute-done.14.received = bf16[528,128]{1,0:T(8,128)(2,1)S(1)} collective-permute-done((bf16[528,128]{1,0:T(8,128)(2,1)S(1)}, bf16[528,128]{1,0:T(8,128)(2,1)S(1)}, u32[]{:S(2)}, u32[]{:S(2)}) %collective-permute-start.14) | collective-permute-done | bytes 135200 | tf_op jit(solution)/shard_map/ppermute | solution.py:30
  51.1 0.3 shard_map.66
  51.4 0.0 collective-permute-done.15.received
  51.4 1.0 %shard_map.68 = (bf16[512,128]{1,0:T(8,128)(2,1)}, f32[1,512]{1,0:T(1,128)}) custom-call(f32[4,11,8,128]{3,2,1,0:T(8,128)S(1)} %get-tuple-element.54.refs_4_.refs_6_.tables, f32[512,128]{1,0:T(8,128)S(1)} %get-tuple-element.92.mine, f32[512,128]{1,0:T(8,128)S(1)} %get-tuple-element.93.mine_tops, f32[512,128]{1,0:T(8,128)S(1)} %get-tuple-element.94.mine_sums, ...), custom_call_target="tpu_custom_call" | custom-call | flops 1024 | bytes 1024 | tf_op jit(solution)/shard_map/pallas_call | solution.py:307
  (8 shorter events, 0.1 us)
Async XLA Ops:
  1.4 11.4 %collective-permute-start.2 = (bf16[1,2,2,32,128]{4,3,2,1,0:T(8,128)(2,1)S(1)}, bf16[1,2,2,32,128]{4,3,2,1,0:T(8,128)(2,1)S(1)}, u32[]{:S(2)}, u32[]{:S(2)}) collective-permute-start(bf16[1,2,2,32,128]{4,3,2,1,0:T(8,128)(2,1)S(1)} %bitcast.3), channel_id=1, source_target_pairs={{0,4},{1,5},{2,6},{3,7},{4,0},{5,1},{6,2},{7,3},{8,12},{9,13},{10,... | collective-permute-start | bytes 98312 | tf_op jit(solution)/shard_map/ppermute | solution.py:30
  9.1 4.9 %collective-permute-start.1 = (bf16[1,2,2,32,128]{4,3,2,1,0:T(8,128)(2,1)S(1)}, bf16[1,2,2,32,128]{4,3,2,1,0:T(8,128)(2,1)S(1)}, u32[]{:S(2)}, u32[]{:S(2)}) collective-permute-start(bf16[1,2,2,32,128]{4,3,2,1,0:T(8,128)(2,1)S(1)} %bitcast.4), channel_id=1, source_target_pairs={{0,6},{1,7},{2,4},{3,5},{4,2},{5,3},{6,0},{7,1},{8,14},{9,15},{10,... | collective-permute-start | bytes 98312 | tf_op jit(solution)/shard_map/ppermute | solution.py:30
  9.1 3.7 %collective-permute-start = (bf16[1,2,2,32,128]{4,3,2,1,0:T(8,128)(2,1)S(1)}, bf16[1,2,2,32,128]{4,3,2,1,0:T(8,128)(2,1)S(1)}, u32[]{:S(2)}, u32[]{:S(2)}) collective-permute-start(bf16[1,2,2,32,128]{4,3,2,1,0:T(8,128)(2,1)S(1)} %bitcast.5), channel_id=1, source_target_pairs={{0,2},{1,3},{2,0},{3,1},{4,6},{5,7},{6,4},{7,5},{8,10},{9,11},{10,... | collective-permute-start | bytes 98312 | tf_op jit(solution)/shard_map/ppermute | solution.py:30
  10.3 0.7 %copy-start = (s32[64]{0:T(128)S(1)}, s32[64]{0:T(128)}, u32[]{:S(2)}) copy-start(s32[64]{0:T(128)} %span.1) | copy-start | bytes 772
  14.0 7.9 %collective-permute-start.5 = (bf16[4,2,2,32,128]{4,3,2,1,0:T(8,128)(2,1)S(1)}, bf16[4,2,2,32,128]{4,3,2,1,0:T(8,128)(2,1)S(1)}, u32[]{:S(2)}, u32[]{:S(2)}) collective-permute-start(bf16[4,2,2,32,128]{4,3,2,1,0:T(8,128)(2,1)S(1)} %pad_maximum_fusion.2), channel_id=1, source_target_pairs={{0,32},{1,33},{2,34},{3,35},{4,36},{5,37},{6,38},{7,39},{8,136},{9... | collective-permute-start | bytes 393224 | tf_op jit(solution)/shard_map/ppermute | solution.py:30
  17.0 5.3 %collective-permute-start.4 = (bf16[4,2,2,32,128]{4,3,2,1,0:T(8,128)(2,1)S(1)}, bf16[4,2,2,32,128]{4,3,2,1,0:T(8,128)(2,1)S(1)}, u32[]{:S(2)}, u32[]{:S(2)}) collective-permute-start(bf16[4,2,2,32,128]{4,3,2,1,0:T(8,128)(2,1)S(1)} %pad_maximum_fusion.2), channel_id=1, source_target_pairs={{0,48},{1,49},{2,50},{3,51},{4,52},{5,53},{6,54},{7,55},{8,200},{9... | collective-permute-start | bytes 393224 | tf_op jit(solution)/shard_map/ppermute | solution.py:30
  17.8 4.1 %collective-permute-start.3 = (bf16[4,2,2,32,128]{4,3,2,1,0:T(8,128)(2,1)S(1)}, bf16[4,2,2,32,128]{4,3,2,1,0:T(8,128)(2,1)S(1)}, u32[]{:S(2)}, u32[]{:S(2)}) collective-permute-start(bf16[4,2,2,32,128]{4,3,2,1,0:T(8,128)(2,1)S(1)} %pad_maximum_fusion.2), channel_id=1, source_target_pairs={{0,16},{1,17},{2,18},{3,19},{4,20},{5,21},{6,22},{7,23},{8,72},{9,... | collective-permute-start | bytes 393224 | tf_op jit(solution)/shard_map/ppermute | solution.py:30
  18.8 4.2 %collective-permute-start.6 = (bf16[512,256]{1,0:T(8,128)(2,1)S(1)}, bf16[512,256]{1,0:T(8,128)(2,1)S(1)}, u32[]{:S(2)}, u32[]{:S(2)}) collective-permute-start(bf16[512,256]{1,0:T(8,128)(2,1)S(1)} %pad_maximum_fusion.1.own), channel_id=1, source_target_pairs={{0,8},{1,9},{2,10},{3,11},{4,12},{5,13},{6,14},{7,15},{8,0},{9,1},... | collective-permute-start | bytes 786440 | tf_op jit(solution)/shard_map/ppermute | solution.py:30
  23.1 6.6 %collective-permute-start.7 = (bf16[8,2,2,32,128]{4,3,2,1,0:T(8,128)(2,1)S(1)}, bf16[8,2,2,32,128]{4,3,2,1,0:T(8,128)(2,1)S(1)}, u32[]{:S(2)}, u32[]{:S(2)}) collective-permute-start(bf16[8,2,2,32,128]{4,3,2,1,0:T(8,128)(2,1)S(1)} %constant_dynamic-update-slice_fusion.refs_0_), channel_id=1, source_target_pairs={{0,64},{1,65},{2,66},{3,67},{4,68},{5,69},{6,70},{7,71},{8,24},{9,... | collective-permute-start | bytes 786440 | tf_op jit(solution)/shard_map/ppermute | solution.py:30
  25.0 6.4 %collective-permute-start.8 = (bf16[8,2,2,32,128]{4,3,2,1,0:T(8,128)(2,1)S(1)}, bf16[8,2,2,32,128]{4,3,2,1,0:T(8,128)(2,1)S(1)}, u32[]{:S(2)}, u32[]{:S(2)}) collective-permute-start(bf16[8,2,2,32,128]{4,3,2,1,0:T(8,128)(2,1)S(1)} %pad_maximum_fusion.refs_1_), channel_id=1, source_target_pairs={{0,192},{1,193},{2,194},{3,195},{4,196},{5,197},{6,198},{7,199},{8... | collective-permute-start | bytes 786440 | tf_op jit(solution)/shard_map/ppermute | solution.py:30
  26.8 7.7 %collective-permute-start.12 = (bf16[8,2,2,32,128]{4,3,2,1,0:T(8,128)(2,1)S(1)}, bf16[8,2,2,32,128]{4,3,2,1,0:T(8,128)(2,1)S(1)}, u32[]{:S(2)}, u32[]{:S(2)}) collective-permute-start(bf16[8,2,2,32,128]{4,3,2,1,0:T(8,128)(2,1)S(1)} %constant_dynamic-update-slice_fusion.refs_0_), channel_id=1, source_target_pairs={{0,192},{1,193},{2,194},{3,195},{4,196},{5,197},{6,198},{7,199},{8... | collective-permute-start | bytes 786440 | tf_op jit(solution)/shard_map/ppermute | solution.py:30
  27.6 6.9 %collective-permute-start.11 = (bf16[8,2,2,32,128]{4,3,2,1,0:T(8,128)(2,1)S(1)}, bf16[8,2,2,32,128]{4,3,2,1,0:T(8,128)(2,1)S(1)}, u32[]{:S(2)}, u32[]{:S(2)}) collective-permute-start(bf16[8,2,2,32,128]{4,3,2,1,0:T(8,128)(2,1)S(1)} %pad_maximum_fusion.refs_1_), channel_id=1, source_target_pairs={{0,64},{1,65},{2,66},{3,67},{4,68},{5,69},{6,70},{7,71},{8,24},{9,... | collective-permute-start | bytes 786440 | tf_op jit(solution)/shard_map/ppermute | solution.py:30
  31.4 7.2 %collective-permute-start.9 = (bf16[8,2,2,32,128]{4,3,2,1,0:T(8,128)(2,1)S(1)}, bf16[8,2,2,32,128]{4,3,2,1,0:T(8,128)(2,1)S(1)}, u32[]{:S(2)}, u32[]{:S(2)}) collective-permute-start(bf16[8,2,2,32,128]{4,3,2,1,0:T(8,128)(2,1)S(1)} %collective-permute-done.7.refs_0_), channel_id=1, source_target_pairs={{0,192},{1,193},{2,194},{3,195},{4,196},{5,197},{6,198},{7,199},{8... | collective-permute-start | bytes 786440 | tf_op jit(solution)/shard_map/ppermute | solution.py:30
  33.2 5.4 %collective-permute-start.10 = (bf16[8,2,2,32,128]{4,3,2,1,0:T(8,128)(2,1)S(1)}, bf16[8,2,2,32,128]{4,3,2,1,0:T(8,128)(2,1)S(1)}, u32[]{:S(2)}, u32[]{:S(2)}) collective-permute-start(bf16[8,2,2,32,128]{4,3,2,1,0:T(8,128)(2,1)S(1)} %collective-permute-done.8.refs_3_), channel_id=1, source_target_pairs={{0,64},{1,65},{2,66},{3,67},{4,68},{5,69},{6,70},{7,71},{8,24},{9,... | collective-permute-start | bytes 786440 | tf_op jit(solution)/shard_map/ppermute | solution.py:30
  40.0 10.2 %collective-permute-start.13 = (bf16[528,128]{1,0:T(8,128)(2,1)S(1)}, bf16[528,128]{1,0:T(8,128)(2,1)S(1)}, u32[]{:S(2)}, u32[]{:S(2)}) collective-permute-start(bf16[528,128]{1,0:T(8,128)(2,1)S(1)} %get-tuple-element.87), channel_id=1, source_target_pairs={{0,15},{1,10},{2,9},{3,12},{4,11},{5,14},{6,13},{7,8},{8,1},{9,0},... | collective-permute-start | bytes 405512 | tf_op jit(solution)/shard_map/ppermute | solution.py:30
  45.5 5.6 %collective-permute-start.14 = (bf16[528,128]{1,0:T(8,128)(2,1)S(1)}, bf16[528,128]{1,0:T(8,128)(2,1)S(1)}, u32[]{:S(2)}, u32[]{:S(2)}) collective-permute-start(bf16[528,128]{1,0:T(8,128)(2,1)S(1)} %get-tuple-element.91), channel_id=1, source_target_pairs={{0,1},{1,0},{2,3},{3,2},{4,5},{5,4},{6,7},{7,6},{8,15},{9,10},{10,... | collective-permute-start | bytes 405512 | tf_op jit(solution)/shard_map/ppermute | solution.py:30
  48.6 2.8 %collective-permute-start.15 = (bf16[528,128]{1,0:T(8,128)(2,1)S(1)}, bf16[528,128]{1,0:T(8,128)(2,1)S(1)}, u32[]{:S(2)}, u32[]{:S(2)}) collective-permute-start(bf16[528,128]{1,0:T(8,128)(2,1)S(1)} %shard_map.67), channel_id=1, source_target_pairs={{0,8},{1,9},{2,10},{3,11},{4,12},{5,13},{6,14},{7,15},{8,0},{9,1},... | collective-permute-start | bytes 405512 | tf_op jit(solution)/shard_map/ppermute | solution.py:30

commit v5 on v4

--- a/solution.py
+++ b/solution.py
@@ -270,11 +270,12 @@
     return value * a + other * b, best, total * a + b
 
 
-def join(acc, tops, sums, received, *outs):
+def join(acc, tops, sums, one, two, *outs):
     for block in range(4):
         rows = slice(block * HEAD, (block + 1) * HEAD)
-        norm = unpack(received, 2 * ROWS, block)
-        state = merge(acc[rows, :], tops[rows, :], sums[rows, :], received[rows, :].astype(F32), norm)
+        state = acc[rows, :], tops[rows, :], sums[rows, :]
+        for received in (one, two):
+            state = merge(*state, received[rows, :].astype(F32), unpack(received, 2 * ROWS, block))
         outs[0][rows, :], outs[1][rows, :], outs[2][rows, :] = state
 
 
@@ -364,7 +365,8 @@
     ready = get_ready(span_of, place, own, other)
     rows = spread(jnp.concatenate(held, axis=0), along_first)
     rows = [jnp.concatenate(rows[:2], axis=0), jnp.concatenate(rows[2:], axis=0)]
-    *rows, both, flags, tables = lax.optimization_barrier((*rows, *ready))
+    both, flags, tables = ready
+    *rows, flags, tables = lax.optimization_barrier((*rows, flags, tables))
     ready = (both, flags, tables)
 
     near = [send(half, along_second(STEPS[1])) for half in rows]
@@ -384,8 +386,7 @@
     mate = send(message, swap_cores)
     state = attend(chips, (0,), across, ready, state[:3], (0,))
     half = 2 * ROWS
-    for message in (cross, side):
-        state = call(join, [shape(half, HEAD)] * 3, *state, message)
+    state = call(join, [shape(half, HEAD)] * 3, *state, cross, side)
     return tuple(call(close, [shape(half, HEAD, dtype=BF16), shape(1, half)], tables, *state, mate))
 
 

time: 52.8 us -> 52.9 us (level)
  starting transfers between devices: 29.8 us -> 30.4 us
    ppermute x16, starting transfers between devices: 29.8 us -> 30.4 us  [send(): return lax.ppermute(value, AXES, pairs)]
    pallas_call x10 -> x9, Pallas kernels: 11.8 us -> 11.6 us  [call(): pl.pallas_call(body, out_shape=outs, in_specs=[pl.BlockSpec(memory_space=...]
where the time goes in v5:
time: 52.9 us; the launch traced here: 52.6 us
  starting transfers between devices  30.4 us (57%)
  Pallas kernels  11.6 us (22%)
  waiting for transfers between devices  7.21 us (14%)
  local copies, waits for them, and re-layouts  1.63 us (3%)
  other arithmetic  0.89 us (2%)
  between operations  0.8 us (2%)
    ppermute x16, starting transfers between devices, send(): return lax.ppermute(value, AXES, pairs)  30.4 us
    pallas_call x9, Pallas kernels, call(): pl.pallas_call(body, out_shape=outs, in_specs=[pl.BlockSpec(memory_space=...  11.6 us
    ppermute x16, waiting for transfers between devices, send(): return lax.ppermute(value, AXES, pairs)  7.21 us
  transfers between devices with their start and end apart: 16, of which 8 were waited for; matrix products, arithmetic and copies ran while one was open for 2% of the time, Pallas kernels for 17%

profile of v5, /device:TPU:1, one launch (start us, length us, event | category | flops | bytes accessed | tf_op | source)
XLA Modules:
  0.0 52.6 jit_solution(776285326076632976)
XLA Ops:
  0.6 0.7 %pad_maximum_fusion.3 = bf16[2,64,128]{2,1,0:T(8,128)(2,1)S(1)} fusion(bf16[1,64,128]{2,1,0:T(8,128)(2,1)} %param.6, bf16[1,64,128]{2,1,0:T(8,128)(2,1)} %param.5), kind=kLoop, calls=%fused_computation.3 | loop fusion | flops 16384 | bytes 65536 | tf_op jit(solution)/shard_map/stack | solution.py:359
  1.4 7.7 %collective-permute-start.2 = (bf16[1,2,2,32,128]{4,3,2,1,0:T(8,128)(2,1)S(1)}, bf16[1,2,2,32,128]{4,3,2,1,0:T(8,128)(2,1)S(1)}, u32[]{:S(2)}, u32[]{:S(2)}) collective-permute-start(bf16[1,2,2,32,128]{4,3,2,1,0:T(8,128)(2,1)S(1)} %bitcast.3), channel_id=1, source_target_pairs={{0,4},{1,5},{2,6},{3,7},{4,0},{5,1},{6,2},{7,3},{8,12},{9,13},{10,... | collective-permute-start | bytes 98312 | tf_op jit(solution)/shard_map/ppermute | solution.py:30
  9.1 0.0 collective-permute-start.1
  9.1 1.2 %collective-permute-start = (bf16[1,2,2,32,128]{4,3,2,1,0:T(8,128)(2,1)S(1)}, bf16[1,2,2,32,128]{4,3,2,1,0:T(8,128)(2,1)S(1)}, u32[]{:S(2)}, u32[]{:S(2)}) collective-permute-start(bf16[1,2,2,32,128]{4,3,2,1,0:T(8,128)(2,1)S(1)} %bitcast.5), channel_id=1, source_target_pairs={{0,2},{1,3},{2,0},{3,1},{4,6},{5,7},{6,4},{7,5},{8,10},{9,11},{10,... | collective-permute-start | bytes 98312 | tf_op jit(solution)/shard_map/ppermute | solution.py:30
  10.3 0.0 copy-start
  10.3 0.1 pad_add_fusion.place
  10.4 0.6 %copy-done = s32[64]{0:T(128)S(1)} copy-done((s32[64]{0:T(128)S(1)}, s32[64]{0:T(128)}, u32[]{:S(2)}) %copy-start) | copy-done | bytes 280
  11.0 0.7 %shard_map.59 = (bf16[4,14,16,128]{3,2,1,0:T(8,128)(2,1)S(1)}, f32[4,11,8,128]{3,2,1,0:T(8,128)S(1)}) custom-call(s32[64]{0:T(128)S(1)} %copy-done, s32[2]{0:T(128)S(1)} %pad_add_fusion.place), custom_call_target="tpu_custom_call" | custom-call | flops 1024 | bytes 1024 | tf_op jit(solution)/shard_map/pallas_call | solution.py:308
  11.7 1.1 %collective-permute-done = bf16[1,2,2,32,128]{4,3,2,1,0:T(8,128)(2,1)S(1)} collective-permute-done((bf16[1,2,2,32,128]{4,3,2,1,0:T(8,128)(2,1)S(1)}, bf16[1,2,2,32,128]{4,3,2,1,0:T(8,128)(2,1)S(1)}, u32[]{:S(2)}, u32[]{:S(2)}) %collective-permute-start) | collective-permute-done | bytes 32800 | tf_op jit(solution)/shard_map/ppermute | solution.py:30
  12.8 0.0 collective-permute-done.2
  12.8 1.2 %collective-permute-done.1 = bf16[1,2,2,32,128]{4,3,2,1,0:T(8,128)(2,1)S(1)} collective-permute-done((bf16[1,2,2,32,128]{4,3,2,1,0:T(8,128)(2,1)S(1)}, bf16[1,2,2,32,128]{4,3,2,1,0:T(8,128)(2,1)S(1)}, u32[]{:S(2)}, u32[]{:S(2)}) %collective-permute-start.1) | collective-permute-done | bytes 32800 | tf_op jit(solution)/shard_map/ppermute | solution.py:30
  14.0 3.0 %collective-permute-start.5 = (bf16[4,2,2,32,128]{4,3,2,1,0:T(8,128)(2,1)S(1)}, bf16[4,2,2,32,128]{4,3,2,1,0:T(8,128)(2,1)S(1)}, u32[]{:S(2)}, u32[]{:S(2)}) collective-permute-start(bf16[4,2,2,32,128]{4,3,2,1,0:T(8,128)(2,1)S(1)} %pad_maximum_fusion.2), channel_id=1, source_target_pairs={{0,32},{1,33},{2,34},{3,35},{4,36},{5,37},{6,38},{7,39},{8,136},{9... | collective-permute-start | bytes 393224 | tf_op jit(solution)/shard_map/ppermute | solution.py:30
  17.0 0.8 %collective-permute-start.4 = (bf16[4,2,2,32,128]{4,3,2,1,0:T(8,128)(2,1)S(1)}, bf16[4,2,2,32,128]{4,3,2,1,0:T(8,128)(2,1)S(1)}, u32[]{:S(2)}, u32[]{:S(2)}) collective-permute-start(bf16[4,2,2,32,128]{4,3,2,1,0:T(8,128)(2,1)S(1)} %pad_maximum_fusion.2), channel_id=1, source_target_pairs={{0,48},{1,49},{2,50},{3,51},{4,52},{5,53},{6,54},{7,55},{8,200},{9... | collective-permute-start | bytes 393224 | tf_op jit(solution)/shard_map/ppermute | solution.py:30
  17.8 0.0 collective-permute-start.3
  17.8 1.0 %constant_dynamic-slice_fusion.1 = (bf16[512,128]{1,0:T(8,128)(2,1)S(1)}, bf16[512,128]{1,0:T(8,128)(2,1)S(1)}) fusion(bf16[512,1024]{1,0:T(8,128)(2,1)} %param.4, s32[]{:T(128)S(6)} %select_n.24, s32[]{:T(128)S(6)} %select_n.29), kind=kLoop, calls=%fused_computation.11 | loop fusion | bytes 524296 | tf_op jit(solution)/shard_map/dynamic_slice | solution.py:363
  18.8 3.0 %collective-permute-start.8 = (bf16[512,256]{1,0:T(8,128)(2,1)S(1)}, bf16[512,256]{1,0:T(8,128)(2,1)S(1)}, u32[]{:S(2)}, u32[]{:S(2)}) collective-permute-start(bf16[512,256]{1,0:T(8,128)(2,1)S(1)} %pad_maximum_fusion.1.own), channel_id=1, source_target_pairs={{0,8},{1,9},{2,10},{3,11},{4,12},{5,13},{6,14},{7,15},{8,0},{9,1},... | collective-permute-start | bytes 786440 | tf_op jit(solution)/shard_map/ppermute | solution.py:30
  21.9 0.0 collective-permute-done.5
  21.9 0.4 collective-permute-done.4
  22.4 0.0 collective-permute-done.3
  22.4 1.4 %collective-permute-start.6 = (bf16[8,2,2,32,128]{4,3,2,1,0:T(8,128)(2,1)S(1)}, bf16[8,2,2,32,128]{4,3,2,1,0:T(8,128)(2,1)S(1)}, u32[]{:S(2)}, u32[]{:S(2)}) collective-permute-start(bf16[8,2,2,32,128]{4,3,2,1,0:T(8,128)(2,1)S(1)} %constant_dynamic-update-slice_fusion.refs_0_), channel_id=1, source_target_pairs={{0,64},{1,65},{2,66},{3,67},{4,68},{5,69},{6,70},{7,71},{8,24},{9,... | collective-permute-start | bytes 786440 | tf_op jit(solution)/shard_map/ppermute | solution.py:30
  23.8 1.8 %collective-permute-start.7 = (bf16[8,2,2,32,128]{4,3,2,1,0:T(8,128)(2,1)S(1)}, bf16[8,2,2,32,128]{4,3,2,1,0:T(8,128)(2,1)S(1)}, u32[]{:S(2)}, u32[]{:S(2)}) collective-permute-start(bf16[8,2,2,32,128]{4,3,2,1,0:T(8,128)(2,1)S(1)} %pad_maximum_fusion.refs_1_), channel_id=1, source_target_pairs={{0,192},{1,193},{2,194},{3,195},{4,196},{5,197},{6,198},{7,199},{8... | collective-permute-start | bytes 786440 | tf_op jit(solution)/shard_map/ppermute | solution.py:30
  25.6 0.9 %collective-permute-start.12 = (bf16[8,2,2,32,128]{4,3,2,1,0:T(8,128)(2,1)S(1)}, bf16[8,2,2,32,128]{4,3,2,1,0:T(8,128)(2,1)S(1)}, u32[]{:S(2)}, u32[]{:S(2)}) collective-permute-start(bf16[8,2,2,32,128]{4,3,2,1,0:T(8,128)(2,1)S(1)} %constant_dynamic-update-slice_fusion.refs_0_), channel_id=1, source_target_pairs={{0,192},{1,193},{2,194},{3,195},{4,196},{5,197},{6,198},{7,199},{8... | collective-permute-start | bytes 786440 | tf_op jit(solution)/shard_map/ppermute | solution.py:30
  26.5 0.0 collective-permute-start.11
  26.5 0.0 collective-permute-done.8.other
  26.5 0.1 shard_map.60.refs_2_.refs_4_
  26.6 2.1 %shard_map.61 = (f32[1024,128]{1,0:T(8,128)S(1)}, f32[1024,128]{1,0:T(8,128)S(1)}, f32[1024,128]{1,0:T(8,128)S(1)}, f32[1024,128]{1,0:T(8,128)S(1)}, f32[1024,128]{1,0:T(8,128)S(1)}, /*index=5*/f32[1024,128]{1,0:T(8,128)S(1)}) custom-call(bf16[8,2,2,32,128]{4,3,2,1,0:T(8,128)(2,1)S(1)} %constant_dynamic-update-slice_fusion.refs_0_, ...), custom_call_target="tpu_custom_call" | custom-call | flops 1024 | bytes 1024 | tf_op jit(solution)/shard_map/pallas_call | solution.py:308
  28.7 0.0 collective-permute-done.6.refs_0_
  28.7 1.5 %collective-permute-done.7.refs_3_ = bf16[8,2,2,32,128]{4,3,2,1,0:T(8,128)(2,1)S(1)} collective-permute-done((bf16[8,2,2,32,128]{4,3,2,1,0:T(8,128)(2,1)S(1)}, bf16[8,2,2,32,128]{4,3,2,1,0:T(8,128)(2,1)S(1)}, u32[]{:S(2)}, u32[]{:S(2)}) %collective-permute-start.7) | collective-permute-done | bytes 262176 | tf_op jit(solution)/shard_map/ppermute | solution.py:30
  30.2 1.8 %collective-permute-start.9 = (bf16[8,2,2,32,128]{4,3,2,1,0:T(8,128)(2,1)S(1)}, bf16[8,2,2,32,128]{4,3,2,1,0:T(8,128)(2,1)S(1)}, u32[]{:S(2)}, u32[]{:S(2)}) collective-permute-start(bf16[8,2,2,32,128]{4,3,2,1,0:T(8,128)(2,1)S(1)} %collective-permute-done.6.refs_0_), channel_id=1, source_target_pairs={{0,192},{1,193},{2,194},{3,195},{4,196},{5,197},{6,198},{7,199},{8... | collective-permute-start | bytes 786440 | tf_op jit(solution)/shard_map/ppermute | solution.py:30
  32.0 0.0 collective-permute-start.10
  32.0 1.3 %collective-permute-done.12.refs_2_ = bf16[8,2,2,32,128]{4,3,2,1,0:T(8,128)(2,1)S(1)} collective-permute-done((bf16[8,2,2,32,128]{4,3,2,1,0:T(8,128)(2,1)S(1)}, bf16[8,2,2,32,128]{4,3,2,1,0:T(8,128)(2,1)S(1)}, u32[]{:S(2)}, u32[]{:S(2)}) %collective-permute-start.12) | collective-permute-done | bytes 262176 | tf_op jit(solution)/shard_map/ppermute | solution.py:30
  33.3 0.0 collective-permute-done.11.refs_1_
  33.3 4.1 %shard_map.62 = (f32[1024,128]{1,0:T(8,128)S(1)}, f32[1024,128]{1,0:T(8,128)S(1)}, f32[1024,128]{1,0:T(8,128)S(1)}, f32[1024,128]{1,0:T(8,128)S(1)}, f32[1024,128]{1,0:T(8,128)S(1)}, /*index=5*/f32[1024,128]{1,0:T(8,128)S(1)}) custom-call(bf16[8,2,2,32,128]{4,3,2,1,0:T(8,128)(2,1)S(1)} %collect, ...), custom_call_target="tpu_custom_call", output_to_operand_aliasing={{0}: (7, {}), {1}: (8, {}), {2}: (9, {}), {3}: (10, {}), {4... | custom-call | flops 1024 | bytes 1024 | tf_op jit(solution)/shard_map/pallas_call | solution.py:308
  37.4 0.0 collective-permute-done.9.refs_0_
  37.4 0.2 collective-permute-done.10.refs_1_
  37.6 1.4 %shard_map.63 = (bf16[528,128]{1,0:T(8,128)(2,1)S(1)}, bf16[528,128]{1,0:T(8,128)(2,1)S(1)}) custom-call(bf16[8,2,2,32,128]{4,3,2,1,0:T(8,128)(2,1)S(1)} %collective-permute-done.9.refs_0_, bf16[8,2,2,32,128]{4,3,2,1,0:T(8,128)(2,1)S(1)} %collective-permute-done.10.refs_1_, bf16[2,512,256]{2,1,0:T(8,128)(2,1)S(1)} %shard_map.60.refs_2_.refs_4_, ...), custom_call_target="tpu_custom_call" | custom-call | flops 1024 | bytes 1024 | tf_op jit(solution)/shard_map/pallas_call | solution.py:308
  39.0 6.5 %collective-permute-start.13 = (bf16[528,128]{1,0:T(8,128)(2,1)S(1)}, bf16[528,128]{1,0:T(8,128)(2,1)S(1)}, u32[]{:S(2)}, u32[]{:S(2)}) collective-permute-start(bf16[528,128]{1,0:T(8,128)(2,1)S(1)} %get-tuple-element.82), channel_id=1, source_target_pairs={{0,15},{1,10},{2,9},{3,12},{4,11},{5,14},{6,13},{7,8},{8,1},{9,0},... | collective-permute-start | bytes 405512 | tf_op jit(solution)/shard_map/ppermute | solution.py:30
  45.5 2.2 %collective-permute-start.14 = (bf16[528,128]{1,0:T(8,128)(2,1)S(1)}, bf16[528,128]{1,0:T(8,128)(2,1)S(1)}, u32[]{:S(2)}, u32[]{:S(2)}) collective-permute-start(bf16[528,128]{1,0:T(8,128)(2,1)S(1)} %get-tuple-element.83), channel_id=1, source_target_pairs={{0,1},{1,0},{2,3},{3,2},{4,5},{5,4},{6,7},{7,6},{8,15},{9,10},{10,... | collective-permute-start | bytes 405512 | tf_op jit(solution)/shard_map/ppermute | solution.py:30
  47.7 0.9 %shard_map.66 = bf16[528,128]{1,0:T(8,128)(2,1)S(1)} custom-call(bf16[8,2,2,32,128]{4,3,2,1,0:T(8,128)(2,1)S(1)} %collective-permute-done.9.refs_0_, bf16[8,2,2,32,128]{4,3,2,1,0:T(8,128)(2,1)S(1)} %collective-permute-done.10.refs_1_, bf16[2,512,256]{2,1,0:T(8,128)(2,1)S(1)} %shard_map.60.refs_2_.refs_4_, ...), custom_call_target="tpu_custom_call" | custom-call | flops 1024 | bytes 1024 | tf_op jit(solution)/shard_map/pallas_call | solution.py:308
  48.6 0.1 collective-permute-start.15
  48.7 0.9 %shard_map.64 = (f32[512,128]{1,0:T(8,128)S(1)}, f32[512,128]{1,0:T(8,128)S(1)}, f32[512,128]{1,0:T(8,128)S(1)}) custom-call(bf16[8,2,2,32,128]{4,3,2,1,0:T(8,128)(2,1)S(1)} %collective-permute-done.9.refs_0_, bf16[8,2,2,32,128]{4,3,2,1,0:T(8,128)(2,1)S(1)} %collective-permute-done.10.refs_1_, bf16[2,512,256]{2,1,0:T(8,128)(2,1)S(1)} %shard_map.60.refs_2_.refs_4_, ...), custom_call_target="tpu_custom_call" | custom-call | flops 1024 | bytes 1024 | tf_op jit(solution)/shard_map/pallas_call | solution.py:308
  49.6 0.6 %collective-permute-done.13.one = bf16[528,128]{1,0:T(8,128)(2,1)S(1)} collective-permute-done((bf16[528,128]{1,0:T(8,128)(2,1)S(1)}, bf16[528,128]{1,0:T(8,128)(2,1)S(1)}, u32[]{:S(2)}, u32[]{:S(2)}) %collective-permute-start.13) | collective-permute-done | bytes 135200 | tf_op jit(solution)/shard_map/ppermute | solution.py:30
  50.3 0.9 %collective-permute-done.14.two = bf16[528,128]{1,0:T(8,128)(2,1)S(1)} collective-permute-done((bf16[528,128]{1,0:T(8,128)(2,1)S(1)}, bf16[528,128]{1,0:T(8,128)(2,1)S(1)}, u32[]{:S(2)}, u32[]{:S(2)}) %collective-permute-start.14) | collective-permute-done | bytes 135200 | tf_op jit(solution)/shard_map/ppermute | solution.py:30
  51.1 0.4 shard_map.65
  51.6 0.0 collective-permute-done.15.received
  51.6 1.0 %shard_map.67 = (bf16[512,128]{1,0:T(8,128)(2,1)}, f32[1,512]{1,0:T(1,128)}) custom-call(f32[4,11,8,128]{3,2,1,0:T(8,128)S(1)} %get-tuple-element.49.refs_4_.refs_6_.tables, f32[512,128]{1,0:T(8,128)S(1)} %get-tuple-element.84.mine, f32[512,128]{1,0:T(8,128)S(1)} %get-tuple-element.85.mine_tops, f32[512,128]{1,0:T(8,128)S(1)} %get-tuple-element.86.mine_sums, ...), custom_call_target="tpu_custom_call" | custom-call | flops 1024 | bytes 1024 | tf_op jit(solution)/shard_map/pallas_call | solution.py:308
  (8 shorter events, 0.1 us)
Async XLA Ops:
  1.4 11.4 %collective-permute-start.2 = (bf16[1,2,2,32,128]{4,3,2,1,0:T(8,128)(2,1)S(1)}, bf16[1,2,2,32,128]{4,3,2,1,0:T(8,128)(2,1)S(1)}, u32[]{:S(2)}, u32[]{:S(2)}) collective-permute-start(bf16[1,2,2,32,128]{4,3,2,1,0:T(8,128)(2,1)S(1)} %bitcast.3), channel_id=1, source_target_pairs={{0,4},{1,5},{2,6},{3,7},{4,0},{5,1},{6,2},{7,3},{8,12},{9,13},{10,... | collective-permute-start | bytes 98312 | tf_op jit(solution)/shard_map/ppermute | solution.py:30
  9.1 4.9 %collective-permute-start.1 = (bf16[1,2,2,32,128]{4,3,2,1,0:T(8,128)(2,1)S(1)}, bf16[1,2,2,32,128]{4,3,2,1,0:T(8,128)(2,1)S(1)}, u32[]{:S(2)}, u32[]{:S(2)}) collective-permute-start(bf16[1,2,2,32,128]{4,3,2,1,0:T(8,128)(2,1)S(1)} %bitcast.4), channel_id=1, source_target_pairs={{0,6},{1,7},{2,4},{3,5},{4,2},{5,3},{6,0},{7,1},{8,14},{9,15},{10,... | collective-permute-start | bytes 98312 | tf_op jit(solution)/shard_map/ppermute | solution.py:30
  9.1 3.7 %collective-permute-start = (bf16[1,2,2,32,128]{4,3,2,1,0:T(8,128)(2,1)S(1)}, bf16[1,2,2,32,128]{4,3,2,1,0:T(8,128)(2,1)S(1)}, u32[]{:S(2)}, u32[]{:S(2)}) collective-permute-start(bf16[1,2,2,32,128]{4,3,2,1,0:T(8,128)(2,1)S(1)} %bitcast.5), channel_id=1, source_target_pairs={{0,2},{1,3},{2,0},{3,1},{4,6},{5,7},{6,4},{7,5},{8,10},{9,11},{10,... | collective-permute-start | bytes 98312 | tf_op jit(solution)/shard_map/ppermute | solution.py:30
  10.3 0.7 %copy-start = (s32[64]{0:T(128)S(1)}, s32[64]{0:T(128)}, u32[]{:S(2)}) copy-start(s32[64]{0:T(128)} %span.1) | copy-start | bytes 772
  14.0 7.9 %collective-permute-start.5 = (bf16[4,2,2,32,128]{4,3,2,1,0:T(8,128)(2,1)S(1)}, bf16[4,2,2,32,128]{4,3,2,1,0:T(8,128)(2,1)S(1)}, u32[]{:S(2)}, u32[]{:S(2)}) collective-permute-start(bf16[4,2,2,32,128]{4,3,2,1,0:T(8,128)(2,1)S(1)} %pad_maximum_fusion.2), channel_id=1, source_target_pairs={{0,32},{1,33},{2,34},{3,35},{4,36},{5,37},{6,38},{7,39},{8,136},{9... | collective-permute-start | bytes 393224 | tf_op jit(solution)/shard_map/ppermute | solution.py:30
  17.0 5.3 %collective-permute-start.4 = (bf16[4,2,2,32,128]{4,3,2,1,0:T(8,128)(2,1)S(1)}, bf16[4,2,2,32,128]{4,3,2,1,0:T(8,128)(2,1)S(1)}, u32[]{:S(2)}, u32[]{:S(2)}) collective-permute-start(bf16[4,2,2,32,128]{4,3,2,1,0:T(8,128)(2,1)S(1)} %pad_maximum_fusion.2), channel_id=1, source_target_pairs={{0,48},{1,49},{2,50},{3,51},{4,52},{5,53},{6,54},{7,55},{8,200},{9... | collective-permute-start | bytes 393224 | tf_op jit(solution)/shard_map/ppermute | solution.py:30
  17.8 4.6 %collective-permute-start.3 = (bf16[4,2,2,32,128]{4,3,2,1,0:T(8,128)(2,1)S(1)}, bf16[4,2,2,32,128]{4,3,2,1,0:T(8,128)(2,1)S(1)}, u32[]{:S(2)}, u32[]{:S(2)}) collective-permute-start(bf16[4,2,2,32,128]{4,3,2,1,0:T(8,128)(2,1)S(1)} %pad_maximum_fusion.2), channel_id=1, source_target_pairs={{0,16},{1,17},{2,18},{3,19},{4,20},{5,21},{6,22},{7,23},{8,72},{9,... | collective-permute-start | bytes 393224 | tf_op jit(solution)/shard_map/ppermute | solution.py:30
  18.8 7.6 %collective-permute-start.8 = (bf16[512,256]{1,0:T(8,128)(2,1)S(1)}, bf16[512,256]{1,0:T(8,128)(2,1)S(1)}, u32[]{:S(2)}, u32[]{:S(2)}) collective-permute-start(bf16[512,256]{1,0:T(8,128)(2,1)S(1)} %pad_maximum_fusion.1.own), channel_id=1, source_target_pairs={{0,8},{1,9},{2,10},{3,11},{4,12},{5,13},{6,14},{7,15},{8,0},{9,1},... | collective-permute-start | bytes 786440 | tf_op jit(solution)/shard_map/ppermute | solution.py:30
  22.4 6.3 %collective-permute-start.6 = (bf16[8,2,2,32,128]{4,3,2,1,0:T(8,128)(2,1)S(1)}, bf16[8,2,2,32,128]{4,3,2,1,0:T(8,128)(2,1)S(1)}, u32[]{:S(2)}, u32[]{:S(2)}) collective-permute-start(bf16[8,2,2,32,128]{4,3,2,1,0:T(8,128)(2,1)S(1)} %constant_dynamic-update-slice_fusion.refs_0_), channel_id=1, source_target_pairs={{0,64},{1,65},{2,66},{3,67},{4,68},{5,69},{6,70},{7,71},{8,24},{9,... | collective-permute-start | bytes 786440 | tf_op jit(solution)/shard_map/ppermute | solution.py:30
  23.8 6.4 %collective-permute-start.7 = (bf16[8,2,2,32,128]{4,3,2,1,0:T(8,128)(2,1)S(1)}, bf16[8,2,2,32,128]{4,3,2,1,0:T(8,128)(2,1)S(1)}, u32[]{:S(2)}, u32[]{:S(2)}) collective-permute-start(bf16[8,2,2,32,128]{4,3,2,1,0:T(8,128)(2,1)S(1)} %pad_maximum_fusion.refs_1_), channel_id=1, source_target_pairs={{0,192},{1,193},{2,194},{3,195},{4,196},{5,197},{6,198},{7,199},{8... | collective-permute-start | bytes 786440 | tf_op jit(solution)/shard_map/ppermute | solution.py:30
  25.6 7.7 %collective-permute-start.12 = (bf16[8,2,2,32,128]{4,3,2,1,0:T(8,128)(2,1)S(1)}, bf16[8,2,2,32,128]{4,3,2,1,0:T(8,128)(2,1)S(1)}, u32[]{:S(2)}, u32[]{:S(2)}) collective-permute-start(bf16[8,2,2,32,128]{4,3,2,1,0:T(8,128)(2,1)S(1)} %constant_dynamic-update-slice_fusion.refs_0_), channel_id=1, source_target_pairs={{0,192},{1,193},{2,194},{3,195},{4,196},{5,197},{6,198},{7,199},{8... | collective-permute-start | bytes 786440 | tf_op jit(solution)/shard_map/ppermute | solution.py:30
  26.5 6.9 %collective-permute-start.11 = (bf16[8,2,2,32,128]{4,3,2,1,0:T(8,128)(2,1)S(1)}, bf16[8,2,2,32,128]{4,3,2,1,0:T(8,128)(2,1)S(1)}, u32[]{:S(2)}, u32[]{:S(2)}) collective-permute-start(bf16[8,2,2,32,128]{4,3,2,1,0:T(8,128)(2,1)S(1)} %pad_maximum_fusion.refs_1_), channel_id=1, source_target_pairs={{0,64},{1,65},{2,66},{3,67},{4,68},{5,69},{6,70},{7,71},{8,24},{9,... | collective-permute-start | bytes 786440 | tf_op jit(solution)/shard_map/ppermute | solution.py:30
  30.2 7.2 %collective-permute-start.9 = (bf16[8,2,2,32,128]{4,3,2,1,0:T(8,128)(2,1)S(1)}, bf16[8,2,2,32,128]{4,3,2,1,0:T(8,128)(2,1)S(1)}, u32[]{:S(2)}, u32[]{:S(2)}) collective-permute-start(bf16[8,2,2,32,128]{4,3,2,1,0:T(8,128)(2,1)S(1)} %collective-permute-done.6.refs_0_), channel_id=1, source_target_pairs={{0,192},{1,193},{2,194},{3,195},{4,196},{5,197},{6,198},{7,199},{8... | collective-permute-start | bytes 786440 | tf_op jit(solution)/shard_map/ppermute | solution.py:30
  32.0 5.5 %collective-permute-start.10 = (bf16[8,2,2,32,128]{4,3,2,1,0:T(8,128)(2,1)S(1)}, bf16[8,2,2,32,128]{4,3,2,1,0:T(8,128)(2,1)S(1)}, u32[]{:S(2)}, u32[]{:S(2)}) collective-permute-start(bf16[8,2,2,32,128]{4,3,2,1,0:T(8,128)(2,1)S(1)} %collective-permute-done.7.refs_3_), channel_id=1, source_target_pairs={{0,64},{1,65},{2,66},{3,67},{4,68},{5,69},{6,70},{7,71},{8,24},{9,... | collective-permute-start | bytes 786440 | tf_op jit(solution)/shard_map/ppermute | solution.py:30
  39.0 11.2 %collective-permute-start.13 = (bf16[528,128]{1,0:T(8,128)(2,1)S(1)}, bf16[528,128]{1,0:T(8,128)(2,1)S(1)}, u32[]{:S(2)}, u32[]{:S(2)}) collective-permute-start(bf16[528,128]{1,0:T(8,128)(2,1)S(1)} %get-tuple-element.82), channel_id=1, source_target_pairs={{0,15},{1,10},{2,9},{3,12},{4,11},{5,14},{6,13},{7,8},{8,1},{9,0},... | collective-permute-start | bytes 405512 | tf_op jit(solution)/shard_map/ppermute | solution.py:30
  45.5 5.6 %collective-permute-start.14 = (bf16[528,128]{1,0:T(8,128)(2,1)S(1)}, bf16[528,128]{1,0:T(8,128)(2,1)S(1)}, u32[]{:S(2)}, u32[]{:S(2)}) collective-permute-start(bf16[528,128]{1,0:T(8,128)(2,1)S(1)} %get-tuple-element.83), channel_id=1, source_target_pairs={{0,1},{1,0},{2,3},{3,2},{4,5},{5,4},{6,7},{7,6},{8,15},{9,10},{10,... | collective-permute-start | bytes 405512 | tf_op jit(solution)/shard_map/ppermute | solution.py:30
  48.6 2.9 %collective-permute-start.15 = (bf16[528,128]{1,0:T(8,128)(2,1)S(1)}, bf16[528,128]{1,0:T(8,128)(2,1)S(1)}, u32[]{:S(2)}, u32[]{:S(2)}) collective-permute-start(bf16[528,128]{1,0:T(8,128)(2,1)S(1)} %shard_map.66), channel_id=1, source_target_pairs={{0,8},{1,9},{2,10},{3,11},{4,12},{5,13},{6,14},{7,15},{8,0},{9,1},... | collective-permute-start | bytes 405512 | tf_op jit(solution)/shard_map/ppermute | solution.py:30

commit v6 on v4

--- a/solution.py
+++ b/solution.py
@@ -364,7 +364,8 @@
     ready = get_ready(span_of, place, own, other)
     rows = spread(jnp.concatenate(held, axis=0), along_first)
     rows = [jnp.concatenate(rows[:2], axis=0), jnp.concatenate(rows[2:], axis=0)]
-    *rows, both, flags, tables = lax.optimization_barrier((*rows, *ready))
+    both, flags, tables = ready
+    *rows, flags, tables = lax.optimization_barrier((*rows, flags, tables))
     ready = (both, flags, tables)
 
     near = [send(half, along_second(STEPS[1])) for half in rows]

time: 52.8 us -> 52.8 us (level)
  waiting for transfers between devices: 7.53 us -> 6.92 us
  starting transfers between devices: 29.8 us -> 30.4 us
    ppermute x16, waiting for transfers between devices: 7.53 us -> 6.92 us  [send(): return lax.ppermute(value, AXES, pairs)]
    ppermute x16, starting transfers between devices: 29.8 us -> 30.4 us  [send(): return lax.ppermute(value, AXES, pairs)]
  transfers between devices with their start and end apart: 16 -> 16, of which waited for: 8 -> 8; matrix products, arithmetic and copies ran while one was open for 2% -> 2% of each run, Pallas kernels for 17% -> 18%
where the time goes in v6:
time: 52.8 us; the launch traced here: 52.5 us
  starting transfers between devices  30.4 us (58%)
  Pallas kernels  11.8 us (22%)
  waiting for transfers between devices  6.92 us (13%)
  local copies, waits for them, and re-layouts  1.63 us (3%)
  other arithmetic  0.89 us (2%)
  between operations  0.8 us (2%)
    ppermute x16, starting transfers between devices, send(): return lax.ppermute(value, AXES, pairs)  30.4 us
    pallas_call x10, Pallas kernels, call(): pl.pallas_call(body, out_shape=outs, in_specs=[pl.BlockSpec(memory_space=...  11.8 us
    ppermute x16, waiting for transfers between devices, send(): return lax.ppermute(value, AXES, pairs)  6.92 us
  transfers between devices with their start and end apart: 16, of which 8 were waited for; matrix products, arithmetic and copies ran while one was open for 2% of the time, Pallas kernels for 18%

profile of v6, /device:TPU:1, one launch (start us, length us, event | category | flops | bytes accessed | tf_op | source)
XLA Modules:
  0.0 52.5 jit_solution(2581816690160731201)
XLA Ops:
  0.6 0.7 %pad_maximum_fusion.3 = bf16[2,64,128]{2,1,0:T(8,128)(2,1)S(1)} fusion(bf16[1,64,128]{2,1,0:T(8,128)(2,1)} %param.6, bf16[1,64,128]{2,1,0:T(8,128)(2,1)} %param.5), kind=kLoop, calls=%fused_computation.3 | loop fusion | flops 16384 | bytes 65536 | tf_op jit(solution)/shard_map/stack | solution.py:358
  1.4 7.7 %collective-permute-start.2 = (bf16[1,2,2,32,128]{4,3,2,1,0:T(8,128)(2,1)S(1)}, bf16[1,2,2,32,128]{4,3,2,1,0:T(8,128)(2,1)S(1)}, u32[]{:S(2)}, u32[]{:S(2)}) collective-permute-start(bf16[1,2,2,32,128]{4,3,2,1,0:T(8,128)(2,1)S(1)} %bitcast.3), channel_id=1, source_target_pairs={{0,4},{1,5},{2,6},{3,7},{4,0},{5,1},{6,2},{7,3},{8,12},{9,13},{10,... | collective-permute-start | bytes 98312 | tf_op jit(solution)/shard_map/ppermute | solution.py:30
  9.1 0.0 collective-permute-start.1
  9.1 1.2 %collective-permute-start = (bf16[1,2,2,32,128]{4,3,2,1,0:T(8,128)(2,1)S(1)}, bf16[1,2,2,32,128]{4,3,2,1,0:T(8,128)(2,1)S(1)}, u32[]{:S(2)}, u32[]{:S(2)}) collective-permute-start(bf16[1,2,2,32,128]{4,3,2,1,0:T(8,128)(2,1)S(1)} %bitcast.5), channel_id=1, source_target_pairs={{0,2},{1,3},{2,0},{3,1},{4,6},{5,7},{6,4},{7,5},{8,10},{9,11},{10,... | collective-permute-start | bytes 98312 | tf_op jit(solution)/shard_map/ppermute | solution.py:30
  10.3 0.0 copy-start
  10.3 0.1 pad_add_fusion.place
  10.4 0.6 %copy-done = s32[64]{0:T(128)S(1)} copy-done((s32[64]{0:T(128)S(1)}, s32[64]{0:T(128)}, u32[]{:S(2)}) %copy-start) | copy-done | bytes 280
  11.0 0.7 %shard_map.59 = (bf16[4,14,16,128]{3,2,1,0:T(8,128)(2,1)S(1)}, f32[4,11,8,128]{3,2,1,0:T(8,128)S(1)}) custom-call(s32[64]{0:T(128)S(1)} %copy-done, s32[2]{0:T(128)S(1)} %pad_add_fusion.place), custom_call_target="tpu_custom_call" | custom-call | flops 1024 | bytes 1024 | tf_op jit(solution)/shard_map/pallas_call | solution.py:307
  11.7 1.1 %collective-permute-done = bf16[1,2,2,32,128]{4,3,2,1,0:T(8,128)(2,1)S(1)} collective-permute-done((bf16[1,2,2,32,128]{4,3,2,1,0:T(8,128)(2,1)S(1)}, bf16[1,2,2,32,128]{4,3,2,1,0:T(8,128)(2,1)S(1)}, u32[]{:S(2)}, u32[]{:S(2)}) %collective-permute-start) | collective-permute-done | bytes 32800 | tf_op jit(solution)/shard_map/ppermute | solution.py:30
  12.8 0.0 collective-permute-done.2
  12.8 1.2 %collective-permute-done.1 = bf16[1,2,2,32,128]{4,3,2,1,0:T(8,128)(2,1)S(1)} collective-permute-done((bf16[1,2,2,32,128]{4,3,2,1,0:T(8,128)(2,1)S(1)}, bf16[1,2,2,32,128]{4,3,2,1,0:T(8,128)(2,1)S(1)}, u32[]{:S(2)}, u32[]{:S(2)}) %collective-permute-start.1) | collective-permute-done | bytes 32800 | tf_op jit(solution)/shard_map/ppermute | solution.py:30
  14.0 3.0 %collective-permute-start.5 = (bf16[4,2,2,32,128]{4,3,2,1,0:T(8,128)(2,1)S(1)}, bf16[4,2,2,32,128]{4,3,2,1,0:T(8,128)(2,1)S(1)}, u32[]{:S(2)}, u32[]{:S(2)}) collective-permute-start(bf16[4,2,2,32,128]{4,3,2,1,0:T(8,128)(2,1)S(1)} %pad_maximum_fusion.2), channel_id=1, source_target_pairs={{0,32},{1,33},{2,34},{3,35},{4,36},{5,37},{6,38},{7,39},{8,136},{9... | collective-permute-start | bytes 393224 | tf_op jit(solution)/shard_map/ppermute | solution.py:30
  17.0 0.8 %collective-permute-start.4 = (bf16[4,2,2,32,128]{4,3,2,1,0:T(8,128)(2,1)S(1)}, bf16[4,2,2,32,128]{4,3,2,1,0:T(8,128)(2,1)S(1)}, u32[]{:S(2)}, u32[]{:S(2)}) collective-permute-start(bf16[4,2,2,32,128]{4,3,2,1,0:T(8,128)(2,1)S(1)} %pad_maximum_fusion.2), channel_id=1, source_target_pairs={{0,48},{1,49},{2,50},{3,51},{4,52},{5,53},{6,54},{7,55},{8,200},{9... | collective-permute-start | bytes 393224 | tf_op jit(solution)/shard_map/ppermute | solution.py:30
  17.8 0.0 collective-permute-start.3
  17.8 1.0 %constant_dynamic-slice_fusion.1 = (bf16[512,128]{1,0:T(8,128)(2,1)S(1)}, bf16[512,128]{1,0:T(8,128)(2,1)S(1)}) fusion(bf16[512,1024]{1,0:T(8,128)(2,1)} %param.4, s32[]{:T(128)S(6)} %select_n.24, s32[]{:T(128)S(6)} %select_n.29), kind=kLoop, calls=%fused_computation.11 | loop fusion | bytes 524296 | tf_op jit(solution)/shard_map/dynamic_slice | solution.py:362
  18.8 3.0 %collective-permute-start.8 = (bf16[512,256]{1,0:T(8,128)(2,1)S(1)}, bf16[512,256]{1,0:T(8,128)(2,1)S(1)}, u32[]{:S(2)}, u32[]{:S(2)}) collective-permute-start(bf16[512,256]{1,0:T(8,128)(2,1)S(1)} %pad_maximum_fusion.1.own), channel_id=1, source_target_pairs={{0,8},{1,9},{2,10},{3,11},{4,12},{5,13},{6,14},{7,15},{8,0},{9,1},... | collective-permute-start | bytes 786440 | tf_op jit(solution)/shard_map/ppermute | solution.py:30
  21.9 0.0 collective-permute-done.5
  21.9 0.4 collective-permute-done.4
  22.4 0.0 collective-permute-done.3
  22.4 1.4 %collective-permute-start.6 = (bf16[8,2,2,32,128]{4,3,2,1,0:T(8,128)(2,1)S(1)}, bf16[8,2,2,32,128]{4,3,2,1,0:T(8,128)(2,1)S(1)}, u32[]{:S(2)}, u32[]{:S(2)}) collective-permute-start(bf16[8,2,2,32,128]{4,3,2,1,0:T(8,128)(2,1)S(1)} %constant_dynamic-update-slice_fusion.refs_0_), channel_id=1, source_target_pairs={{0,64},{1,65},{2,66},{3,67},{4,68},{5,69},{6,70},{7,71},{8,24},{9,... | collective-permute-start | bytes 786440 | tf_op jit(solution)/shard_map/ppermute | solution.py:30
  23.8 1.8 %collective-permute-start.7 = (bf16[8,2,2,32,128]{4,3,2,1,0:T(8,128)(2,1)S(1)}, bf16[8,2,2,32,128]{4,3,2,1,0:T(8,128)(2,1)S(1)}, u32[]{:S(2)}, u32[]{:S(2)}) collective-permute-start(bf16[8,2,2,32,128]{4,3,2,1,0:T(8,128)(2,1)S(1)} %pad_maximum_fusion.refs_1_), channel_id=1, source_target_pairs={{0,192},{1,193},{2,194},{3,195},{4,196},{5,197},{6,198},{7,199},{8... | collective-permute-start | bytes 786440 | tf_op jit(solution)/shard_map/ppermute | solution.py:30
  25.6 0.9 %collective-permute-start.12 = (bf16[8,2,2,32,128]{4,3,2,1,0:T(8,128)(2,1)S(1)}, bf16[8,2,2,32,128]{4,3,2,1,0:T(8,128)(2,1)S(1)}, u32[]{:S(2)}, u32[]{:S(2)}) collective-permute-start(bf16[8,2,2,32,128]{4,3,2,1,0:T(8,128)(2,1)S(1)} %constant_dynamic-update-slice_fusion.refs_0_), channel_id=1, source_target_pairs={{0,192},{1,193},{2,194},{3,195},{4,196},{5,197},{6,198},{7,199},{8... | collective-permute-start | bytes 786440 | tf_op jit(solution)/shard_map/ppermute | solution.py:30
  26.5 0.0 collective-permute-start.11
  26.5 0.0 collective-permute-done.8.other
  26.5 0.1 shard_map.60.refs_2_.refs_4_
  26.6 2.1 %shard_map.61 = (f32[1024,128]{1,0:T(8,128)S(1)}, f32[1024,128]{1,0:T(8,128)S(1)}, f32[1024,128]{1,0:T(8,128)S(1)}, f32[1024,128]{1,0:T(8,128)S(1)}, f32[1024,128]{1,0:T(8,128)S(1)}, /*index=5*/f32[1024,128]{1,0:T(8,128)S(1)}) custom-call(bf16[8,2,2,32,128]{4,3,2,1,0:T(8,128)(2,1)S(1)} %constant_dynamic-update-slice_fusion.refs_0_, ...), custom_call_target="tpu_custom_call" | custom-call | flops 1024 | bytes 1024 | tf_op jit(solution)/shard_map/pallas_call | solution.py:307
  28.7 0.0 collective-permute-done.6.refs_0_
  28.7 1.5 %collective-permute-done.7.refs_3_ = bf16[8,2,2,32,128]{4,3,2,1,0:T(8,128)(2,1)S(1)} collective-permute-done((bf16[8,2,2,32,128]{4,3,2,1,0:T(8,128)(2,1)S(1)}, bf16[8,2,2,32,128]{4,3,2,1,0:T(8,128)(2,1)S(1)}, u32[]{:S(2)}, u32[]{:S(2)}) %collective-permute-start.7) | collective-permute-done | bytes 262176 | tf_op jit(solution)/shard_map/ppermute | solution.py:30
  30.2 1.8 %collective-permute-start.9 = (bf16[8,2,2,32,128]{4,3,2,1,0:T(8,128)(2,1)S(1)}, bf16[8,2,2,32,128]{4,3,2,1,0:T(8,128)(2,1)S(1)}, u32[]{:S(2)}, u32[]{:S(2)}) collective-permute-start(bf16[8,2,2,32,128]{4,3,2,1,0:T(8,128)(2,1)S(1)} %collective-permute-done.6.refs_0_), channel_id=1, source_target_pairs={{0,192},{1,193},{2,194},{3,195},{4,196},{5,197},{6,198},{7,199},{8... | collective-permute-start | bytes 786440 | tf_op jit(solution)/shard_map/ppermute | solution.py:30
  32.0 0.0 collective-permute-start.10
  32.0 1.3 %collective-permute-done.12.refs_2_ = bf16[8,2,2,32,128]{4,3,2,1,0:T(8,128)(2,1)S(1)} collective-permute-done((bf16[8,2,2,32,128]{4,3,2,1,0:T(8,128)(2,1)S(1)}, bf16[8,2,2,32,128]{4,3,2,1,0:T(8,128)(2,1)S(1)}, u32[]{:S(2)}, u32[]{:S(2)}) %collective-permute-start.12) | collective-permute-done | bytes 262176 | tf_op jit(solution)/shard_map/ppermute | solution.py:30
  33.3 0.0 collective-permute-done.11.refs_1_
  33.3 4.1 %shard_map.62 = (f32[1024,128]{1,0:T(8,128)S(1)}, f32[1024,128]{1,0:T(8,128)S(1)}, f32[1024,128]{1,0:T(8,128)S(1)}, f32[1024,128]{1,0:T(8,128)S(1)}, f32[1024,128]{1,0:T(8,128)S(1)}, /*index=5*/f32[1024,128]{1,0:T(8,128)S(1)}) custom-call(bf16[8,2,2,32,128]{4,3,2,1,0:T(8,128)(2,1)S(1)} %collect, ...), custom_call_target="tpu_custom_call", output_to_operand_aliasing={{0}: (7, {}), {1}: (8, {}), {2}: (9, {}), {3}: (10, {}), {4... | custom-call | flops 1024 | bytes 1024 | tf_op jit(solution)/shard_map/pallas_call | solution.py:307
  37.4 0.0 collective-permute-done.9.refs_0_
  37.4 0.2 collective-permute-done.10.refs_1_
  37.6 1.4 %shard_map.63 = (bf16[528,128]{1,0:T(8,128)(2,1)S(1)}, bf16[528,128]{1,0:T(8,128)(2,1)S(1)}) custom-call(bf16[8,2,2,32,128]{4,3,2,1,0:T(8,128)(2,1)S(1)} %collective-permute-done.9.refs_0_, bf16[8,2,2,32,128]{4,3,2,1,0:T(8,128)(2,1)S(1)} %collective-permute-done.10.refs_1_, bf16[2,512,256]{2,1,0:T(8,128)(2,1)S(1)} %shard_map.60.refs_2_.refs_4_, ...), custom_call_target="tpu_custom_call" | custom-call | flops 1024 | bytes 1024 | tf_op jit(solution)/shard_map/pallas_call | solution.py:307
  39.0 6.5 %collective-permute-start.13 = (bf16[528,128]{1,0:T(8,128)(2,1)S(1)}, bf16[528,128]{1,0:T(8,128)(2,1)S(1)}, u32[]{:S(2)}, u32[]{:S(2)}) collective-permute-start(bf16[528,128]{1,0:T(8,128)(2,1)S(1)} %get-tuple-element.85), channel_id=1, source_target_pairs={{0,15},{1,10},{2,9},{3,12},{4,11},{5,14},{6,13},{7,8},{8,1},{9,0},... | collective-permute-start | bytes 405512 | tf_op jit(solution)/shard_map/ppermute | solution.py:30
  45.5 2.2 %collective-permute-start.14 = (bf16[528,128]{1,0:T(8,128)(2,1)S(1)}, bf16[528,128]{1,0:T(8,128)(2,1)S(1)}, u32[]{:S(2)}, u32[]{:S(2)}) collective-permute-start(bf16[528,128]{1,0:T(8,128)(2,1)S(1)} %get-tuple-element.89), channel_id=1, source_target_pairs={{0,1},{1,0},{2,3},{3,2},{4,5},{5,4},{6,7},{7,6},{8,15},{9,10},{10,... | collective-permute-start | bytes 405512 | tf_op jit(solution)/shard_map/ppermute | solution.py:30
  47.7 0.9 %shard_map.67 = bf16[528,128]{1,0:T(8,128)(2,1)S(1)} custom-call(bf16[8,2,2,32,128]{4,3,2,1,0:T(8,128)(2,1)S(1)} %collective-permute-done.9.refs_0_, bf16[8,2,2,32,128]{4,3,2,1,0:T(8,128)(2,1)S(1)} %collective-permute-done.10.refs_1_, bf16[2,512,256]{2,1,0:T(8,128)(2,1)S(1)} %shard_map.60.refs_2_.refs_4_, ...), custom_call_target="tpu_custom_call" | custom-call | flops 1024 | bytes 1024 | tf_op jit(solution)/shard_map/pallas_call | solution.py:307
  48.6 0.1 collective-permute-start.15
  48.7 0.9 %shard_map.64 = (f32[512,128]{1,0:T(8,128)S(1)}, f32[512,128]{1,0:T(8,128)S(1)}, f32[512,128]{1,0:T(8,128)S(1)}) custom-call(bf16[8,2,2,32,128]{4,3,2,1,0:T(8,128)(2,1)S(1)} %collective-permute-done.9.refs_0_, bf16[8,2,2,32,128]{4,3,2,1,0:T(8,128)(2,1)S(1)} %collective-permute-done.10.refs_1_, bf16[2,512,256]{2,1,0:T(8,128)(2,1)S(1)} %shard_map.60.refs_2_.refs_4_, ...), custom_call_target="tpu_custom_call" | custom-call | flops 1024 | bytes 1024 | tf_op jit(solution)/shard_map/pallas_call | solution.py:307
  49.6 0.6 %collective-permute-done.13.received = bf16[528,128]{1,0:T(8,128)(2,1)S(1)} collective-permute-done((bf16[528,128]{1,0:T(8,128)(2,1)S(1)}, bf16[528,128]{1,0:T(8,128)(2,1)S(1)}, u32[]{:S(2)}, u32[]{:S(2)}) %collective-permute-start.13) | collective-permute-done | bytes 135200 | tf_op jit(solution)/shard_map/ppermute | solution.py:30
  50.3 0.3 shard_map.65
  50.5 0.6 %collective-permute-done.14.received = bf16[528,128]{1,0:T(8,128)(2,1)S(1)} collective-permute-done((bf16[528,128]{1,0:T(8,128)(2,1)S(1)}, bf16[528,128]{1,0:T(8,128)(2,1)S(1)}, u32[]{:S(2)}, u32[]{:S(2)}) %collective-permute-start.14) | collective-permute-done | bytes 135200 | tf_op jit(solution)/shard_map/ppermute | solution.py:30
  51.1 0.3 shard_map.66
  51.4 0.0 collective-permute-done.15.received
  51.4 1.0 %shard_map.68 = (bf16[512,128]{1,0:T(8,128)(2,1)}, f32[1,512]{1,0:T(1,128)}) custom-call(f32[4,11,8,128]{3,2,1,0:T(8,128)S(1)} %get-tuple-element.52.refs_4_.refs_6_.tables, f32[512,128]{1,0:T(8,128)S(1)} %get-tuple-element.90.mine, f32[512,128]{1,0:T(8,128)S(1)} %get-tuple-element.91.mine_tops, f32[512,128]{1,0:T(8,128)S(1)} %get-tuple-element.92.mine_sums, ...), custom_call_target="tpu_custom_call" | custom-call | flops 1024 | bytes 1024 | tf_op jit(solution)/shard_map/pallas_call | solution.py:307
  (8 shorter events, 0.1 us)
Async XLA Ops:
  1.4 11.4 %collective-permute-start.2 = (bf16[1,2,2,32,128]{4,3,2,1,0:T(8,128)(2,1)S(1)}, bf16[1,2,2,32,128]{4,3,2,1,0:T(8,128)(2,1)S(1)}, u32[]{:S(2)}, u32[]{:S(2)}) collective-permute-start(bf16[1,2,2,32,128]{4,3,2,1,0:T(8,128)(2,1)S(1)} %bitcast.3), channel_id=1, source_target_pairs={{0,4},{1,5},{2,6},{3,7},{4,0},{5,1},{6,2},{7,3},{8,12},{9,13},{10,... | collective-permute-start | bytes 98312 | tf_op jit(solution)/shard_map/ppermute | solution.py:30
  9.1 4.9 %collective-permute-start.1 = (bf16[1,2,2,32,128]{4,3,2,1,0:T(8,128)(2,1)S(1)}, bf16[1,2,2,32,128]{4,3,2,1,0:T(8,128)(2,1)S(1)}, u32[]{:S(2)}, u32[]{:S(2)}) collective-permute-start(bf16[1,2,2,32,128]{4,3,2,1,0:T(8,128)(2,1)S(1)} %bitcast.4), channel_id=1, source_target_pairs={{0,6},{1,7},{2,4},{3,5},{4,2},{5,3},{6,0},{7,1},{8,14},{9,15},{10,... | collective-permute-start | bytes 98312 | tf_op jit(solution)/shard_map/ppermute | solution.py:30
  9.1 3.7 %collective-permute-start = (bf16[1,2,2,32,128]{4,3,2,1,0:T(8,128)(2,1)S(1)}, bf16[1,2,2,32,128]{4,3,2,1,0:T(8,128)(2,1)S(1)}, u32[]{:S(2)}, u32[]{:S(2)}) collective-permute-start(bf16[1,2,2,32,128]{4,3,2,1,0:T(8,128)(2,1)S(1)} %bitcast.5), channel_id=1, source_target_pairs={{0,2},{1,3},{2,0},{3,1},{4,6},{5,7},{6,4},{7,5},{8,10},{9,11},{10,... | collective-permute-start | bytes 98312 | tf_op jit(solution)/shard_map/ppermute | solution.py:30
  10.3 0.7 %copy-start = (s32[64]{0:T(128)S(1)}, s32[64]{0:T(128)}, u32[]{:S(2)}) copy-start(s32[64]{0:T(128)} %span.1) | copy-start | bytes 772
  14.0 7.9 %collective-permute-start.5 = (bf16[4,2,2,32,128]{4,3,2,1,0:T(8,128)(2,1)S(1)}, bf16[4,2,2,32,128]{4,3,2,1,0:T(8,128)(2,1)S(1)}, u32[]{:S(2)}, u32[]{:S(2)}) collective-permute-start(bf16[4,2,2,32,128]{4,3,2,1,0:T(8,128)(2,1)S(1)} %pad_maximum_fusion.2), channel_id=1, source_target_pairs={{0,32},{1,33},{2,34},{3,35},{4,36},{5,37},{6,38},{7,39},{8,136},{9... | collective-permute-start | bytes 393224 | tf_op jit(solution)/shard_map/ppermute | solution.py:30
  17.0 5.3 %collective-permute-start.4 = (bf16[4,2,2,32,128]{4,3,2,1,0:T(8,128)(2,1)S(1)}, bf16[4,2,2,32,128]{4,3,2,1,0:T(8,128)(2,1)S(1)}, u32[]{:S(2)}, u32[]{:S(2)}) collective-permute-start(bf16[4,2,2,32,128]{4,3,2,1,0:T(8,128)(2,1)S(1)} %pad_maximum_fusion.2), channel_id=1, source_target_pairs={{0,48},{1,49},{2,50},{3,51},{4,52},{5,53},{6,54},{7,55},{8,200},{9... | collective-permute-start | bytes 393224 | tf_op jit(solution)/shard_map/ppermute | solution.py:30
  17.8 4.6 %collective-permute-start.3 = (bf16[4,2,2,32,128]{4,3,2,1,0:T(8,128)(2,1)S(1)}, bf16[4,2,2,32,128]{4,3,2,1,0:T(8,128)(2,1)S(1)}, u32[]{:S(2)}, u32[]{:S(2)}) collective-permute-start(bf16[4,2,2,32,128]{4,3,2,1,0:T(8,128)(2,1)S(1)} %pad_maximum_fusion.2), channel_id=1, source_target_pairs={{0,16},{1,17},{2,18},{3,19},{4,20},{5,21},{6,22},{7,23},{8,72},{9,... | collective-permute-start | bytes 393224 | tf_op jit(solution)/shard_map/ppermute | solution.py:30
  18.8 7.6 %collective-permute-start.8 = (bf16[512,256]{1,0:T(8,128)(2,1)S(1)}, bf16[512,256]{1,0:T(8,128)(2,1)S(1)}, u32[]{:S(2)}, u32[]{:S(2)}) collective-permute-start(bf16[512,256]{1,0:T(8,128)(2,1)S(1)} %pad_maximum_fusion.1.own), channel_id=1, source_target_pairs={{0,8},{1,9},{2,10},{3,11},{4,12},{5,13},{6,14},{7,15},{8,0},{9,1},... | collective-permute-start | bytes 786440 | tf_op jit(solution)/shard_map/ppermute | solution.py:30
  22.4 6.3 %collective-permute-start.6 = (bf16[8,2,2,32,128]{4,3,2,1,0:T(8,128)(2,1)S(1)}, bf16[8,2,2,32,128]{4,3,2,1,0:T(8,128)(2,1)S(1)}, u32[]{:S(2)}, u32[]{:S(2)}) collective-permute-start(bf16[8,2,2,32,128]{4,3,2,1,0:T(8,128)(2,1)S(1)} %constant_dynamic-update-slice_fusion.refs_0_), channel_id=1, source_target_pairs={{0,64},{1,65},{2,66},{3,67},{4,68},{5,69},{6,70},{7,71},{8,24},{9,... | collective-permute-start | bytes 786440 | tf_op jit(solution)/shard_map/ppermute | solution.py:30
  23.8 6.4 %collective-permute-start.7 = (bf16[8,2,2,32,128]{4,3,2,1,0:T(8,128)(2,1)S(1)}, bf16[8,2,2,32,128]{4,3,2,1,0:T(8,128)(2,1)S(1)}, u32[]{:S(2)}, u32[]{:S(2)}) collective-permute-start(bf16[8,2,2,32,128]{4,3,2,1,0:T(8,128)(2,1)S(1)} %pad_maximum_fusion.refs_1_), channel_id=1, source_target_pairs={{0,192},{1,193},{2,194},{3,195},{4,196},{5,197},{6,198},{7,199},{8... | collective-permute-start | bytes 786440 | tf_op jit(solution)/shard_map/ppermute | solution.py:30
  25.6 7.7 %collective-permute-start.12 = (bf16[8,2,2,32,128]{4,3,2,1,0:T(8,128)(2,1)S(1)}, bf16[8,2,2,32,128]{4,3,2,1,0:T(8,128)(2,1)S(1)}, u32[]{:S(2)}, u32[]{:S(2)}) collective-permute-start(bf16[8,2,2,32,128]{4,3,2,1,0:T(8,128)(2,1)S(1)} %constant_dynamic-update-slice_fusion.refs_0_), channel_id=1, source_target_pairs={{0,192},{1,193},{2,194},{3,195},{4,196},{5,197},{6,198},{7,199},{8... | collective-permute-start | bytes 786440 | tf_op jit(solution)/shard_map/ppermute | solution.py:30
  26.5 6.9 %collective-permute-start.11 = (bf16[8,2,2,32,128]{4,3,2,1,0:T(8,128)(2,1)S(1)}, bf16[8,2,2,32,128]{4,3,2,1,0:T(8,128)(2,1)S(1)}, u32[]{:S(2)}, u32[]{:S(2)}) collective-permute-start(bf16[8,2,2,32,128]{4,3,2,1,0:T(8,128)(2,1)S(1)} %pad_maximum_fusion.refs_1_), channel_id=1, source_target_pairs={{0,64},{1,65},{2,66},{3,67},{4,68},{5,69},{6,70},{7,71},{8,24},{9,... | collective-permute-start | bytes 786440 | tf_op jit(solution)/shard_map/ppermute | solution.py:30
  30.2 7.2 %collective-permute-start.9 = (bf16[8,2,2,32,128]{4,3,2,1,0:T(8,128)(2,1)S(1)}, bf16[8,2,2,32,128]{4,3,2,1,0:T(8,128)(2,1)S(1)}, u32[]{:S(2)}, u32[]{:S(2)}) collective-permute-start(bf16[8,2,2,32,128]{4,3,2,1,0:T(8,128)(2,1)S(1)} %collective-permute-done.6.refs_0_), channel_id=1, source_target_pairs={{0,192},{1,193},{2,194},{3,195},{4,196},{5,197},{6,198},{7,199},{8... | collective-permute-start | bytes 786440 | tf_op jit(solution)/shard_map/ppermute | solution.py:30
  32.0 5.5 %collective-permute-start.10 = (bf16[8,2,2,32,128]{4,3,2,1,0:T(8,128)(2,1)S(1)}, bf16[8,2,2,32,128]{4,3,2,1,0:T(8,128)(2,1)S(1)}, u32[]{:S(2)}, u32[]{:S(2)}) collective-permute-start(bf16[8,2,2,32,128]{4,3,2,1,0:T(8,128)(2,1)S(1)} %collective-permute-done.7.refs_3_), channel_id=1, source_target_pairs={{0,64},{1,65},{2,66},{3,67},{4,68},{5,69},{6,70},{7,71},{8,24},{9,... | collective-permute-start | bytes 786440 | tf_op jit(solution)/shard_map/ppermute | solution.py:30
  39.0 11.2 %collective-permute-start.13 = (bf16[528,128]{1,0:T(8,128)(2,1)S(1)}, bf16[528,128]{1,0:T(8,128)(2,1)S(1)}, u32[]{:S(2)}, u32[]{:S(2)}) collective-permute-start(bf16[528,128]{1,0:T(8,128)(2,1)S(1)} %get-tuple-element.85), channel_id=1, source_target_pairs={{0,15},{1,10},{2,9},{3,12},{4,11},{5,14},{6,13},{7,8},{8,1},{9,0},... | collective-permute-start | bytes 405512 | tf_op jit(solution)/shard_map/ppermute | solution.py:30
  45.5 5.6 %collective-permute-start.14 = (bf16[528,128]{1,0:T(8,128)(2,1)S(1)}, bf16[528,128]{1,0:T(8,128)(2,1)S(1)}, u32[]{:S(2)}, u32[]{:S(2)}) collective-permute-start(bf16[528,128]{1,0:T(8,128)(2,1)S(1)} %get-tuple-element.89), channel_id=1, source_target_pairs={{0,1},{1,0},{2,3},{3,2},{4,5},{5,4},{6,7},{7,6},{8,15},{9,10},{10,... | collective-permute-start | bytes 405512 | tf_op jit(solution)/shard_map/ppermute | solution.py:30
  48.6 2.8 %collective-permute-start.15 = (bf16[528,128]{1,0:T(8,128)(2,1)S(1)}, bf16[528,128]{1,0:T(8,128)(2,1)S(1)}, u32[]{:S(2)}, u32[]{:S(2)}) collective-permute-start(bf16[528,128]{1,0:T(8,128)(2,1)S(1)} %shard_map.67), channel_id=1, source_target_pairs={{0,8},{1,9},{2,10},{3,11},{4,12},{5,13},{6,14},{7,15},{8,0},{9,1},... | collective-permute-start | bytes 405512 | tf_op jit(solution)/shard_map/ppermute | solution.py:30
